TPU v7x, 32 devices: a whole 2x2x4 slice. The times are simulated.
32 devices in a mesh: row: 2 (over core), col: 16 (over z, y, x).
Axes of the slice: x: 2, y: 2, z: 4, core: 2. Of those that a mesh axis runs over, the one named last changes fastest.
Arguments:
- signal: bfloat16 [65536, 512], P(('row', 'col')), may hold values from -6 to 6
- features: bfloat16 [65536, 80], P(('row', 'col')), may hold values from -6 to 6
- position: int32 [65536], P(('row', 'col')), may hold values from 0 to 15999, as said below
- valid: int32 [65536], P(('row', 'col')), may hold values 0 or 1
- w_past: bfloat16 [512, 1024], replicated, may hold values from -0.1875 to 0.1875
- w_now: bfloat16 [512, 1024], replicated, may hold values from -0.1875 to 0.1875
- b_conv: float32 [1024], replicated, may hold values from -2 to 2
- w_cond: bfloat16 [80, 1024], replicated, may hold values from -0.3125 to 0.3125
- w_res: bfloat16 [512, 512], replicated, may hold values from -0.75 to 0.75
- b_res: float32 [512], replicated, may hold values from -2 to 2
- w_skip: bfloat16 [512, 512], replicated, may hold values from -0.75 to 0.75
- b_skip: float32 [512], replicated, may hold values from -2 to 2
- grad_out: bfloat16 [65536, 512], P(('row', 'col')), may hold values from -6 to 6
- grad_skip: bfloat16 [65536, 512], P(('row', 'col')), may hold values from -6 to 6
Outputs:
- output: bfloat16 [65536, 512], P(('row', 'col'))
- skip_out: bfloat16 [65536, 512], P(('row', 'col'))
- grad_signal: float32 [65536, 512], P(('row', 'col'))
- grad_features: float32 [65536, 80], P(('row', 'col'))
- grad_w_past: float32 [512, 1024], replicated
- grad_w_now: float32 [512, 1024], replicated
- grad_b_conv: float32 [1024], replicated
- grad_w_cond: float32 [80, 1024], replicated
- grad_w_res: float32 [512, 512], replicated
- grad_b_res: float32 [512], replicated
- grad_w_skip: float32 [512, 512], replicated
- grad_b_skip: float32 [512], replicated
Inputs may be any that keep to these rules, and one draw needn't show every extreme that they name: position counts up by one from sample to sample and falls to 0 where a clip begins; clips hold 2000 to 16000 samples, except the first and last, which may be cut; one clip has exactly 16000.
All inputs are finite; a program needn't handle non-finite values. No bound on the sum of `valid` on one device may be relied on, other than what follows from the above.
Results may differ from a plain program's by a relative error of at most 0.0047.
Values may be sent and summed in bfloat16 or wider, within the bound.
No kernel may reach another device: no remote copies, remote signals or barrier semaphores. Data moves between devices by JAX's collectives and lax.ppermute only.
A program may use at most 128 MiB of HBM per device.

v0:
```python
import functools

import jax
import jax.numpy as jnp
from jax import lax
from jax.experimental import pallas as pl
from jax.experimental.pallas import tpu as pltpu
from jax.sharding import Mesh
from jax.sharding import PartitionSpec as P

DILATION_STEP = 256
AXES = ("outer", "core", "far", "near")
HALVES = 2
NEAR = 4
LANES = 128
ROWS = 512
ONES = 16
F32 = jnp.float32
BF16 = jnp.bfloat16
MEGA = 1 << 20
COSTS = {
    "load": 8, "head": 2, "near_sum_0": 7, "mine_1": 2,
    "far_sum_0": 8, "near_sum_1": 4, "near_join_0_1": 2, "near_join_1_1": 4, "far_join_0": 4,
}
FLOPS = 10**9


def dot(left, right):
    return jnp.dot(left, right, preferred_element_type=F32)


def across(left, right):
    return lax.dot_general(left, right, (((0,), (0,)), ((), ())), preferred_element_type=F32)


def against(left, weight):
    return lax.dot_general(left, weight, (((1,), (1,)), ((), ())), preferred_element_type=F32)


def column(lines):
    turned = lines.astype(F32).T
    return jnp.concatenate([turned[:, k : k + 1] for k in range(lines.shape[0])], axis=0)


def row(lines):
    return jnp.concatenate([lines[k : k + 1] for k in range(lines.shape[0])], axis=1)


def tap_of(lines):
    return jnp.where(lines >= DILATION_STEP, 1, 0)


def lines_of(ref, rows):
    return ref[rows.start // LANES : rows.stop // LANES, :]


def picked(pieces, rows):
    found, at = [], 0
    for ref in pieces:
        low, high = max(rows.start, at), min(rows.stop, at + ref.shape[0])
        if low < high:
            found.append(ref[low - at : high - at, :])
        at += ref.shape[0]
    return found[0] if len(found) == 1 else jnp.concatenate(found, axis=0)


def call(kernel, name, in_specs, out_specs, out_shape, scratch=(), aliases=None, grid=(), vmem=24):
    return pl.pallas_call(
        kernel,
        grid=grid,
        in_specs=in_specs,
        out_specs=out_specs,
        out_shape=out_shape,
        scratch_shapes=list(scratch),
        input_output_aliases=aliases or {},
        cost_estimate=pl.CostEstimate(
            flops=1 + int(FLOPS * COSTS.get(name, COSTS.get(name.split("_")[0], 0))), bytes_accessed=1, transcendentals=0
        ),
        name=name,
        compiler_params=pltpu.CompilerParams(vmem_limit_bytes=vmem * MEGA),
    )


VMEM = pl.BlockSpec(memory_space=pltpu.VMEM)
ANYWHERE = pl.BlockSpec(memory_space=pl.ANY)
MARK = jax.ShapeDtypeStruct((8, LANES), F32)


def beside(*parts):
    return jnp.concatenate(parts, axis=1)


def below(*parts):
    return jnp.concatenate(parts, axis=0)


def gate_product(half, k, rows, past, sig, feats, w_in, w_cond, b_conv):
    width = sig.shape[1]
    part = w_in.shape[1] // 2 // HALVES
    at = (k * HALVES + half) * part
    here = slice(at, at + part)
    own = dot(past, w_in[:width, here]) + dot(sig[rows, :], w_in[width:, here])
    return own + across(feats, w_cond[:, here]) + b_conv[:, here]


def back_product(half, rows, gout, gskip, w_res, w_skip):
    part = w_res.shape[0] // HALVES
    here = slice(half * part, (half + 1) * part)
    return against(gout[rows, :], w_res[here, :]) + against(gskip[rows, :], w_skip[here, :])


def finish(pre_a, pre_s, dgated, valid_lines):
    act = jnp.tanh(pre_a)
    gate = 0.5 + 0.5 * jnp.tanh(0.5 * pre_s)
    slope = (column(valid_lines) * dgated) * gate
    dpre = beside(slope * (1.0 - act * act), slope * act * (1.0 - gate)).astype(BF16)
    gated = (act * gate).astype(BF16)
    return gated, gated.T * row(valid_lines.astype(BF16)), dpre


def forward_tiles(half, tiles, prepare, arrive, valid, past, sig, x_turned, gout, gskip, weights, outs, base):
    w_in, w_cond, b_conv, w_res, w_skip = weights
    gated_out, kept_out, dpre_out = outs
    cond = w_cond.shape[0]
    width = sig.shape[1]

    def product(rows, k):
        if arrive:
            arrive(rows, k)
        if k == 2:
            return back_product(half, rows, gout, gskip, w_res, w_skip)
        feats = x_turned[2 * width : 2 * width + cond, rows]
        return gate_product(half, k, rows, past[rows, :], sig, feats, w_in, w_cond, b_conv)

    def done(rows, made):
        there = slice(rows.start - base, rows.stop - base)
        gated_out[there, :], kept_out[:, there], dpre_out[there, :] = finish(*made, lines_of(valid, rows))

    ahead = None
    for rows in tiles:
        if prepare:
            prepare(rows)
        made = [product(rows, k) for k in range(3)]
        if ahead:
            done(*ahead)
        ahead = (rows, made)
    done(*ahead)


def tiles_of(start, stop):
    return [slice(a, a + DILATION_STEP) for a in range(start, stop, DILATION_STEP)]


def split_rows(rows):
    return rows // 2


def load_body(
    valid, pos, b_conv, b_res, b_skip, feat, w_cond, w_res, w_skip, w_past, w_now, sig, gout, gskip,
    valid_to, pos_to, b_conv_to, b_res_to, b_skip_to, w_cond_to, w_res_to, w_skip_to, w_in, past, sig_to, x_turned,
    gout_to, gskip_to, gated_rest, kept_rest, dpre_rest, sems,
):
    rows_all, width = sig.shape
    cond = feat.shape[0]
    count = 0

    def start(source, target):
        nonlocal count
        copy = pltpu.make_async_copy(source, target, sems.at[count])
        copy.start()
        count += 1
        return copy

    def tile(i, source, target):
        rows = pl.ds(i * ROWS, ROWS)
        return start(source.at[rows], target.at[rows])

    signals = [[tile(0, sig, sig_to)]]
    needs = [
        [
            start(pos, pos_to),
            start(w_past, w_in.at[pl.ds(0, width)]),
            start(w_now, w_in.at[pl.ds(width, width)]),
            start(feat, x_turned.at[pl.ds(2 * width, cond)]),
            start(w_cond, w_cond_to),
            start(b_conv, b_conv_to),
        ],
        [],
        [start(valid, valid_to), start(w_res, w_res_to), start(w_skip, w_skip_to)],
    ]
    cotangents = [[tile(0, gout, gout_to), tile(0, gskip, gskip_to)]]
    for i in range(1, rows_all // ROWS):
        signals.append([tile(i, sig, sig_to)])
        cotangents.append([tile(i, gout, gout_to), tile(i, gskip, gskip_to)])
    last = [start(b_res, b_res_to), start(b_skip, b_skip_to)]

    def wait(copies):
        for copy in copies:
            copy.wait()
        copies.clear()

    def prepare(rows):
        i = rows.start // ROWS
        wait(signals[i])
        wait(needs[0])
        whole = rows if i else slice(0, rows.stop)
        before = slice(rows.start - DILATION_STEP, rows.stop - DILATION_STEP)
        tap = tap_of(lines_of(pos_to, rows)).astype(F32)
        past[rows, :] = sig_to[before, :] * column(tap).astype(BF16)
        x_turned[width : 2 * width, whole] = sig_to[whole, :].T
        x_turned[:width, rows] = x_turned[width : 2 * width, before] * row(tap).astype(BF16)

    def arrive(rows, k):
        wait(needs[k])
        if k == 2:
            wait(cotangents[rows.start // ROWS])

    x_turned[2 * width + cond :, :] = jnp.ones((x_turned.shape[0] - 2 * width - cond, rows_all), BF16)
    forward_tiles(
        0, tiles_of(DILATION_STEP, rows_all), prepare, arrive, valid_to, past, sig_to, x_turned, gout_to, gskip_to,
        (w_in, w_cond_to, b_conv_to, w_res_to, w_skip_to), (gated_rest, kept_rest, dpre_rest), DILATION_STEP,
    )
    wait(last)


def rest_shapes(rest, part):
    return [jax.ShapeDtypeStruct(shape, BF16) for shape in ((rest, part), (part, rest), (rest, 2 * part))]


def load(*arrays):
    sources = [in_hbm(x) for x in arrays]
    feat, w_cond, w_res, w_skip, w_past, w_now, sig, gout, gskip = arrays[5:]
    rows, width = sig.shape
    hidden = w_res.shape[0]
    shapes = [jax.ShapeDtypeStruct(x.shape, x.dtype) for x in arrays[:5] + (w_cond, w_res, w_skip)] + [
        jax.ShapeDtypeStruct(shape, BF16)
        for shape in (
            (2 * width, 2 * hidden), sig.shape, sig.shape, (2 * width + feat.shape[0] + ONES, rows), gout.shape, gskip.shape,
        )
    ]
    shapes += rest_shapes(rows - DILATION_STEP, hidden // HALVES)
    return call(
        load_body,
        "load",
        [ANYWHERE] * len(sources),
        [VMEM] * len(shapes),
        shapes,
        scratch=[pltpu.SemaphoreType.DMA((11 + 3 * (rows // ROWS),))],
    )(*sources)


def side_by_side(dpre_0, dpre_1):
    part = dpre_0.shape[1] // 2
    return beside(dpre_0[:, :part], dpre_1[:, :part], dpre_0[:, part:], dpre_1[:, part:])


def head_rows(half, halo, pos, valid, sig, x_turned, gout, gskip, weights, outs):
    w_in, w_cond, b_conv, w_res, w_skip = weights
    rows = slice(0, DILATION_STEP)
    width = halo.shape[1]
    feats = x_turned[2 * width : 2 * width + w_cond.shape[0], rows]
    past = halo[...] * column(tap_of(lines_of(pos, rows)).astype(F32)).astype(BF16)
    made = [gate_product(half, k, rows, past, sig, feats, w_in, w_cond, b_conv) for k in range(2)]
    made.append(back_product(half, rows, gout, gskip, w_res, w_skip))
    for ref, value in zip(outs, finish(*made, lines_of(valid, rows))):
        ref[...] = value


def head_body(halo, pos, valid, sig, x_turned, gout, gskip, w_in, w_cond, b_conv, w_res, w_skip, past_out, *outs):
    tap = tap_of(lines_of(pos, slice(0, DILATION_STEP))).astype(F32)
    past_out[...] = halo[...].T * row(tap).astype(BF16)
    head_rows(0, halo, pos, valid, sig, x_turned, gout, gskip, (w_in, w_cond, b_conv, w_res, w_skip), outs)


def head(halo, *args):
    width = halo.shape[1]
    part = args[-1].shape[0] // HALVES
    past, *parts = call(
        head_body,
        "head",
        [VMEM] * (1 + len(args)),
        [VMEM] * 4,
        [jax.ShapeDtypeStruct((width, DILATION_STEP), BF16)] + rest_shapes(DILATION_STEP, part),
    )(halo, *args)
    return past, parts


def early_body(token, pos, dpre_0, dpre_1, w_in, early):
    tap = column(tap_of(lines_of(pos, slice(0, DILATION_STEP))))
    early[...] = (tap * against(side_by_side(dpre_0[...], dpre_1[...]), w_in[: early.shape[1], :])).astype(BF16)


def early_rows(token, pos, dpre_0, dpre_1, w_in):
    return call(
        early_body,
        "early",
        [ANYWHERE] + [VMEM] * 4,
        VMEM,
        jax.ShapeDtypeStruct((DILATION_STEP, w_in.shape[0] // 2), BF16),
    )(token, pos, dpre_0, dpre_1, w_in)


def most_body(token, valid, past, sig, x_turned, gout, gskip, w_in, w_cond, b_conv, w_res, w_skip, *outs):
    forward_tiles(
        1, tiles_of(DILATION_STEP, split_rows(sig.shape[0])), None, None, valid, past, sig, x_turned, gout, gskip,
        (w_in, w_cond, b_conv, w_res, w_skip), outs, DILATION_STEP,
    )


def forward_most(token, *args):
    part = args[-1].shape[0] // HALVES
    return call(
        most_body,
        "forward_1",
        [ANYWHERE] + [VMEM] * len(args),
        [VMEM] * 3,
        rest_shapes(split_rows(args[2].shape[0]) - DILATION_STEP, part),
    )(token, *args)


def ends_body(token, halo, pos, valid, past, sig, x_turned, gout, gskip, w_in, w_cond, b_conv, w_res, w_skip, *outs):
    weights = (w_in, w_cond, b_conv, w_res, w_skip)
    rows = sig.shape[0]
    head_rows(1, halo, pos, valid, sig, x_turned, gout, gskip, weights, outs[:3])
    forward_tiles(
        1, tiles_of(split_rows(rows), rows), None, None, valid, past, sig, x_turned, gout, gskip, weights, outs[3:],
        split_rows(rows),
    )


def forward_ends(token, *args):
    part = args[-1].shape[0] // HALVES
    rows = args[4].shape[0]
    parts = call(
        ends_body,
        "ends_1",
        [ANYWHERE] + [VMEM] * len(args),
        [VMEM] * 6,
        rest_shapes(DILATION_STEP, part) + rest_shapes(rows - split_rows(rows), part),
    )(token, *args)
    return parts[:3], parts[3:]


def own_place():
    return [lax.axis_index(name) for name in ("core", "far", "near")]


def turned(index, count):
    bits = (count - 1).bit_length()
    result = 0
    for bit in range(bits):
        result = result | (((index >> bit) & 1) << (bits - 1 - bit))
    return result


def gradients_body(far, block, half, own, count, token, valid, x_turned, gout, gskip, past_head, *refs):
    kepts, dpres, (out, acc) = refs[:count], refs[count : 2 * count], refs[2 * count :]
    width = past_head.shape[0]
    part = kepts[0].shape[0]
    ends, rows = x_turned.shape
    size = far * block
    core, z, xy = own_place()
    which = core if own else 1 - core

    def product(left_of, rights):
        total, at = None, 0
        for k, right in enumerate(rights):
            here = slice(at, at + right.shape[0])
            made = dot(left_of(here, k), right[...])
            total = made if at == 0 else total + made
            at = here.stop
        return total

    def region(k):
        low, high = k * size, min((k + 1) * size, ends)

        def turned_rows(here, piece):
            if piece == 0 and low < width:
                return below(past_head[low : min(high, width), :], x_turned[width : max(high, width), here])
            return x_turned[low:high, here]

        acc[: high - low, :] = product(turned_rows, dpres)
        at = high - low
        if high == ends:
            mask = jnp.broadcast_to(row(lines_of(valid, slice(0, rows)).astype(F32)).astype(BF16), (ONES, rows))

            def kept_rows(here, piece):
                return below(kepts[piece][...], mask[:, here])

            for i, ref in enumerate((gout, gskip)):
                cuts = [0]
                for kept in kepts:
                    cuts.append(cuts[-1] + kept.shape[1])
                made = product(kept_rows, [ref.at[pl.ds(a, b - a)] for a, b in zip(cuts, cuts[1:])])
                acc[at : at + part, :] = made[:part]
                at += part
                if i == half:
                    acc[high - low + 2 * part : high - low + 2 * part + ONES, :] = made[part:]
            at += ONES
            acc[at:, :] = jnp.zeros((size - at, acc.shape[1]), F32)
        for r in range(far):
            for c in range(NEAR):
                value = acc[r * block : (r + 1) * block, c * LANES : (c + 1) * LANES]
                out[c ^ xy, turned(r ^ z, far)] = value.astype(out.dtype)

    for k in range(2):
        pl.when(which == k)(functools.partial(region, k))


def gradients(half, own, token, far, block, valid, x_turned, gout, gskip, past_head, pieces):
    packed = (NEAR, far, block, LANES)
    wide = pieces[0][2].shape[1]
    count = len(pieces)
    return call(
        functools.partial(gradients_body, far, block, half, own, count),
        ("mine" if own else "theirs") + f"_{half}",
        [ANYWHERE] + [VMEM] * (5 + 2 * count),
        VMEM,
        jax.ShapeDtypeStruct(packed, F32 if own else BF16),
        scratch=[pltpu.VMEM((far * block, wide), F32)],
    )(token, valid, x_turned, gout, gskip, past_head, *(p[1] for p in pieces), *(p[2] for p in pieces))


def outputs_body(counts, token, valid, sig, w_res, w_skip, b_res, b_skip, *refs):
    first, second = refs[: counts[0]], refs[counts[0] : sum(counts)]
    out, skip, mark, rooms, sems = refs[sum(counts) :]
    copies = []
    for i in range(sig.shape[0] // ROWS):
        rows = slice(i * ROWS, (i + 1) * ROWS)
        mask = column(lines_of(valid, rows))
        gated = beside(picked(first, rows), picked(second, rows))
        branch = dot(gated, w_res[...]) + b_res[...]
        rooms[i, 0] = (sig[rows, :].astype(F32) + mask * branch).astype(BF16)
        side = dot(gated, w_skip[...]) + b_skip[...]
        rooms[i, 1] = (mask * side).astype(BF16)
        for k, ref in enumerate((out, skip)):
            copies.append(pltpu.make_async_copy(rooms.at[i, k], ref.at[pl.ds(i * ROWS, ROWS)], sems.at[i, k]))
            copies[-1].start()
    mark[...] = jnp.zeros_like(mark)
    for copy in copies:
        copy.wait()


def outputs(token, valid, sig, gated_0, gated_1, w_res, w_skip, b_res, b_skip):
    rows, width = sig.shape
    counts = (len(gated_0), len(gated_1))
    return call(
        functools.partial(outputs_body, counts),
        "outputs",
        [ANYWHERE] + [VMEM] * (6 + sum(counts)),
        [ANYWHERE, ANYWHERE, VMEM],
        [
            jax.ShapeDtypeStruct((rows, width), BF16),
            jax.ShapeDtypeStruct((rows, w_skip.shape[1]), BF16),
            MARK,
        ],
        scratch=[
            pltpu.VMEM((rows // ROWS, 2, ROWS, width), BF16),
            pltpu.SemaphoreType.DMA((rows // ROWS, 2)),
        ],
    )(token, valid, sig, w_res, w_skip, b_res, b_skip, *gated_0, *gated_1)


def inputs_body(steps, counts, token, received, gout, pos, w_in, w_cond, *refs):
    first, second = refs[: counts[0]], refs[counts[0] : sum(counts)]
    gsig, gfeat, mark, room, room_feat, sems = refs[-6:]
    rows, width = gout.shape
    copies = []
    wide = 2 * LANES

    def copy(source, target):
        copies.append(pltpu.make_async_copy(source, target, sems.at[len(copies)]))
        copies[-1].start()

    for i, step in enumerate(steps):
        begin = step * ROWS
        here = slice(begin, begin + ROWS)
        after = slice(begin + DILATION_STEP, min(begin + DILATION_STEP + ROWS, rows))
        now = side_by_side(picked(first, here), picked(second, here))
        later = side_by_side(picked(first, after), picked(second, after))
        tap = column(tap_of(lines_of(pos, after)))
        room_feat[i] = against(w_cond[...], now)
        copy(room_feat.at[i], gfeat.at[:, pl.ds(begin, ROWS)])
        for k in range(width // wide):
            some = slice(k * wide, (k + 1) * wide)
            tail = tap * against(later, w_in[some, :])
            if tail.shape[0] < ROWS:
                tail = below(tail, received[:, some].astype(F32))
            room[i, k] = gout[here, some].astype(F32) + against(now, w_in[width + k * wide : width + (k + 1) * wide, :]) + tail
            copy(room.at[i, k], gsig.at[pl.ds(begin, ROWS), pl.ds(k * wide, wide)])
    mark[...] = jnp.zeros_like(mark)
    for one in copies:
        one.wait()


def inputs(steps, token, received, gout, pos, dpre_0, dpre_1, w_in, w_cond, before):
    rows, width = gout.shape
    cond = w_cond.shape[0]
    count = width // (2 * LANES)
    counts = (len(dpre_0), len(dpre_1))
    operands = 6 + sum(counts)
    return call(
        functools.partial(inputs_body, steps, counts),
        f"inputs_{steps[0]}",
        [ANYWHERE] + [VMEM] * (operands - 1) + [ANYWHERE] * len(before),
        [ANYWHERE, ANYWHERE, VMEM],
        [
            jax.ShapeDtypeStruct((rows, width), F32),
            jax.ShapeDtypeStruct((cond, rows), F32),
            MARK,
        ],
        scratch=[
            pltpu.VMEM((len(steps), count, ROWS, 2 * LANES), F32),
            pltpu.VMEM((len(steps), cond, ROWS), F32),
            pltpu.SemaphoreType.DMA((len(steps) * (count + 1),)),
        ],
        aliases={operands + k: k for k in range(len(before))},
    )(token, received, gout, pos, w_in, w_cond, *dpre_0, *dpre_1, *before)


SHARES = ((0, 3), (1, 2))


def unpack_body(far, block, token, *refs):
    blocks, arrays, (mark, room) = refs[: 2 * len(SHARES)], refs[-9:-2], refs[-2:]
    mine, theirs = blocks[: len(SHARES)], blocks[len(SHARES) :]
    mark[...] = jnp.zeros_like(mark)
    core, z, xy = own_place()

    @pl.when(pl.program_id(0) == 0)
    def _():
        for k, parts in ((core, mine), (1 - core, theirs)):
            for share, ref in zip(SHARES, parts):
                for i, c in enumerate(share):
                    for r in range(far):
                        rows = pl.ds(pl.multiple_of((k * far + (r ^ z)) * block, 16), block)
                        room[c ^ xy, rows, :] = ref[i, turned(r, far)]

    for j in range(NEAR // 2):
        c = pl.program_id(0) * (NEAR // 2) + j
        here = pl.ds(j * LANES, LANES)
        top = 0
        for ref in arrays:
            count = ref.shape[0]
            size = max(count, ONES)
            ref[:, here] = room[c, top : top + size, :].astype(F32)[:count]
            top += size


def unpack(half, token, far, block, mine, theirs, width, cond, hidden, skip_width, before):
    part = hidden // HALVES
    gates = 2 * hidden
    own = (width, skip_width)[half]

    def wide(size):
        return pl.BlockSpec((size, part), lambda s: (0, HALVES * s + half))

    def tall(size):
        return pl.BlockSpec((part, size // 2), lambda s: (half, s))

    specs = [wide(width), wide(width), wide(cond), wide(1), tall(width), tall(skip_width), pl.BlockSpec((1, own // 2), lambda s: (0, s))]
    shapes = [(width, gates), (width, gates), (cond, gates), (1, gates), (hidden, width), (hidden, skip_width), (1, own)]
    blocks = [pl.BlockSpec(x.shape, lambda s: (0,) * 4) for x in (*mine, *theirs)]
    return call(
        functools.partial(unpack_body, far, block),
        f"unpack_{half}",
        [ANYWHERE, *blocks] + [ANYWHERE] * len(before),
        specs + [pl.BlockSpec(MARK.shape, lambda s: (0, 0))],
        [jax.ShapeDtypeStruct(shape, F32) for shape in shapes] + [MARK],
        scratch=[pltpu.VMEM((NEAR, 2 * far * block, LANES), BF16)],
        aliases={1 + len(blocks) + k: k for k in range(len(before))},
        grid=(2,),
    )(token, *mine, *theirs, *before)


def swapped(x, axis, k):
    return lax.ppermute(x, axis, [(i, i ^ k) for i in range(lax.axis_size(axis))])


def exchanged(blocks):
    return [swapped(block, "near", k + 1) for k, block in enumerate(blocks)]


def add_body(sizes, token, *refs):
    count = len(sizes)
    kept, got, outs = refs[0], refs[1:-count], refs[-count:]
    at = 0
    for out, size in zip(outs, sizes):
        for k in range(size):
            total = kept[at + k].astype(F32)
            for ref in got:
                total = total + ref[at + k].astype(F32)
            out[k] = total.astype(out.dtype)
        at += size


def added(name, token, kept, got, outs):
    sizes = [size for size, _ in outs]
    result = call(
        functools.partial(add_body, sizes),
        name,
        [ANYWHERE] + [VMEM] * (1 + len(got)),
        [VMEM] * len(outs),
        [jax.ShapeDtypeStruct((size, *kept.shape[1:]), dtype) for size, dtype in outs],
    )(token, kept, *got)
    return result


def mirror_body(token, mine, got, out):
    count = mine.shape[0]
    for k in range(count):
        out[k] = (mine[k].astype(F32) + got[count - 1 - k].astype(F32)).astype(out.dtype)


def mirrored(name, token, mine, got):
    return call(
        mirror_body,
        name,
        [ANYWHERE, VMEM, VMEM],
        VMEM,
        jax.ShapeDtypeStruct(mine.shape, BF16),
    )(token, mine, got)


def join_body(token, *refs):
    out = refs[-1]
    at = 0
    for ref in refs[:-1]:
        out[at : at + ref.shape[0]] = ref[...]
        at += ref.shape[0]


def joined(name, token, parts):
    count = sum(part.shape[0] for part in parts)
    return call(
        join_body,
        name,
        [ANYWHERE] + [VMEM] * len(parts),
        VMEM,
        jax.ShapeDtypeStruct((count, *parts[0].shape[1:]), BF16),
    )(token, *parts)


def over_outer(total):
    for bit in range((lax.axis_size("outer") - 1).bit_length()):
        total = (total.astype(F32) + swapped(total, "outer", 1 << bit).astype(F32)).astype(BF16)
    return total


def passed_along(x, by):
    peers = lax.axis_size(AXES)
    pairs = [(i, i + by) for i in range(peers) if 0 <= i + by < peers]
    return lax.ppermute(x, AXES, pairs)


def in_hbm(x):
    return pltpu.with_memory_space_constraint(x, pltpu.HBM)


def body(
    signal,
    features,
    position,
    valid,
    w_past,
    w_now,
    b_conv,
    w_cond,
    w_res,
    b_res,
    w_skip,
    b_skip,
    grad_out,
    grad_skip,
):
    rows, width = signal.shape
    features = features.T
    cond = features.shape[0]
    hidden = w_res.shape[0]
    skip_width = w_skip.shape[1]
    far = lax.axis_size("far")
    far_bits = (far - 1).bit_length()
    used = 2 * width + cond + ONES + 2 * (hidden // HALVES) + ONES
    block = -(-used // (2 * far * 16)) * 16
    lines = (rows // LANES, LANES)
    pos, val = position.reshape(lines), valid.reshape(lines)
    b_conv, b_res, b_skip = (b.reshape(1, -1) for b in (b_conv, b_res, b_skip))

    def core_sum(half, token, theirs, mine):
        kept, *sent = added(
            f"core_sum_{half}", token, mine, [swapped(theirs, "core", 1)], [(1, F32)] + [(1, BF16)] * (NEAR - 1)
        )
        return kept[0], exchanged([x[0] for x in sent])

    def near_sum(half, token, kept, got):
        kept, sent = added(f"near_sum_{half}", token, kept, got, [(far // 2, F32), (far // 2, BF16)])
        return kept, swapped(sent, "far", 1)

    def far_sum(half, token, kept, got):
        for bit in range(1, far_bits - 1):
            size = kept.shape[0] // 2
            kept, sent = added(f"far_sum_{half}_{bit}", token, kept, [got], [(size, F32), (size, BF16)])
            got = swapped(sent, "far", 1 << bit)
        (mine,) = added(f"far_sum_{half}", token, kept, [got], [(kept.shape[0], BF16)])
        return mine, swapped(mine, "far", 1 << (far_bits - 1))

    def far_end(half, token, mine, got):
        total = over_outer(mirrored(f"far_end_{half}", token, mine, got))
        return total, swapped(total, "far", 1 << (far_bits - 2))

    def far_join(half, token, mine, got):
        total = joined(f"far_join_{half}", token, [mine, got])
        for bit in reversed(range(far_bits - 2)):
            total = joined(f"far_join_{half}_{bit}", token, [total, swapped(total, "far", 1 << bit)])
        return total, exchanged([total] * (NEAR - 1))

    def near_join(half, k, token, mine, got):
        blocks = [mine, *got]
        total = joined(f"near_join_{half}_{k}", token, [blocks[c][None] for c in SHARES[k]])
        return total, swapped(total, "core", 1)

    def input_gradients(steps, token, before):
        last = (steps[-1] + 1) * ROWS == rows
        return inputs(steps, token, received if last else head_0[0], grad_out, pos, dpre_0, dpre_1, w_in, w_cond, before)

    halo = passed_along(signal[rows - DILATION_STEP :], 1)
    val, pos, b_conv, b_res, b_skip, w_cond, w_res, w_skip, w_in, past, signal, x_turned, grad_out, grad_skip, *rest_0 = load(
        val, pos, b_conv, b_res, b_skip, features, w_cond, w_res, w_skip, w_past, w_now, signal, grad_out, grad_skip
    )
    common = (signal, x_turned, grad_out, grad_skip, w_in, w_cond, b_conv, w_res, w_skip)
    past_head, head_0 = head(halo, pos, val, *common)
    made_0 = (head_0, rest_0)
    fixed = (far, block, val, x_turned, grad_out, grad_skip, past_head)
    theirs_0 = gradients(0, False, past_head, *fixed, made_0)
    mine_0 = gradients(0, True, theirs_0, *fixed, made_0)
    most_1 = forward_most(mine_0, val, past, *common)
    kept_0, got_0 = core_sum(0, most_1[0], theirs_0, mine_0)
    head_1, last_1 = forward_ends(kept_0, halo, pos, val, past, *common)
    made_1 = (head_1, most_1, last_1)
    dpre_0, dpre_1 = ([p[2] for p in made] for made in (made_0, made_1))
    theirs_1 = gradients(1, False, kept_0, *fixed, made_1)
    mine_1 = gradients(1, True, theirs_1, *fixed, made_1)
    kept_0, got_0 = near_sum(0, mine_1, kept_0, got_0)
    kept_1, got_1 = core_sum(1, kept_0, theirs_1, mine_1)
    ends_0, got_0 = far_sum(0, kept_1, kept_0, got_0)
    *grads, mark = input_gradients((0, 1), ends_0, [])
    ends_0, got_0 = far_end(0, mark, ends_0, got_0)
    kept_1, got_1 = near_sum(1, ends_0, kept_1, got_1)
    ends_0, got_0 = far_join(0, kept_1, ends_0, got_0)
    ends_1, got_1 = far_sum(1, ends_0, kept_1, got_1)
    output, skip_out, mark = outputs(
        ends_1, val, signal, [p[0] for p in made_0], [p[0] for p in made_1], w_res, w_skip, b_res, b_skip
    )
    ends_1, got_1 = far_end(1, mark, ends_1, got_1)
    early = early_rows(ends_1, pos, head_0[2], head_1[2], w_in)
    received = passed_along(early, -1)
    first = near_join(0, 0, early, ends_0, got_0)
    second = near_join(0, 1, first[0], ends_0, got_0)
    pairs_0 = [first, second]
    ends_1, got_1 = far_join(1, second[0], ends_1, got_1)
    *grads, mark = input_gradients((2, 3), ends_1, grads)
    first = near_join(1, 0, mark, ends_1, got_1)
    second = near_join(1, 1, first[0], ends_1, got_1)
    pairs_1 = [first, second]
    sizes = (width, cond, hidden, skip_width)
    *done, own_0, mark = unpack(0, first[1], far, block, *zip(*pairs_0), *sizes, [])
    *done, own_1, _ = unpack(1, mark, far, block, *zip(*pairs_1), *sizes, done)
    g_past, g_now, g_cond, g_bias, g_res, g_skip = done
    grad_signal, grad_features = grads
    return (
        output,
        skip_out,
        grad_signal,
        grad_features.T,
        g_past,
        g_now,
        g_bias.reshape(-1),
        g_cond,
        g_res,
        own_0.reshape(-1),
        g_skip,
        own_1.reshape(-1),
    )


def solution(mesh):
    row, col = mesh.shape["row"], mesh.shape["col"]
    fine = Mesh(mesh.devices.reshape(row // 2, 2, col // NEAR, NEAR), AXES)
    rows = P(AXES, None)
    line = P(AXES)
    return jax.shard_map(
        body,
        mesh=fine,
        in_specs=(rows, rows, line, line) + (P(),) * 8 + (rows, rows),
        out_specs=(rows,) * 4 + (P(),) * 8,
        check_vma=False,
    )
```

profile of v0, /device:TPU:3, one launch (start us, length us, event | category | flops | bytes accessed | tf_op | source)
XLA Modules:
  0.0 85.4 jit_solution(10358850363654346736)
XLA Ops:
  0.6 1.0 %slice.3 = bf16[256,512]{1,0:T(8,128)(2,1)S(1)} slice(bf16[2048,512]{1,0:T(8,128)(2,1)} %sig.1), slice={[1792:2048], [0:512]} | slice | bytes 524288 | tf_op jit(solution)/shard_map/slice | solution.py:726
  1.6 3.1 %collective-permute-start = (bf16[256,512]{1,0:T(8,128)(2,1)S(1)}, bf16[256,512]{1,0:T(8,128)(2,1)S(1)}, u32[]{:S(2)}, u32[]{:S(2)}) collective-permute-start(bf16[256,512]{1,0:T(8,128)(2,1)S(1)} %slice.3), channel_id=1, source_target_pairs={{0,1},{1,2},{2,3},{3,4},{4,5},{5,6},{6,7},{7,8},{8,9},{9,10},{10,1... | collective-permute-start | bytes 786440 | tf_op jit(solution)/shard_map/ppermute | solution.py:653
  4.7 8.0 %load.1 = (s32[16,128]{1,0:T(8,128)S(1)}, s32[16,128]{1,0:T(8,128)S(1)}, f32[1,1024]{1,0:T(1,128)S(1)}, f32[1,512]{1,0:T(1,128)S(1)}, f32[1,512]{1,0:T(1,128)S(1...) custom-call(s32[16,128]{1,0:T(8,128)} %bitcast.48, ...), custom_call_target="tpu_custom_call" | custom-call | flops 8000000000 | bytes 1 | tf_op jit(solution)/shard_map/load/pallas_call | solution.py:242
  13.5 2.0 %theirs_0.1.token = bf16[4,4,208,128]{3,2,1,0:T(8,128)(2,1)S(1)} custom-call(bf16[512,256]{1,0:T(8,128)(2,1)S(1)} %get-tuple-element.89.token.past_head, s32[16,128]{1,0:T(8,128)S(1)} %get-tuple-element.79.valid, bf16[1120,2048]{1,0:T(8,128)(2,1)S(1)} %get-tuple-element.81.x_turned, bf16[2048,512]{1,0:T(8,128)(2,1)S(1)} %get-tuple-element.82.gout, ...), custom_call_target="tpu_custom_call" | custom-call | flops 1 | bytes 1 | tf_op jit(solution)/shard_map/theirs_0/pallas_call | solution.py:414
  15.5 1.0 %collective-permute-start.1 = (bf16[4,4,208,128]{3,2,1,0:T(8,128)(2,1)S(1)}, bf16[4,4,208,128]{3,2,1,0:T(8,128)(2,1)S(1)}, u32[]{:S(2)}, u32[]{:S(2)}) collective-permute-start(bf16[4,4,208,128]{3,2,1,0:T(8,128)(2,1)S(1)} %theirs_0.1.token), channel_id=1, source_target_pairs={{0,16},{16,0},{1,17},{17,1},{2,18},{18,2},{3,19},{19,3},{4,20},{20... | collective-permute-start | bytes 2555912 | tf_op jit(solution)/shard_map/ppermute | solution.py:577
  16.5 2.2 %mine_0.1.token.refs_0_ = f32[4,4,208,128]{3,2,1,0:T(8,128)S(1)} custom-call(bf16[4,4,208,128]{3,2,1,0:T(8,128)(2,1)S(1)} %theirs_0.1.token, s32[16,128]{1,0:T(8,128)S(1)} %get-tuple-element.79.valid, bf16[1120,2048]{1,0:T(8,128)(2,1)S(1)} %get-tuple-element.81.x_turned, bf16[2048,512]{1,0:T(8,128)(2,1)S(1)} %get-tuple-element.82.gout, ...), custom_call_target="tpu_custom_call" | custom-call | flops 1 | bytes 1 | tf_op jit(solution)/shard_map/mine_0/pallas_call | solution.py:414
  18.7 1.9 %forward_1.1 = (bf16[768,256]{1,0:T(8,128)(2,1)S(1)}, bf16[256,768]{1,0:T(8,128)(2,1)S(1)}, bf16[768,512]{1,0:T(8,128)(2,1)S(1)}) custom-call(f32[4,4,208,128]{3,2,1,0:T(8,128)S(1)} %mine_0.1.token.refs_0_, s32[16,128]{1,0:T(8,128)S(1)} %get-tuple-element.79.valid, bf16[2048,512]{1,0:T(8,128)(2,1)S(1)} %get-tuple-element.94.past, ...), custom_call_target="tpu_custom_call" | custom-call | flops 1 | bytes 1 | tf_op jit(solution)/shard_map/forward_1/pallas_call | solution.py:312
  21.1 1.2 %collective-permute-start.3 = (bf16[4,208,128]{2,1,0:T(8,128)(2,1)S(1)}, bf16[4,208,128]{2,1,0:T(8,128)(2,1)S(1)}, u32[]{:S(2)}, u32[]{:S(2)}) collective-permute-start(bf16[4,208,128]{2,1,0:T(8,128)(2,1)S(1)} %bitcast.43), channel_id=1, source_target_pairs={{0,2},{1,3},{2,0},{3,1},{4,6},{5,7},{6,4},{7,5},{8,10},{9,11},{10,... | collective-permute-start | bytes 638984 | tf_op jit(solution)/shard_map/ppermute | solution.py:577
  22.4 1.2 %collective-permute-start.4 = (bf16[4,208,128]{2,1,0:T(8,128)(2,1)S(1)}, bf16[4,208,128]{2,1,0:T(8,128)(2,1)S(1)}, u32[]{:S(2)}, u32[]{:S(2)}) collective-permute-start(bf16[4,208,128]{2,1,0:T(8,128)(2,1)S(1)} %bitcast.41), channel_id=1, source_target_pairs={{0,3},{1,2},{2,1},{3,0},{4,7},{5,6},{6,5},{7,4},{8,11},{9,10},{10,... | collective-permute-start | bytes 638984 | tf_op jit(solution)/shard_map/ppermute | solution.py:577
  23.5 3.0 %ends_1.1 = (bf16[256,256]{1,0:T(8,128)(2,1)S(1)}, bf16[256,256]{1,0:T(8,128)(2,1)S(1)}, bf16[256,512]{1,0:T(8,128)(2,1)S(1)}, bf16[1024,256]{1,0:T(8,128)(2,1)S...) custom-call(f32[4,208,128]{2,1,0:T(8,128)S(1)} %bitcast.27, ...), custom_call_target="tpu_custom_call" | custom-call | flops 1 | bytes 1 | tf_op jit(solution)/shard_map/ends_1/pallas_call | solution.py:334
  26.5 2.0 %theirs_1.1.token = bf16[4,4,208,128]{3,2,1,0:T(8,128)(2,1)S(1)} custom-call(f32[4,208,128]{2,1,0:T(8,128)S(1)} %bitcast.28, s32[16,128]{1,0:T(8,128)S(1)} %get-tuple-element.79.valid, bf16[1120,2048]{1,0:T(8,128)(2,1)S(1)} %get-tuple-element.81.x_turned, bf16[2048,512]{1,0:T(8,128)(2,1)S(1)} %get-tuple-element.82.gout, ...), custom_call_target="tpu_custom_call" | custom-call | flops 1 | bytes 1 | tf_op jit(solution)/shard_map/theirs_1/pallas_call | solution.py:414
  29.4 2.2 %mine_1.1.token.refs_0_ = f32[4,4,208,128]{3,2,1,0:T(8,128)S(1)} custom-call(bf16[4,4,208,128]{3,2,1,0:T(8,128)(2,1)S(1)} %theirs_1.1.token, s32[16,128]{1,0:T(8,128)S(1)} %get-tuple-element.79.valid, bf16[1120,2048]{1,0:T(8,128)(2,1)S(1)} %get-tuple-element.81.x_turned, bf16[2048,512]{1,0:T(8,128)(2,1)S(1)} %get-tuple-element.82.gout, ...), custom_call_target="tpu_custom_call" | custom-call | flops 2000000000 | bytes 1 | tf_op jit(solution)/shard_map/mine_1/pallas_call | solution.py:414
  31.7 1.6 %collective-permute-done.4.refs_3_ = bf16[4,208,128]{2,1,0:T(8,128)(2,1)S(1)} collective-permute-done((bf16[4,208,128]{2,1,0:T(8,128)(2,1)S(1)}, bf16[4,208,128]{2,1,0:T(8,128)(2,1)S(1)}, u32[]{:S(2)}, u32[]{:S(2)}) %collective-permute-start.4) | collective-permute-done | bytes 213024 | tf_op jit(solution)/shard_map/ppermute | solution.py:577
  33.4 1.4 %collective-permute-start.6 = (bf16[2,208,128]{2,1,0:T(8,128)(2,1)S(1)}, bf16[2,208,128]{2,1,0:T(8,128)(2,1)S(1)}, u32[]{:S(2)}, u32[]{:S(2)}) collective-permute-start(bf16[2,208,128]{2,1,0:T(8,128)(2,1)S(1)} %get-tuple-element.108), channel_id=1, source_target_pairs={{0,4},{4,0},{8,12},{12,8},{1,5},{5,1},{9,13},{13,9},{2,6},{6,2},{1... | collective-permute-start | bytes 319496 | tf_op jit(solution)/shard_map/ppermute | solution.py:577
  35.3 1.1 %collective-permute-start.9 = (bf16[4,208,128]{2,1,0:T(8,128)(2,1)S(1)}, bf16[4,208,128]{2,1,0:T(8,128)(2,1)S(1)}, u32[]{:S(2)}, u32[]{:S(2)}) collective-permute-start(bf16[4,208,128]{2,1,0:T(8,128)(2,1)S(1)} %bitcast.39), channel_id=1, source_target_pairs={{0,2},{1,3},{2,0},{3,1},{4,6},{5,7},{6,4},{7,5},{8,10},{9,11},{10,... | collective-permute-start | bytes 638984 | tf_op jit(solution)/shard_map/ppermute | solution.py:577
  36.5 1.2 %collective-permute-start.10 = (bf16[4,208,128]{2,1,0:T(8,128)(2,1)S(1)}, bf16[4,208,128]{2,1,0:T(8,128)(2,1)S(1)}, u32[]{:S(2)}, u32[]{:S(2)}) collective-permute-start(bf16[4,208,128]{2,1,0:T(8,128)(2,1)S(1)} %bitcast.37), channel_id=1, source_target_pairs={{0,3},{1,2},{2,1},{3,0},{4,7},{5,6},{6,5},{7,4},{8,11},{9,10},{10,... | collective-permute-start | bytes 638984 | tf_op jit(solution)/shard_map/ppermute | solution.py:577
  37.7 1.7 %collective-permute-start.7 = (bf16[2,208,128]{2,1,0:T(8,128)(2,1)S(1)}, bf16[2,208,128]{2,1,0:T(8,128)(2,1)S(1)}, u32[]{:S(2)}, u32[]{:S(2)}) collective-permute-start(bf16[2,208,128]{2,1,0:T(8,128)(2,1)S(1)} %far_sum_0.1.token.mine), channel_id=1, source_target_pairs={{0,8},{4,12},{8,0},{12,4},{1,9},{5,13},{9,1},{13,5},{2,10},{6,14},... | collective-permute-start | bytes 319496 | tf_op jit(solution)/shard_map/ppermute | solution.py:577
  39.4 3.9 %inputs_0.1 = (f32[2048,512]{1,0:T(8,128)}, f32[80,2048]{1,0:T(8,128)}, f32[8,128]{1,0:T(8,128)S(1)}) custom-call(bf16[2,208,128]{2,1,0:T(8,128)(2,1)S(1)} %far_sum_0.1.token.mine, bf16[256,256]{1,0:T(8,128)(2,1)S(1)} %get-tuple-element.109.received.refs_0_, bf16[2048,512]{1,0:T(8,128)(2,1)S(1)} %get-tuple-element.82.gout, ...), custom_call_target="tpu_custom_call" | custom-call | flops 1 | bytes 1 | tf_op jit(solution)/shard_map/inputs_0/pallas_call | solution.py:502
  45.4 1.8 %collective-permute-done.11.refs_1_ = bf16[2,208,128]{2,1,0:T(8,128)(2,1)S(1)} collective-permute-done((bf16[2,208,128]{2,1,0:T(8,128)(2,1)S(1)}, bf16[2,208,128]{2,1,0:T(8,128)(2,1)S(1)}, u32[]{:S(2)}, u32[]{:S(2)}) %collective-permute-start.11) | collective-permute-done | bytes 106528 | tf_op jit(solution)/shard_map/ppermute | solution.py:577
  47.2 1.2 %collective-permute-start.14 = (bf16[4,208,128]{2,1,0:T(8,128)(2,1)S(1)}, bf16[4,208,128]{2,1,0:T(8,128)(2,1)S(1)}, u32[]{:S(2)}, u32[]{:S(2)}) collective-permute-start(bf16[4,208,128]{2,1,0:T(8,128)(2,1)S(1)} %far_join_0.1.token), channel_id=1, source_target_pairs={{0,3},{1,2},{2,1},{3,0},{4,7},{5,6},{6,5},{7,4},{8,11},{9,10},{10,... | collective-permute-start | bytes 638984 | tf_op jit(solution)/shard_map/ppermute | solution.py:577
  48.4 1.1 %collective-permute-start.16 = (bf16[4,208,128]{2,1,0:T(8,128)(2,1)S(1)}, bf16[4,208,128]{2,1,0:T(8,128)(2,1)S(1)}, u32[]{:S(2)}, u32[]{:S(2)}) collective-permute-start(bf16[4,208,128]{2,1,0:T(8,128)(2,1)S(1)} %far_join_0.1.token), channel_id=1, source_target_pairs={{0,2},{1,3},{2,0},{3,1},{4,6},{5,7},{6,4},{7,5},{8,10},{9,11},{10,... | collective-permute-start | bytes 638984 | tf_op jit(solution)/shard_map/ppermute | solution.py:577
  49.9 2.4 %collective-permute-start.13 = (bf16[2,208,128]{2,1,0:T(8,128)(2,1)S(1)}, bf16[2,208,128]{2,1,0:T(8,128)(2,1)S(1)}, u32[]{:S(2)}, u32[]{:S(2)}) collective-permute-start(bf16[2,208,128]{2,1,0:T(8,128)(2,1)S(1)} %far_sum_1.1.token.mine), channel_id=1, source_target_pairs={{0,8},{4,12},{8,0},{12,4},{1,9},{5,13},{9,1},{13,5},{2,10},{6,14},... | collective-permute-start | bytes 319496 | tf_op jit(solution)/shard_map/ppermute | solution.py:577
  52.3 3.6 %outputs.1 = (bf16[2048,512]{1,0:T(8,128)(2,1)}, bf16[2048,512]{1,0:T(8,128)(2,1)}, f32[8,128]{1,0:T(8,128)S(1)}) custom-call(bf16[2,208,128]{2,1,0:T(8,128)(2,1)S(1)} %far_sum_1.1.token.mine, s32[16,128]{1,0:T(8,128)S(1)} %get-tuple-element.79.valid, bf16[2048,512]{1,0:T(8,128)(2,1)S(1)} %get-tuple-element.80.sig, ...), custom_call_target="tpu_custom_call" | custom-call | flops 1 | bytes 1 | tf_op jit(solution)/shard_map/outputs/pallas_call | solution.py:447
  56.7 2.9 %collective-permute-start.18 = (bf16[256,512]{1,0:T(8,128)(2,1)S(1)}, bf16[256,512]{1,0:T(8,128)(2,1)S(1)}, u32[]{:S(2)}, u32[]{:S(2)}) collective-permute-start(bf16[256,512]{1,0:T(8,128)(2,1)S(1)} %early.1.token), channel_id=1, source_target_pairs={{1,0},{2,1},{3,2},{4,3},{5,4},{6,5},{7,6},{8,7},{9,8},{10,9},{11,1... | collective-permute-start | bytes 786440 | tf_op jit(solution)/shard_map/ppermute | solution.py:653
  60.1 1.4 %collective-permute-start.19 = (bf16[4,208,128]{2,1,0:T(8,128)(2,1)S(1)}, bf16[4,208,128]{2,1,0:T(8,128)(2,1)S(1)}, u32[]{:S(2)}, u32[]{:S(2)}) collective-permute-start(bf16[4,208,128]{2,1,0:T(8,128)(2,1)S(1)} %far_join_1.1.token), channel_id=1, source_target_pairs={{0,3},{1,2},{2,1},{3,0},{4,7},{5,6},{6,5},{7,4},{8,11},{9,10},{10,... | collective-permute-start | bytes 638984 | tf_op jit(solution)/shard_map/ppermute | solution.py:577
  61.6 8.2 %collective-permute-start.24 = (bf16[4,208,128]{2,1,0:T(8,128)(2,1)S(1)}, bf16[4,208,128]{2,1,0:T(8,128)(2,1)S(1)}, u32[]{:S(2)}, u32[]{:S(2)}) collective-permute-start(bf16[4,208,128]{2,1,0:T(8,128)(2,1)S(1)} %far_join_1.1.token), channel_id=1, source_target_pairs={{0,2},{1,3},{2,0},{3,1},{4,6},{5,7},{6,4},{7,5},{8,10},{9,11},{10,... | collective-permute-start | bytes 638984 | tf_op jit(solution)/shard_map/ppermute | solution.py:577
  69.8 1.7 %collective-permute-start.21 = (bf16[2,4,208,128]{3,2,1,0:T(8,128)(2,1)S(1)}, bf16[2,4,208,128]{3,2,1,0:T(8,128)(2,1)S(1)}, u32[]{:S(2)}, u32[]{:S(2)}) collective-permute-start(bf16[2,4,208,128]{3,2,1,0:T(8,128)(2,1)S(1)} %near_join_0_0.1.token.refs_0_), channel_id=1, source_target_pairs={{0,16},{16,0},{1,17},{17,1},{2,18},{18,2},{3,19},{19,3},{4,20},{20... | collective-permute-start | bytes 1277960 | tf_op jit(solution)/shard_map/ppermute | solution.py:577
  71.4 3.8 %inputs_2.1 = (f32[2048,512]{1,0:T(8,128)}, f32[80,2048]{1,0:T(8,128)}, f32[8,128]{1,0:T(8,128)S(1)}) custom-call(bf16[4,208,128]{2,1,0:T(8,128)(2,1)S(1)} %far_join_1.1.token, bf16[256,512]{1,0:T(8,128)(2,1)S(1)} %collective-permute-done.18.received, bf16[2048,512]{1,0:T(8,128)(2,1)S(1)} %get-tuple-element.82.gout, ...), custom_call_target="tpu_custom_call", output_to_operand_aliasing={{0}: (11, {}), {1}: (12, {})} | custom-call | flops 1 | bytes 1 | tf_op jit(solution)/shard_map/inputs_2/pallas_call | solution.py:502
  75.4 4.4 %collective-permute-done.24 = bf16[4,208,128]{2,1,0:T(8,128)(2,1)S(1)} collective-permute-done((bf16[4,208,128]{2,1,0:T(8,128)(2,1)S(1)}, bf16[4,208,128]{2,1,0:T(8,128)(2,1)S(1)}, u32[]{:S(2)}, u32[]{:S(2)}) %collective-permute-start.24) | collective-permute-done | bytes 213024 | tf_op jit(solution)/shard_map/ppermute | solution.py:577
  79.8 1.0 %collective-permute-done.23 = bf16[4,208,128]{2,1,0:T(8,128)(2,1)S(1)} collective-permute-done((bf16[4,208,128]{2,1,0:T(8,128)(2,1)S(1)}, bf16[4,208,128]{2,1,0:T(8,128)(2,1)S(1)}, u32[]{:S(2)}, u32[]{:S(2)}) %collective-permute-start.23) | collective-permute-done | bytes 213024 | tf_op jit(solution)/shard_map/ppermute | solution.py:577
  81.3 2.0 %unpack_0.1 = (f32[512,1024]{1,0:T(8,128)}, f32[512,1024]{1,0:T(8,128)}, f32[80,1024]{1,0:T(8,128)}, f32[1,1024]{1,0:T(1,128)}, f32[512,512]{1,0:T(8,128)}, /*in...) custom-call(bf16[2,4,208,128]{3,2,1,0:T(8,128)(2,1)S(1)} %collective-permute-done.20.token.refs_2_, ...), custom_call_target="tpu_custom_call" | custom-call | flops 1 | bytes 1 | tf_op jit(solution)/shard_map/unpack_0/pallas_call | solution.py:564
  83.3 2.0 %unpack_1.1 = (f32[512,1024]{1,0:T(8,128)}, f32[512,1024]{1,0:T(8,128)}, f32[80,1024]{1,0:T(8,128)}, f32[1,1024]{1,0:T(1,128)}, f32[512,512]{1,0:T(8,128)}, /*in...) custom-call(f32[8,128]{1,0:T(8,128)S(1)} %get-tuple-element.129.toke, ...), custom_call_target="tpu_custom_call", output_to_operand_aliasing={{0}: (5, {}), {1}: (6, {}), {2}: (7, {}), {3}: (8, {}), {4}... | custom-call | flops 1 | bytes 1 | tf_op jit(solution)/shard_map/unpack_1/pallas_call | solution.py:564
  (49 shorter events, 7.4 us)
Async XLA Ops:
  1.6 11.1 %collective-permute-start = (bf16[256,512]{1,0:T(8,128)(2,1)S(1)}, bf16[256,512]{1,0:T(8,128)(2,1)S(1)}, u32[]{:S(2)}, u32[]{:S(2)}) collective-permute-start(bf16[256,512]{1,0:T(8,128)(2,1)S(1)} %slice.3), channel_id=1, source_target_pairs={{0,1},{1,2},{2,3},{3,4},{4,5},{5,6},{6,7},{7,8},{8,9},{9,10},{10,1... | collective-permute-start | bytes 786440 | tf_op jit(solution)/shard_map/ppermute | solution.py:653
  15.5 5.1 %collective-permute-start.1 = (bf16[4,4,208,128]{3,2,1,0:T(8,128)(2,1)S(1)}, bf16[4,4,208,128]{3,2,1,0:T(8,128)(2,1)S(1)}, u32[]{:S(2)}, u32[]{:S(2)}) collective-permute-start(bf16[4,4,208,128]{3,2,1,0:T(8,128)(2,1)S(1)} %theirs_0.1.token), channel_id=1, source_target_pairs={{0,16},{16,0},{1,17},{17,1},{2,18},{18,2},{3,19},{19,3},{4,20},{20... | collective-permute-start | bytes 2555912 | tf_op jit(solution)/shard_map/ppermute | solution.py:577
  20.8 10.8 %collective-permute-start.2 = (bf16[4,208,128]{2,1,0:T(8,128)(2,1)S(1)}, bf16[4,208,128]{2,1,0:T(8,128)(2,1)S(1)}, u32[]{:S(2)}, u32[]{:S(2)}) collective-permute-start(bf16[4,208,128]{2,1,0:T(8,128)(2,1)S(1)} %bitcast.44), channel_id=1, source_target_pairs={{0,1},{1,0},{2,3},{3,2},{4,5},{5,4},{6,7},{7,6},{8,9},{9,8},{10,11... | collective-permute-start | bytes 638984 | tf_op jit(solution)/shard_map/ppermute | solution.py:577
  21.1 10.5 %collective-permute-start.3 = (bf16[4,208,128]{2,1,0:T(8,128)(2,1)S(1)}, bf16[4,208,128]{2,1,0:T(8,128)(2,1)S(1)}, u32[]{:S(2)}, u32[]{:S(2)}) collective-permute-start(bf16[4,208,128]{2,1,0:T(8,128)(2,1)S(1)} %bitcast.43), channel_id=1, source_target_pairs={{0,2},{1,3},{2,0},{3,1},{4,6},{5,7},{6,4},{7,5},{8,10},{9,11},{10,... | collective-permute-start | bytes 638984 | tf_op jit(solution)/shard_map/ppermute | solution.py:577
  22.4 10.9 %collective-permute-start.4 = (bf16[4,208,128]{2,1,0:T(8,128)(2,1)S(1)}, bf16[4,208,128]{2,1,0:T(8,128)(2,1)S(1)}, u32[]{:S(2)}, u32[]{:S(2)}) collective-permute-start(bf16[4,208,128]{2,1,0:T(8,128)(2,1)S(1)} %bitcast.41), channel_id=1, source_target_pairs={{0,3},{1,2},{2,1},{3,0},{4,7},{5,6},{6,5},{7,4},{8,11},{9,10},{10,... | collective-permute-start | bytes 638984 | tf_op jit(solution)/shard_map/ppermute | solution.py:577
  28.5 6.3 %collective-permute-start.5 = (bf16[4,4,208,128]{3,2,1,0:T(8,128)(2,1)S(1)}, bf16[4,4,208,128]{3,2,1,0:T(8,128)(2,1)S(1)}, u32[]{:S(2)}, u32[]{:S(2)}) collective-permute-start(bf16[4,4,208,128]{3,2,1,0:T(8,128)(2,1)S(1)} %theirs_1.1.token), channel_id=1, source_target_pairs={{0,16},{16,0},{1,17},{17,1},{2,18},{18,2},{3,19},{19,3},{4,20},{20... | collective-permute-start | bytes 2555912 | tf_op jit(solution)/shard_map/ppermute | solution.py:577
  33.4 4.3 %collective-permute-start.6 = (bf16[2,208,128]{2,1,0:T(8,128)(2,1)S(1)}, bf16[2,208,128]{2,1,0:T(8,128)(2,1)S(1)}, u32[]{:S(2)}, u32[]{:S(2)}) collective-permute-start(bf16[2,208,128]{2,1,0:T(8,128)(2,1)S(1)} %get-tuple-element.108), channel_id=1, source_target_pairs={{0,4},{4,0},{8,12},{12,8},{1,5},{5,1},{9,13},{13,9},{2,6},{6,2},{1... | collective-permute-start | bytes 319496 | tf_op jit(solution)/shard_map/ppermute | solution.py:577
  35.0 9.3 %collective-permute-start.8 = (bf16[4,208,128]{2,1,0:T(8,128)(2,1)S(1)}, bf16[4,208,128]{2,1,0:T(8,128)(2,1)S(1)}, u32[]{:S(2)}, u32[]{:S(2)}) collective-permute-start(bf16[4,208,128]{2,1,0:T(8,128)(2,1)S(1)} %bitcast.42), channel_id=1, source_target_pairs={{0,1},{1,0},{2,3},{3,2},{4,5},{5,4},{6,7},{7,6},{8,9},{9,8},{10,11... | collective-permute-start | bytes 638984 | tf_op jit(solution)/shard_map/ppermute | solution.py:577
  35.3 8.9 %collective-permute-start.9 = (bf16[4,208,128]{2,1,0:T(8,128)(2,1)S(1)}, bf16[4,208,128]{2,1,0:T(8,128)(2,1)S(1)}, u32[]{:S(2)}, u32[]{:S(2)}) collective-permute-start(bf16[4,208,128]{2,1,0:T(8,128)(2,1)S(1)} %bitcast.39), channel_id=1, source_target_pairs={{0,2},{1,3},{2,0},{3,1},{4,6},{5,7},{6,4},{7,5},{8,10},{9,11},{10,... | collective-permute-start | bytes 638984 | tf_op jit(solution)/shard_map/ppermute | solution.py:577
  36.5 8.6 %collective-permute-start.10 = (bf16[4,208,128]{2,1,0:T(8,128)(2,1)S(1)}, bf16[4,208,128]{2,1,0:T(8,128)(2,1)S(1)}, u32[]{:S(2)}, u32[]{:S(2)}) collective-permute-start(bf16[4,208,128]{2,1,0:T(8,128)(2,1)S(1)} %bitcast.37), channel_id=1, source_target_pairs={{0,3},{1,2},{2,1},{3,0},{4,7},{5,6},{6,5},{7,4},{8,11},{9,10},{10,... | collective-permute-start | bytes 638984 | tf_op jit(solution)/shard_map/ppermute | solution.py:577
  37.7 5.7 %collective-permute-start.7 = (bf16[2,208,128]{2,1,0:T(8,128)(2,1)S(1)}, bf16[2,208,128]{2,1,0:T(8,128)(2,1)S(1)}, u32[]{:S(2)}, u32[]{:S(2)}) collective-permute-start(bf16[2,208,128]{2,1,0:T(8,128)(2,1)S(1)} %far_sum_0.1.token.mine), channel_id=1, source_target_pairs={{0,8},{4,12},{8,0},{12,4},{1,9},{5,13},{9,1},{13,5},{2,10},{6,14},... | collective-permute-start | bytes 319496 | tf_op jit(solution)/shard_map/ppermute | solution.py:577
  43.4 3.8 %collective-permute-start.11 = (bf16[2,208,128]{2,1,0:T(8,128)(2,1)S(1)}, bf16[2,208,128]{2,1,0:T(8,128)(2,1)S(1)}, u32[]{:S(2)}, u32[]{:S(2)}) collective-permute-start(bf16[2,208,128]{2,1,0:T(8,128)(2,1)S(1)} %far_end_0.1.token.refs_0_), channel_id=1, source_target_pairs={{0,4},{4,0},{8,12},{12,8},{1,5},{5,1},{9,13},{13,9},{2,6},{6,2},{1... | collective-permute-start | bytes 319496 | tf_op jit(solution)/shard_map/ppermute | solution.py:577
  45.1 4.8 %collective-permute-start.12 = (bf16[2,208,128]{2,1,0:T(8,128)(2,1)S(1)}, bf16[2,208,128]{2,1,0:T(8,128)(2,1)S(1)}, u32[]{:S(2)}, u32[]{:S(2)}) collective-permute-start(bf16[2,208,128]{2,1,0:T(8,128)(2,1)S(1)} %get-tuple-element.115), channel_id=1, source_target_pairs={{0,4},{4,0},{8,12},{12,8},{1,5},{5,1},{9,13},{13,9},{2,6},{6,2},{1... | collective-permute-start | bytes 319496 | tf_op jit(solution)/shard_map/ppermute | solution.py:577
  47.2 12.4 %collective-permute-start.14 = (bf16[4,208,128]{2,1,0:T(8,128)(2,1)S(1)}, bf16[4,208,128]{2,1,0:T(8,128)(2,1)S(1)}, u32[]{:S(2)}, u32[]{:S(2)}) collective-permute-start(bf16[4,208,128]{2,1,0:T(8,128)(2,1)S(1)} %far_join_0.1.token), channel_id=1, source_target_pairs={{0,3},{1,2},{2,1},{3,0},{4,7},{5,6},{6,5},{7,4},{8,11},{9,10},{10,... | collective-permute-start | bytes 638984 | tf_op jit(solution)/shard_map/ppermute | solution.py:577
  48.4 11.2 %collective-permute-start.16 = (bf16[4,208,128]{2,1,0:T(8,128)(2,1)S(1)}, bf16[4,208,128]{2,1,0:T(8,128)(2,1)S(1)}, u32[]{:S(2)}, u32[]{:S(2)}) collective-permute-start(bf16[4,208,128]{2,1,0:T(8,128)(2,1)S(1)} %far_join_0.1.token), channel_id=1, source_target_pairs={{0,2},{1,3},{2,0},{3,1},{4,6},{5,7},{6,4},{7,5},{8,10},{9,11},{10,... | collective-permute-start | bytes 638984 | tf_op jit(solution)/shard_map/ppermute | solution.py:577
  49.5 10.2 %collective-permute-start.15 = (bf16[4,208,128]{2,1,0:T(8,128)(2,1)S(1)}, bf16[4,208,128]{2,1,0:T(8,128)(2,1)S(1)}, u32[]{:S(2)}, u32[]{:S(2)}) collective-permute-start(bf16[4,208,128]{2,1,0:T(8,128)(2,1)S(1)} %far_join_0.1.token), channel_id=1, source_target_pairs={{0,1},{1,0},{2,3},{3,2},{4,5},{5,4},{6,7},{7,6},{8,9},{9,8},{10,11... | collective-permute-start | bytes 638984 | tf_op jit(solution)/shard_map/ppermute | solution.py:577
  49.9 6.0 %collective-permute-start.13 = (bf16[2,208,128]{2,1,0:T(8,128)(2,1)S(1)}, bf16[2,208,128]{2,1,0:T(8,128)(2,1)S(1)}, u32[]{:S(2)}, u32[]{:S(2)}) collective-permute-start(bf16[2,208,128]{2,1,0:T(8,128)(2,1)S(1)} %far_sum_1.1.token.mine), channel_id=1, source_target_pairs={{0,8},{4,12},{8,0},{12,4},{1,9},{5,13},{9,1},{13,5},{2,10},{6,14},... | collective-permute-start | bytes 319496 | tf_op jit(solution)/shard_map/ppermute | solution.py:577
  55.9 4.2 %collective-permute-start.17 = (bf16[2,208,128]{2,1,0:T(8,128)(2,1)S(1)}, bf16[2,208,128]{2,1,0:T(8,128)(2,1)S(1)}, u32[]{:S(2)}, u32[]{:S(2)}) collective-permute-start(bf16[2,208,128]{2,1,0:T(8,128)(2,1)S(1)} %far_end_1.1.token.refs_0_), channel_id=1, source_target_pairs={{0,4},{4,0},{8,12},{12,8},{1,5},{5,1},{9,13},{13,9},{2,6},{6,2},{1... | collective-permute-start | bytes 319496 | tf_op jit(solution)/shard_map/ppermute | solution.py:577
  56.7 13.1 %collective-permute-start.18 = (bf16[256,512]{1,0:T(8,128)(2,1)S(1)}, bf16[256,512]{1,0:T(8,128)(2,1)S(1)}, u32[]{:S(2)}, u32[]{:S(2)}) collective-permute-start(bf16[256,512]{1,0:T(8,128)(2,1)S(1)} %early.1.token), channel_id=1, source_target_pairs={{1,0},{2,1},{3,2},{4,3},{5,4},{6,5},{7,6},{8,7},{9,8},{10,9},{11,1... | collective-permute-start | bytes 786440 | tf_op jit(solution)/shard_map/ppermute | solution.py:653
  60.1 15.1 %collective-permute-start.19 = (bf16[4,208,128]{2,1,0:T(8,128)(2,1)S(1)}, bf16[4,208,128]{2,1,0:T(8,128)(2,1)S(1)}, u32[]{:S(2)}, u32[]{:S(2)}) collective-permute-start(bf16[4,208,128]{2,1,0:T(8,128)(2,1)S(1)} %far_join_1.1.token), channel_id=1, source_target_pairs={{0,3},{1,2},{2,1},{3,0},{4,7},{5,6},{6,5},{7,4},{8,11},{9,10},{10,... | collective-permute-start | bytes 638984 | tf_op jit(solution)/shard_map/ppermute | solution.py:577
  61.6 18.2 %collective-permute-start.24 = (bf16[4,208,128]{2,1,0:T(8,128)(2,1)S(1)}, bf16[4,208,128]{2,1,0:T(8,128)(2,1)S(1)}, u32[]{:S(2)}, u32[]{:S(2)}) collective-permute-start(bf16[4,208,128]{2,1,0:T(8,128)(2,1)S(1)} %far_join_1.1.token), channel_id=1, source_target_pairs={{0,2},{1,3},{2,0},{3,1},{4,6},{5,7},{6,4},{7,5},{8,10},{9,11},{10,... | collective-permute-start | bytes 638984 | tf_op jit(solution)/shard_map/ppermute | solution.py:577
  69.7 11.1 %collective-permute-start.23 = (bf16[4,208,128]{2,1,0:T(8,128)(2,1)S(1)}, bf16[4,208,128]{2,1,0:T(8,128)(2,1)S(1)}, u32[]{:S(2)}, u32[]{:S(2)}) collective-permute-start(bf16[4,208,128]{2,1,0:T(8,128)(2,1)S(1)} %far_join_1.1.token), channel_id=1, source_target_pairs={{0,1},{1,0},{2,3},{3,2},{4,5},{5,4},{6,7},{7,6},{8,9},{9,8},{10,11... | collective-permute-start | bytes 638984 | tf_op jit(solution)/shard_map/ppermute | solution.py:577
  69.7 11.6 %collective-permute-start.22 = (bf16[2,4,208,128]{3,2,1,0:T(8,128)(2,1)S(1)}, bf16[2,4,208,128]{3,2,1,0:T(8,128)(2,1)S(1)}, u32[]{:S(2)}, u32[]{:S(2)}) collective-permute-start(bf16[2,4,208,128]{3,2,1,0:T(8,128)(2,1)S(1)} %near_join_0_1.1.token.refs_1_), channel_id=1, source_target_pairs={{0,16},{16,0},{1,17},{17,1},{2,18},{18,2},{3,19},{19,3},{4,20},{20... | collective-permute-start | bytes 1277960 | tf_op jit(solution)/shard_map/ppermute | solution.py:577
  69.8 11.6 %collective-permute-start.21 = (bf16[2,4,208,128]{3,2,1,0:T(8,128)(2,1)S(1)}, bf16[2,4,208,128]{3,2,1,0:T(8,128)(2,1)S(1)}, u32[]{:S(2)}, u32[]{:S(2)}) collective-permute-start(bf16[2,4,208,128]{3,2,1,0:T(8,128)(2,1)S(1)} %near_join_0_0.1.token.refs_0_), channel_id=1, source_target_pairs={{0,16},{16,0},{1,17},{17,1},{2,18},{18,2},{3,19},{19,3},{4,20},{20... | collective-permute-start | bytes 1277960 | tf_op jit(solution)/shard_map/ppermute | solution.py:577
  75.3 6.1 %collective-permute-start.20 = (bf16[2,4,208,128]{3,2,1,0:T(8,128)(2,1)S(1)}, bf16[2,4,208,128]{3,2,1,0:T(8,128)(2,1)S(1)}, u32[]{:S(2)}, u32[]{:S(2)}) collective-permute-start(bf16[2,4,208,128]{3,2,1,0:T(8,128)(2,1)S(1)} %near_join_1_0.1.token.refs_0_), channel_id=1, source_target_pairs={{0,16},{16,0},{1,17},{17,1},{2,18},{18,2},{3,19},{19,3},{4,20},{20... | collective-permute-start | bytes 1277960 | tf_op jit(solution)/shard_map/ppermute | solution.py:577
  80.8 2.5 %collective-permute-start.25 = (bf16[2,4,208,128]{3,2,1,0:T(8,128)(2,1)S(1)}, bf16[2,4,208,128]{3,2,1,0:T(8,128)(2,1)S(1)}, u32[]{:S(2)}, u32[]{:S(2)}) collective-permute-start(bf16[2,4,208,128]{3,2,1,0:T(8,128)(2,1)S(1)} %near_join_1_1.1.refs_1_), channel_id=1, source_target_pairs={{0,16},{16,0},{1,17},{17,1},{2,18},{18,2},{3,19},{19,3},{4,20},{20... | collective-permute-start | bytes 1277960 | tf_op jit(solution)/shard_map/ppermute | solution.py:577
where the time goes:
time: 85.8 us; the launch traced here: 85.4 us
  Pallas kernels  38.6 us (45%)
  starting transfers between devices  34.7 us (40%)
  waiting for transfers between devices  10.2 us (12%)
  between operations  1 us (1%)
  local copies, waits for them, and re-layouts  0.97 us (1%)
    ppermute x24, starting transfers between devices, swapped(): lax.ppermute(x, axis, [(i, i ^ k) for i in range(lax.axis_size(axis))])  28.7 us
    ppermute x24, waiting for transfers between devices, swapped(): lax.ppermute(x, axis, [(i, i ^ k) for i in range(lax.axis_size(axis))])  10.2 us
    pallas_call x4, Pallas kernels, gradients(): call(functools.partial(gradients_body, far, block, half, own, count), ('m...  8.35 us
    pallas_call x1, Pallas kernels, load(): call(load_body, 'load', [ANYWHERE] * len(sources), [VMEM] * len(shapes),...  7.95 us
    pallas_call x2, Pallas kernels, inputs(): call(functools.partial(inputs_body, steps, counts), f'inputs_{steps[0]}',...  7.67 us
    ppermute x2, starting transfers between devices, passed_along(): return lax.ppermute(x, AXES, pairs)  6.03 us
    pallas_call x2, Pallas kernels, unpack(): call(functools.partial(unpack_body, far, block), f'unpack_{half}', [ANYWH...  4 us
    pallas_call x1, Pallas kernels, outputs(): call(functools.partial(outputs_body, counts), 'outputs', [ANYWHERE] + [VM...  3.61 us
  transfers between devices with their start and end apart: 26, of which 6 were waited for; matrix products, arithmetic and copies ran while one was open for 0% of the time, Pallas kernels for 39%

commit v1 on v0

--- a/solution.py
+++ b/solution.py
@@ -96,17 +96,33 @@
 
 def gate_product(half, k, rows, past, sig, feats, w_in, w_cond, b_conv):
     width = sig.shape[1]
-    part = w_in.shape[1] // 2 // HALVES
-    at = (k * HALVES + half) * part
-    here = slice(at, at + part)
+    part = w_in.shape[1] // 2
+    here = slice(k * part, (k + 1) * part)
+    there = slice((k * HALVES + half) * part, (k * HALVES + half + 1) * part)
     own = dot(past, w_in[:width, here]) + dot(sig[rows, :], w_in[width:, here])
-    return own + across(feats, w_cond[:, here]) + b_conv[:, here]
-
-
-def back_product(half, rows, gout, gskip, w_res, w_skip):
+    return own + across(feats, w_cond[:, there]) + b_conv[:, there]
+
+
+def back_product(rows, gout, gskip, w_res, w_skip):
+    return against(gout[rows, :], w_res[...]) + against(gskip[rows, :], w_skip[...])
+
+
+def weight_copies(half, w_past, w_now, w_res, w_skip, w_in_to, w_res_to, w_skip_to):
+    width = w_past.shape[0]
+    part = w_res_to.shape[0]
+    pairs = []
+    for k in range(2):
+        here = pl.ds((k * HALVES + half) * part, part)
+        for i, ref in enumerate((w_past, w_now)):
+            pairs.append((ref.at[:, here], w_in_to.at[pl.ds(i * width, width), pl.ds(k * part, part)]))
+    rows = pl.ds(half * part, part)
+    return pairs + [(w_res.at[rows], w_res_to), (w_skip.at[rows], w_skip_to)]
+
+
+def half_weights(w_past, w_res, w_skip):
     part = w_res.shape[0] // HALVES
-    here = slice(half * part, (half + 1) * part)
-    return against(gout[rows, :], w_res[here, :]) + against(gskip[rows, :], w_skip[here, :])
+    shapes = ((2 * w_past.shape[0], 2 * part), (part, w_res.shape[1]), (part, w_skip.shape[1]))
+    return [jax.ShapeDtypeStruct(shape, BF16) for shape in shapes]
 
 
 def finish(pre_a, pre_s, dgated, valid_lines):
@@ -128,7 +144,7 @@
         if arrive:
             arrive(rows, k)
         if k == 2:
-            return back_product(half, rows, gout, gskip, w_res, w_skip)
+            return back_product(rows, gout, gskip, w_res, w_skip)
         feats = x_turned[2 * width : 2 * width + cond, rows]
         return gate_product(half, k, rows, past[rows, :], sig, feats, w_in, w_cond, b_conv)
 
@@ -152,12 +168,12 @@
 
 
 def split_rows(rows):
-    return rows // 2
+    return 3 * DILATION_STEP
 
 
 def load_body(
-    valid, pos, b_conv, b_res, b_skip, feat, w_cond, w_res, w_skip, w_past, w_now, sig, gout, gskip,
-    valid_to, pos_to, b_conv_to, b_res_to, b_skip_to, w_cond_to, w_res_to, w_skip_to, w_in, past, sig_to, x_turned,
+    valid, pos, b_conv, feat, w_cond, w_res, w_skip, w_past, w_now, sig, gout, gskip,
+    valid_to, pos_to, b_conv_to, w_cond_to, w_in, w_res_to, w_skip_to, past, sig_to, x_turned,
     gout_to, gskip_to, gated_rest, kept_rest, dpre_rest, sems,
 ):
     rows_all, width = sig.shape
@@ -175,24 +191,23 @@
         rows = pl.ds(i * ROWS, ROWS)
         return start(source.at[rows], target.at[rows])
 
+    weights = weight_copies(0, w_past, w_now, w_res, w_skip, w_in, w_res_to, w_skip_to)
     signals = [[tile(0, sig, sig_to)]]
     needs = [
         [
             start(pos, pos_to),
-            start(w_past, w_in.at[pl.ds(0, width)]),
-            start(w_now, w_in.at[pl.ds(width, width)]),
+            *(start(*pair) for pair in weights[:2]),
             start(feat, x_turned.at[pl.ds(2 * width, cond)]),
             start(w_cond, w_cond_to),
             start(b_conv, b_conv_to),
         ],
-        [],
-        [start(valid, valid_to), start(w_res, w_res_to), start(w_skip, w_skip_to)],
+        [start(*pair) for pair in weights[2:4]],
+        [start(valid, valid_to), *(start(*pair) for pair in weights[4:])],
     ]
     cotangents = [[tile(0, gout, gout_to), tile(0, gskip, gskip_to)]]
     for i in range(1, rows_all // ROWS):
         signals.append([tile(i, sig, sig_to)])
         cotangents.append([tile(i, gout, gout_to), tile(i, gskip, gskip_to)])
-    last = [start(b_res, b_res_to), start(b_skip, b_skip_to)]
 
     def wait(copies):
         for copy in copies:
@@ -220,7 +235,6 @@
         0, tiles_of(DILATION_STEP, rows_all), prepare, arrive, valid_to, past, sig_to, x_turned, gout_to, gskip_to,
         (w_in, w_cond_to, b_conv_to, w_res_to, w_skip_to), (gated_rest, kept_rest, dpre_rest), DILATION_STEP,
     )
-    wait(last)
 
 
 def rest_shapes(rest, part):
@@ -229,13 +243,14 @@
 
 def load(*arrays):
     sources = [in_hbm(x) for x in arrays]
-    feat, w_cond, w_res, w_skip, w_past, w_now, sig, gout, gskip = arrays[5:]
+    feat, w_cond, w_res, w_skip, w_past, _, sig, gout, gskip = arrays[3:]
     rows, width = sig.shape
     hidden = w_res.shape[0]
-    shapes = [jax.ShapeDtypeStruct(x.shape, x.dtype) for x in arrays[:5] + (w_cond, w_res, w_skip)] + [
+    shapes = [jax.ShapeDtypeStruct(x.shape, x.dtype) for x in arrays[:3] + (w_cond,)]
+    shapes += half_weights(w_past, w_res, w_skip) + [
         jax.ShapeDtypeStruct(shape, BF16)
         for shape in (
-            (2 * width, 2 * hidden), sig.shape, sig.shape, (2 * width + feat.shape[0] + ONES, rows), gout.shape, gskip.shape,
+            sig.shape, sig.shape, (2 * width + feat.shape[0] + ONES, rows), gout.shape, gskip.shape,
         )
     ]
     shapes += rest_shapes(rows - DILATION_STEP, hidden // HALVES)
@@ -261,7 +276,7 @@
     feats = x_turned[2 * width : 2 * width + w_cond.shape[0], rows]
     past = halo[...] * column(tap_of(lines_of(pos, rows)).astype(F32)).astype(BF16)
     made = [gate_product(half, k, rows, past, sig, feats, w_in, w_cond, b_conv) for k in range(2)]
-    made.append(back_product(half, rows, gout, gskip, w_res, w_skip))
+    made.append(back_product(rows, gout, gskip, w_res, w_skip))
     for ref, value in zip(outs, finish(*made, lines_of(valid, rows))):
         ref[...] = value
 
@@ -274,7 +289,7 @@
 
 def head(halo, *args):
     width = halo.shape[1]
-    part = args[-1].shape[0] // HALVES
+    part = args[-1].shape[0]
     past, *parts = call(
         head_body,
         "head",
@@ -285,19 +300,20 @@
     return past, parts
 
 
-def early_body(token, pos, dpre_0, dpre_1, w_in, early):
+def early_body(token, pos, dpre_0, dpre_1, w_in_0, w_in_1, early):
     tap = column(tap_of(lines_of(pos, slice(0, DILATION_STEP))))
-    early[...] = (tap * against(side_by_side(dpre_0[...], dpre_1[...]), w_in[: early.shape[1], :])).astype(BF16)
-
-
-def early_rows(token, pos, dpre_0, dpre_1, w_in):
+    some = slice(0, early.shape[1])
+    early[...] = (tap * (against(dpre_0[...], w_in_0[some, :]) + against(dpre_1[...], w_in_1[some, :]))).astype(BF16)
+
+
+def early_rows(token, pos, dpre_0, dpre_1, w_in_0, w_in_1):
     return call(
         early_body,
         "early",
-        [ANYWHERE] + [VMEM] * 4,
+        [ANYWHERE] + [VMEM] * 5,
         VMEM,
-        jax.ShapeDtypeStruct((DILATION_STEP, w_in.shape[0] // 2), BF16),
-    )(token, pos, dpre_0, dpre_1, w_in)
+        jax.ShapeDtypeStruct((DILATION_STEP, w_in_0.shape[0] // 2), BF16),
+    )(token, pos, dpre_0, dpre_1, w_in_0, w_in_1)
 
 
 def most_body(token, valid, past, sig, x_turned, gout, gskip, w_in, w_cond, b_conv, w_res, w_skip, *outs):
@@ -308,7 +324,7 @@
 
 
 def forward_most(token, *args):
-    part = args[-1].shape[0] // HALVES
+    part = args[-1].shape[0]
     return call(
         most_body,
         "forward_1",
@@ -329,7 +345,7 @@
 
 
 def forward_ends(token, *args):
-    part = args[-1].shape[0] // HALVES
+    part = args[-1].shape[0]
     rows = args[4].shape[0]
     parts = call(
         ends_body,
@@ -353,8 +369,16 @@
     return result
 
 
-def gradients_body(far, block, half, own, count, token, valid, x_turned, gout, gskip, past_head, *refs):
-    kepts, dpres, (out, acc) = refs[:count], refs[count : 2 * count], refs[2 * count :]
+def gradients_body(far, block, half, own, count, extra, token, valid, x_turned, gout, gskip, past_head, *refs):
+    kepts, dpres, refs = refs[:count], refs[count : 2 * count], refs[2 * count :]
+    sources, (out, *targets) = refs[:extra], refs[extra : len(refs) - 1 - bool(extra)]
+    acc = refs[-1 - bool(extra)]
+    copies = []
+    if extra:
+        pairs = weight_copies(1, *sources[:4], *targets[:3]) + list(zip(sources[4:], targets[3:]))
+        copies = [pltpu.make_async_copy(*pair, refs[-1].at[k]) for k, pair in enumerate(pairs)]
+    for copy in copies:
+        copy.start()
     width = past_head.shape[0]
     part = kepts[0].shape[0]
     ends, rows = x_turned.shape
@@ -405,33 +429,41 @@
 
     for k in range(2):
         pl.when(which == k)(functools.partial(region, k))
-
-
-def gradients(half, own, token, far, block, valid, x_turned, gout, gskip, past_head, pieces):
+    for copy in copies:
+        copy.wait()
+
+
+def gradients(half, own, token, far, block, valid, x_turned, gout, gskip, past_head, pieces, loads=()):
     packed = (NEAR, far, block, LANES)
     wide = pieces[0][2].shape[1]
     count = len(pieces)
+    sources = [in_hbm(x) for x in loads]
+    outs = [jax.ShapeDtypeStruct(packed, F32 if own else BF16)]
+    scratch = [pltpu.VMEM((far * block, wide), F32)]
+    if loads:
+        outs += half_weights(loads[0], *loads[2:4]) + [jax.ShapeDtypeStruct(x.shape, x.dtype) for x in loads[4:]]
+        scratch.append(pltpu.SemaphoreType.DMA((6 + len(loads[4:]),)))
     return call(
-        functools.partial(gradients_body, far, block, half, own, count),
+        functools.partial(gradients_body, far, block, half, own, count, len(loads)),
         ("mine" if own else "theirs") + f"_{half}",
-        [ANYWHERE] + [VMEM] * (5 + 2 * count),
-        VMEM,
-        jax.ShapeDtypeStruct(packed, F32 if own else BF16),
-        scratch=[pltpu.VMEM((far * block, wide), F32)],
-    )(token, valid, x_turned, gout, gskip, past_head, *(p[1] for p in pieces), *(p[2] for p in pieces))
-
-
-def outputs_body(counts, token, valid, sig, w_res, w_skip, b_res, b_skip, *refs):
+        [ANYWHERE] + [VMEM] * (5 + 2 * count) + [ANYWHERE] * len(loads),
+        [VMEM] * len(outs),
+        outs,
+        scratch=scratch,
+    )(token, valid, x_turned, gout, gskip, past_head, *(p[1] for p in pieces), *(p[2] for p in pieces), *sources)
+
+
+def outputs_body(counts, token, valid, sig, w_res_0, w_skip_0, w_res_1, w_skip_1, b_res, b_skip, *refs):
     first, second = refs[: counts[0]], refs[counts[0] : sum(counts)]
     out, skip, mark, rooms, sems = refs[sum(counts) :]
     copies = []
     for i in range(sig.shape[0] // ROWS):
         rows = slice(i * ROWS, (i + 1) * ROWS)
         mask = column(lines_of(valid, rows))
-        gated = beside(picked(first, rows), picked(second, rows))
-        branch = dot(gated, w_res[...]) + b_res[...]
+        left, right = picked(first, rows), picked(second, rows)
+        branch = dot(left, w_res_0[...]) + dot(right, w_res_1[...]) + b_res[...]
         rooms[i, 0] = (sig[rows, :].astype(F32) + mask * branch).astype(BF16)
-        side = dot(gated, w_skip[...]) + b_skip[...]
+        side = dot(left, w_skip_0[...]) + dot(right, w_skip_1[...]) + b_skip[...]
         rooms[i, 1] = (mask * side).astype(BF16)
         for k, ref in enumerate((out, skip)):
             copies.append(pltpu.make_async_copy(rooms.at[i, k], ref.at[pl.ds(i * ROWS, ROWS)], sems.at[i, k]))
@@ -441,27 +473,27 @@
         copy.wait()
 
 
-def outputs(token, valid, sig, gated_0, gated_1, w_res, w_skip, b_res, b_skip):
+def outputs(token, valid, sig, gated_0, gated_1, weights_0, weights_1, b_res, b_skip):
     rows, width = sig.shape
     counts = (len(gated_0), len(gated_1))
     return call(
         functools.partial(outputs_body, counts),
         "outputs",
-        [ANYWHERE] + [VMEM] * (6 + sum(counts)),
+        [ANYWHERE] + [VMEM] * (8 + sum(counts)),
         [ANYWHERE, ANYWHERE, VMEM],
         [
             jax.ShapeDtypeStruct((rows, width), BF16),
-            jax.ShapeDtypeStruct((rows, w_skip.shape[1]), BF16),
+            jax.ShapeDtypeStruct((rows, weights_0[1].shape[1]), BF16),
             MARK,
         ],
         scratch=[
             pltpu.VMEM((rows // ROWS, 2, ROWS, width), BF16),
             pltpu.SemaphoreType.DMA((rows // ROWS, 2)),
         ],
-    )(token, valid, sig, w_res, w_skip, b_res, b_skip, *gated_0, *gated_1)
-
-
-def inputs_body(steps, counts, token, received, gout, pos, w_in, w_cond, *refs):
+    )(token, valid, sig, *weights_0, *weights_1, b_res, b_skip, *gated_0, *gated_1)
+
+
+def inputs_body(steps, counts, token, received, gout, pos, w_in_0, w_in_1, w_cond, *refs):
     first, second = refs[: counts[0]], refs[counts[0] : sum(counts)]
     gsig, gfeat, mark, room, room_feat, sems = refs[-6:]
     rows, width = gout.shape
@@ -476,29 +508,31 @@
         begin = step * ROWS
         here = slice(begin, begin + ROWS)
         after = slice(begin + DILATION_STEP, min(begin + DILATION_STEP + ROWS, rows))
-        now = side_by_side(picked(first, here), picked(second, here))
-        later = side_by_side(picked(first, after), picked(second, after))
+        now = [picked(pieces, here) for pieces in (first, second)]
+        later = [picked(pieces, after) for pieces in (first, second)]
         tap = column(tap_of(lines_of(pos, after)))
-        room_feat[i] = against(w_cond[...], now)
+        room_feat[i] = against(w_cond[...], side_by_side(*now))
         copy(room_feat.at[i], gfeat.at[:, pl.ds(begin, ROWS)])
         for k in range(width // wide):
             some = slice(k * wide, (k + 1) * wide)
-            tail = tap * against(later, w_in[some, :])
+            tail = tap * (against(later[0], w_in_0[some, :]) + against(later[1], w_in_1[some, :]))
             if tail.shape[0] < ROWS:
                 tail = below(tail, received[:, some].astype(F32))
-            room[i, k] = gout[here, some].astype(F32) + against(now, w_in[width + k * wide : width + (k + 1) * wide, :]) + tail
+            below_past = slice(width + k * wide, width + (k + 1) * wide)
+            own = against(now[0], w_in_0[below_past, :]) + against(now[1], w_in_1[below_past, :])
+            room[i, k] = gout[here, some].astype(F32) + own + tail
             copy(room.at[i, k], gsig.at[pl.ds(begin, ROWS), pl.ds(k * wide, wide)])
     mark[...] = jnp.zeros_like(mark)
     for one in copies:
         one.wait()
 
 
-def inputs(steps, token, received, gout, pos, dpre_0, dpre_1, w_in, w_cond, before):
+def inputs(steps, token, received, gout, pos, dpre_0, dpre_1, w_in_0, w_in_1, w_cond, before):
     rows, width = gout.shape
     cond = w_cond.shape[0]
     count = width // (2 * LANES)
     counts = (len(dpre_0), len(dpre_1))
-    operands = 6 + sum(counts)
+    operands = 7 + sum(counts)
     return call(
         functools.partial(inputs_body, steps, counts),
         f"inputs_{steps[0]}",
@@ -515,7 +549,7 @@
             pltpu.SemaphoreType.DMA((len(steps) * (count + 1),)),
         ],
         aliases={operands + k: k for k in range(len(before))},
-    )(token, received, gout, pos, w_in, w_cond, *dpre_0, *dpre_1, *before)
+    )(token, received, gout, pos, w_in_0, w_in_1, w_cond, *dpre_0, *dpre_1, *before)
 
 
 SHARES = ((0, 3), (1, 2))
@@ -721,25 +755,28 @@
 
     def input_gradients(steps, token, before):
         last = (steps[-1] + 1) * ROWS == rows
-        return inputs(steps, token, received if last else head_0[0], grad_out, pos, dpre_0, dpre_1, w_in, w_cond, before)
+        return inputs(steps, token, received if last else head_0[0], grad_out, pos, dpre_0, dpre_1, w_in_0, w_in_1, w_cond, before)
 
     halo = passed_along(signal[rows - DILATION_STEP :], 1)
-    val, pos, b_conv, b_res, b_skip, w_cond, w_res, w_skip, w_in, past, signal, x_turned, grad_out, grad_skip, *rest_0 = load(
-        val, pos, b_conv, b_res, b_skip, features, w_cond, w_res, w_skip, w_past, w_now, signal, grad_out, grad_skip
+    loads = (w_past, w_now, w_res, w_skip, b_res, b_skip)
+    val, pos, b_conv, w_cond, w_in_0, *outer_0, past, signal, x_turned, grad_out, grad_skip, a, b, c = load(
+        val, pos, b_conv, features, w_cond, w_res, w_skip, w_past, w_now, signal, grad_out, grad_skip
     )
-    common = (signal, x_turned, grad_out, grad_skip, w_in, w_cond, b_conv, w_res, w_skip)
-    past_head, head_0 = head(halo, pos, val, *common)
+    rest_0 = (a, b, c)
+    common = (signal, x_turned, grad_out, grad_skip)
+    past_head, head_0 = head(halo, pos, val, *common, w_in_0, w_cond, b_conv, *outer_0)
     made_0 = (head_0, rest_0)
     fixed = (far, block, val, x_turned, grad_out, grad_skip, past_head)
-    theirs_0 = gradients(0, False, past_head, *fixed, made_0)
-    mine_0 = gradients(0, True, theirs_0, *fixed, made_0)
-    most_1 = forward_most(mine_0, val, past, *common)
+    theirs_0, w_in_1, *outer_1, b_res, b_skip = gradients(0, False, past_head, *fixed, made_0, loads)
+    weights_1 = (w_in_1, w_cond, b_conv, *outer_1)
+    (mine_0,) = gradients(0, True, theirs_0, *fixed, made_0)
+    most_1 = forward_most(mine_0, val, past, *common, *weights_1)
     kept_0, got_0 = core_sum(0, most_1[0], theirs_0, mine_0)
-    head_1, last_1 = forward_ends(kept_0, halo, pos, val, past, *common)
+    head_1, last_1 = forward_ends(kept_0, halo, pos, val, past, *common, *weights_1)
     made_1 = (head_1, most_1, last_1)
     dpre_0, dpre_1 = ([p[2] for p in made] for made in (made_0, made_1))
-    theirs_1 = gradients(1, False, kept_0, *fixed, made_1)
-    mine_1 = gradients(1, True, theirs_1, *fixed, made_1)
+    (theirs_1,) = gradients(1, False, kept_0, *fixed, made_1)
+    (mine_1,) = gradients(1, True, theirs_1, *fixed, made_1)
     kept_0, got_0 = near_sum(0, mine_1, kept_0, got_0)
     kept_1, got_1 = core_sum(1, kept_0, theirs_1, mine_1)
     ends_0, got_0 = far_sum(0, kept_1, kept_0, got_0)
@@ -749,10 +786,10 @@
     ends_0, got_0 = far_join(0, kept_1, ends_0, got_0)
     ends_1, got_1 = far_sum(1, ends_0, kept_1, got_1)
     output, skip_out, mark = outputs(
-        ends_1, val, signal, [p[0] for p in made_0], [p[0] for p in made_1], w_res, w_skip, b_res, b_skip
+        ends_1, val, signal, [p[0] for p in made_0], [p[0] for p in made_1], outer_0, outer_1, b_res, b_skip
     )
     ends_1, got_1 = far_end(1, mark, ends_1, got_1)
-    early = early_rows(ends_1, pos, head_0[2], head_1[2], w_in)
+    early = early_rows(ends_1, pos, head_0[2], head_1[2], w_in_0, w_in_1)
     received = passed_along(early, -1)
     first = near_join(0, 0, early, ends_0, got_0)
     second = near_join(0, 1, first[0], ends_0, got_0)

time: 85.8 us -> 85.2 us (level)
  transfers between devices with their start and end apart: 26 -> 26, of which waited for: 6 -> 7; matrix products, arithmetic and copies ran while one was open for 0% -> 0% of each run, Pallas kernels for 39% -> 39%
where the time goes in v1:
time: 85.2 us; the launch traced here: 84.8 us
  Pallas kernels  38.4 us (45%)
  starting transfers between devices  34.6 us (41%)
  waiting for transfers between devices  9.8 us (12%)
  between operations  1.01 us (1%)
  local copies, waits for them, and re-layouts  0.97 us (1%)
    ppermute x24, starting transfers between devices, swapped(): lax.ppermute(x, axis, [(i, i ^ k) for i in range(lax.axis_size(axis))])  28.6 us
    ppermute x24, waiting for transfers between devices, swapped(): lax.ppermute(x, axis, [(i, i ^ k) for i in range(lax.axis_size(axis))])  9.8 us
    pallas_call x4, Pallas kernels, gradients(): call(functools.partial(gradients_body, far, block, half, own, count, len(...  8.43 us
    pallas_call x1, Pallas kernels, load(): call(load_body, 'load', [ANYWHERE] * len(sources), [VMEM] * len(shapes),...  7.83 us
    pallas_call x2, Pallas kernels, inputs(): call(functools.partial(inputs_body, steps, counts), f'inputs_{steps[0]}',...  7.67 us
    ppermute x2, starting transfers between devices, passed_along(): return lax.ppermute(x, AXES, pairs)  6.03 us
    pallas_call x2, Pallas kernels, unpack(): call(functools.partial(unpack_body, far, block), f'unpack_{half}', [ANYWH...  4 us
    pallas_call x1, Pallas kernels, outputs(): call(functools.partial(outputs_body, counts), 'outputs', [ANYWHERE] + [VM...  3.61 us
  transfers between devices with their start and end apart: 26, of which 7 were waited for; matrix products, arithmetic and copies ran while one was open for 0% of the time, Pallas kernels for 39%

profile of v1, /device:TPU:3, one launch (start us, length us, event | category | flops | bytes accessed | tf_op | source)
XLA Modules:
  0.0 84.8 jit_solution(15674580278493922390)
XLA Ops:
  0.6 1.0 %slice.3 = bf16[256,512]{1,0:T(8,128)(2,1)S(1)} slice(bf16[2048,512]{1,0:T(8,128)(2,1)} %sig.1), slice={[1792:2048], [0:512]} | slice | bytes 524288 | tf_op jit(solution)/shard_map/slice | solution.py:760
  1.6 3.1 %collective-permute-start = (bf16[256,512]{1,0:T(8,128)(2,1)S(1)}, bf16[256,512]{1,0:T(8,128)(2,1)S(1)}, u32[]{:S(2)}, u32[]{:S(2)}) collective-permute-start(bf16[256,512]{1,0:T(8,128)(2,1)S(1)} %slice.3), channel_id=1, source_target_pairs={{0,1},{1,2},{2,3},{3,4},{4,5},{5,6},{6,7},{7,8},{8,9},{9,10},{10,1... | collective-permute-start | bytes 786440 | tf_op jit(solution)/shard_map/ppermute | solution.py:687
  4.7 7.8 %load.1 = (s32[16,128]{1,0:T(8,128)S(1)}, s32[16,128]{1,0:T(8,128)S(1)}, f32[1,1024]{1,0:T(1,128)S(1)}, bf16[80,1024]{1,0:T(8,128)(2,1)S(1)}, bf16[1024,512]{1,0...) custom-call(s32[16,128]{1,0:T(8,128)} %bitcast.50, ...), custom_call_target="tpu_custom_call" | custom-call | flops 8000000000 | bytes 1 | tf_op jit(solution)/shard_map/load/pallas_call | solution.py:257
  13.4 2.1 %theirs_0.1 = (bf16[4,4,208,128]{3,2,1,0:T(8,128)(2,1)S(1)}, bf16[1024,512]{1,0:T(8,128)(2,1)S(1)}, bf16[256,512]{1,0:T(8,128)(2,1)S(1)}, bf16[256,512]{1,0:T(8,...) custom-call(bf16[512,256]{1,0:T(8,128)(2,1)S(1)} %get-tuple-element.93.token.past_head, ...), custom_call_target="tpu_custom_call" | custom-call | flops 1 | bytes 1 | tf_op jit(solution)/shard_map/theirs_0/pallas_call | solution.py:446
  15.5 1.0 %collective-permute-start.1 = (bf16[4,4,208,128]{3,2,1,0:T(8,128)(2,1)S(1)}, bf16[4,4,208,128]{3,2,1,0:T(8,128)(2,1)S(1)}, u32[]{:S(2)}, u32[]{:S(2)}) collective-permute-start(bf16[4,4,208,128]{3,2,1,0:T(8,128)(2,1)S(1)} %get-tuple-element.98.token), channel_id=1, source_target_pairs={{0,16},{16,0},{1,17},{17,1},{2,18},{18,2},{3,19},{19,3},{4,20},{20... | collective-permute-start | bytes 2555912 | tf_op jit(solution)/shard_map/ppermute | solution.py:611
  16.5 2.2 %mine_0.1.token.refs_0_ = f32[4,4,208,128]{3,2,1,0:T(8,128)S(1)} custom-call(bf16[4,4,208,128]{3,2,1,0:T(8,128)(2,1)S(1)} %get-tuple-element.98.token, s32[16,128]{1,0:T(8,128)S(1)} %get-tuple-element.83.valid, bf16[1120,2048]{1,0:T(8,128)(2,1)S(1)} %get-tuple-element.85.x_turned, bf16[2048,512]{1,0:T(8,128)(2,1)S(1)} %get-tuple-element.86.gout, ...), custom_call_target="tpu_custom_call" | custom-call | flops 1 | bytes 1 | tf_op jit(solution)/shard_map/mine_0/pallas_call | solution.py:446
  18.7 1.4 %forward_1.1 = (bf16[512,256]{1,0:T(8,128)(2,1)S(1)}, bf16[256,512]{1,0:T(8,128)(2,1)S(1)}, bf16[512,512]{1,0:T(8,128)(2,1)S(1)}) custom-call(f32[4,4,208,128]{3,2,1,0:T(8,128)S(1)} %mine_0.1.token.refs_0_, s32[16,128]{1,0:T(8,128)S(1)} %get-tuple-element.83.valid, bf16[2048,512]{1,0:T(8,128)(2,1)S(1)} %get-tuple-element.99.past, ...), custom_call_target="tpu_custom_call" | custom-call | flops 1 | bytes 1 | tf_op jit(solution)/shard_map/forward_1/pallas_call | solution.py:328
  20.5 1.2 %collective-permute-start.3 = (bf16[4,208,128]{2,1,0:T(8,128)(2,1)S(1)}, bf16[4,208,128]{2,1,0:T(8,128)(2,1)S(1)}, u32[]{:S(2)}, u32[]{:S(2)}) collective-permute-start(bf16[4,208,128]{2,1,0:T(8,128)(2,1)S(1)} %bitcast.43), channel_id=1, source_target_pairs={{0,2},{1,3},{2,0},{3,1},{4,6},{5,7},{6,4},{7,5},{8,10},{9,11},{10,... | collective-permute-start | bytes 638984 | tf_op jit(solution)/shard_map/ppermute | solution.py:611
  21.8 1.2 %collective-permute-start.4 = (bf16[4,208,128]{2,1,0:T(8,128)(2,1)S(1)}, bf16[4,208,128]{2,1,0:T(8,128)(2,1)S(1)}, u32[]{:S(2)}, u32[]{:S(2)}) collective-permute-start(bf16[4,208,128]{2,1,0:T(8,128)(2,1)S(1)} %bitcast.41), channel_id=1, source_target_pairs={{0,3},{1,2},{2,1},{3,0},{4,7},{5,6},{6,5},{7,4},{8,11},{9,10},{10,... | collective-permute-start | bytes 638984 | tf_op jit(solution)/shard_map/ppermute | solution.py:611
  22.9 3.5 %ends_1.1 = (bf16[256,256]{1,0:T(8,128)(2,1)S(1)}, bf16[256,256]{1,0:T(8,128)(2,1)S(1)}, bf16[256,512]{1,0:T(8,128)(2,1)S(1)}, bf16[1280,256]{1,0:T(8,128)(2,1)S...) custom-call(f32[4,208,128]{2,1,0:T(8,128)S(1)} %bitcast.27, ...), custom_call_target="tpu_custom_call" | custom-call | flops 1 | bytes 1 | tf_op jit(solution)/shard_map/ends_1/pallas_call | solution.py:350
  26.4 2.0 %theirs_1.1.token = bf16[4,4,208,128]{3,2,1,0:T(8,128)(2,1)S(1)} custom-call(f32[4,208,128]{2,1,0:T(8,128)S(1)} %bitcast.28, s32[16,128]{1,0:T(8,128)S(1)} %get-tuple-element.83.valid, bf16[1120,2048]{1,0:T(8,128)(2,1)S(1)} %get-tuple-element.85.x_turned, bf16[2048,512]{1,0:T(8,128)(2,1)S(1)} %get-tuple-element.86.gout, ...), custom_call_target="tpu_custom_call" | custom-call | flops 1 | bytes 1 | tf_op jit(solution)/shard_map/theirs_1/pallas_call | solution.py:446
  29.3 2.2 %mine_1.1.token.refs_0_ = f32[4,4,208,128]{3,2,1,0:T(8,128)S(1)} custom-call(bf16[4,4,208,128]{3,2,1,0:T(8,128)(2,1)S(1)} %theirs_1.1.token, s32[16,128]{1,0:T(8,128)S(1)} %get-tuple-element.83.valid, bf16[1120,2048]{1,0:T(8,128)(2,1)S(1)} %get-tuple-element.85.x_turned, bf16[2048,512]{1,0:T(8,128)(2,1)S(1)} %get-tuple-element.86.gout, ...), custom_call_target="tpu_custom_call" | custom-call | flops 2000000000 | bytes 1 | tf_op jit(solution)/shard_map/mine_1/pallas_call | solution.py:446
  31.5 1.2 %collective-permute-done.4.refs_3_ = bf16[4,208,128]{2,1,0:T(8,128)(2,1)S(1)} collective-permute-done((bf16[4,208,128]{2,1,0:T(8,128)(2,1)S(1)}, bf16[4,208,128]{2,1,0:T(8,128)(2,1)S(1)}, u32[]{:S(2)}, u32[]{:S(2)}) %collective-permute-start.4) | collective-permute-done | bytes 213024 | tf_op jit(solution)/shard_map/ppermute | solution.py:611
  32.8 1.4 %collective-permute-start.6 = (bf16[2,208,128]{2,1,0:T(8,128)(2,1)S(1)}, bf16[2,208,128]{2,1,0:T(8,128)(2,1)S(1)}, u32[]{:S(2)}, u32[]{:S(2)}) collective-permute-start(bf16[2,208,128]{2,1,0:T(8,128)(2,1)S(1)} %get-tuple-element.116), channel_id=1, source_target_pairs={{0,4},{4,0},{8,12},{12,8},{1,5},{5,1},{9,13},{13,9},{2,6},{6,2},{1... | collective-permute-start | bytes 319496 | tf_op jit(solution)/shard_map/ppermute | solution.py:611
  34.7 1.1 %collective-permute-start.9 = (bf16[4,208,128]{2,1,0:T(8,128)(2,1)S(1)}, bf16[4,208,128]{2,1,0:T(8,128)(2,1)S(1)}, u32[]{:S(2)}, u32[]{:S(2)}) collective-permute-start(bf16[4,208,128]{2,1,0:T(8,128)(2,1)S(1)} %bitcast.40), channel_id=1, source_target_pairs={{0,2},{1,3},{2,0},{3,1},{4,6},{5,7},{6,4},{7,5},{8,10},{9,11},{10,... | collective-permute-start | bytes 638984 | tf_op jit(solution)/shard_map/ppermute | solution.py:611
  35.9 1.2 %collective-permute-start.10 = (bf16[4,208,128]{2,1,0:T(8,128)(2,1)S(1)}, bf16[4,208,128]{2,1,0:T(8,128)(2,1)S(1)}, u32[]{:S(2)}, u32[]{:S(2)}) collective-permute-start(bf16[4,208,128]{2,1,0:T(8,128)(2,1)S(1)} %bitcast.38), channel_id=1, source_target_pairs={{0,3},{1,2},{2,1},{3,0},{4,7},{5,6},{6,5},{7,4},{8,11},{9,10},{10,... | collective-permute-start | bytes 638984 | tf_op jit(solution)/shard_map/ppermute | solution.py:611
  37.1 1.8 %collective-permute-start.7 = (bf16[2,208,128]{2,1,0:T(8,128)(2,1)S(1)}, bf16[2,208,128]{2,1,0:T(8,128)(2,1)S(1)}, u32[]{:S(2)}, u32[]{:S(2)}) collective-permute-start(bf16[2,208,128]{2,1,0:T(8,128)(2,1)S(1)} %far_sum_0.1.token.mine), channel_id=1, source_target_pairs={{0,8},{4,12},{8,0},{12,4},{1,9},{5,13},{9,1},{13,5},{2,10},{6,14},... | collective-permute-start | bytes 319496 | tf_op jit(solution)/shard_map/ppermute | solution.py:611
  38.9 3.9 %inputs_0.1 = (f32[2048,512]{1,0:T(8,128)}, f32[80,2048]{1,0:T(8,128)}, f32[8,128]{1,0:T(8,128)S(1)}) custom-call(bf16[2,208,128]{2,1,0:T(8,128)(2,1)S(1)} %far_sum_0.1.token.mine, bf16[256,256]{1,0:T(8,128)(2,1)S(1)} %get-tuple-element.117.received.refs_0_, bf16[2048,512]{1,0:T(8,128)(2,1)S(1)} %get-tuple-element.86.gout, ...), custom_call_target="tpu_custom_call" | custom-call | flops 1 | bytes 1 | tf_op jit(solution)/shard_map/inputs_0/pallas_call | solution.py:536
  44.8 1.8 %collective-permute-done.11.refs_1_ = bf16[2,208,128]{2,1,0:T(8,128)(2,1)S(1)} collective-permute-done((bf16[2,208,128]{2,1,0:T(8,128)(2,1)S(1)}, bf16[2,208,128]{2,1,0:T(8,128)(2,1)S(1)}, u32[]{:S(2)}, u32[]{:S(2)}) %collective-permute-start.11) | collective-permute-done | bytes 106528 | tf_op jit(solution)/shard_map/ppermute | solution.py:611
  46.6 1.2 %collective-permute-start.14 = (bf16[4,208,128]{2,1,0:T(8,128)(2,1)S(1)}, bf16[4,208,128]{2,1,0:T(8,128)(2,1)S(1)}, u32[]{:S(2)}, u32[]{:S(2)}) collective-permute-start(bf16[4,208,128]{2,1,0:T(8,128)(2,1)S(1)} %far_join_0.1.token), channel_id=1, source_target_pairs={{0,3},{1,2},{2,1},{3,0},{4,7},{5,6},{6,5},{7,4},{8,11},{9,10},{10,... | collective-permute-start | bytes 638984 | tf_op jit(solution)/shard_map/ppermute | solution.py:611
  47.8 1.1 %collective-permute-start.16 = (bf16[4,208,128]{2,1,0:T(8,128)(2,1)S(1)}, bf16[4,208,128]{2,1,0:T(8,128)(2,1)S(1)}, u32[]{:S(2)}, u32[]{:S(2)}) collective-permute-start(bf16[4,208,128]{2,1,0:T(8,128)(2,1)S(1)} %far_join_0.1.token), channel_id=1, source_target_pairs={{0,2},{1,3},{2,0},{3,1},{4,6},{5,7},{6,4},{7,5},{8,10},{9,11},{10,... | collective-permute-start | bytes 638984 | tf_op jit(solution)/shard_map/ppermute | solution.py:611
  49.3 2.2 %collective-permute-start.13 = (bf16[2,208,128]{2,1,0:T(8,128)(2,1)S(1)}, bf16[2,208,128]{2,1,0:T(8,128)(2,1)S(1)}, u32[]{:S(2)}, u32[]{:S(2)}) collective-permute-start(bf16[2,208,128]{2,1,0:T(8,128)(2,1)S(1)} %far_sum_1.1.token.mine), channel_id=1, source_target_pairs={{0,8},{4,12},{8,0},{12,4},{1,9},{5,13},{9,1},{13,5},{2,10},{6,14},... | collective-permute-start | bytes 319496 | tf_op jit(solution)/shard_map/ppermute | solution.py:611
  51.6 3.6 %outputs.1 = (bf16[2048,512]{1,0:T(8,128)(2,1)}, bf16[2048,512]{1,0:T(8,128)(2,1)}, f32[8,128]{1,0:T(8,128)S(1)}) custom-call(bf16[2,208,128]{2,1,0:T(8,128)(2,1)S(1)} %far_sum_1.1.token.mine, s32[16,128]{1,0:T(8,128)S(1)} %get-tuple-element.83.valid, bf16[2048,512]{1,0:T(8,128)(2,1)S(1)} %get-tuple-element.84.sig, ...), custom_call_target="tpu_custom_call" | custom-call | flops 1 | bytes 1 | tf_op jit(solution)/shard_map/outputs/pallas_call | solution.py:479
  56.1 2.9 %collective-permute-start.18 = (bf16[256,512]{1,0:T(8,128)(2,1)S(1)}, bf16[256,512]{1,0:T(8,128)(2,1)S(1)}, u32[]{:S(2)}, u32[]{:S(2)}) collective-permute-start(bf16[256,512]{1,0:T(8,128)(2,1)S(1)} %early.1.token), channel_id=1, source_target_pairs={{1,0},{2,1},{3,2},{4,3},{5,4},{6,5},{7,6},{8,7},{9,8},{10,9},{11,1... | collective-permute-start | bytes 786440 | tf_op jit(solution)/shard_map/ppermute | solution.py:687
  59.7 1.3 %collective-permute-start.19 = (bf16[4,208,128]{2,1,0:T(8,128)(2,1)S(1)}, bf16[4,208,128]{2,1,0:T(8,128)(2,1)S(1)}, u32[]{:S(2)}, u32[]{:S(2)}) collective-permute-start(bf16[4,208,128]{2,1,0:T(8,128)(2,1)S(1)} %far_join_1.1.token), channel_id=1, source_target_pairs={{0,3},{1,2},{2,1},{3,0},{4,7},{5,6},{6,5},{7,4},{8,11},{9,10},{10,... | collective-permute-start | bytes 638984 | tf_op jit(solution)/shard_map/ppermute | solution.py:611
  61.0 8.2 %collective-permute-start.24 = (bf16[4,208,128]{2,1,0:T(8,128)(2,1)S(1)}, bf16[4,208,128]{2,1,0:T(8,128)(2,1)S(1)}, u32[]{:S(2)}, u32[]{:S(2)}) collective-permute-start(bf16[4,208,128]{2,1,0:T(8,128)(2,1)S(1)} %far_join_1.1.token), channel_id=1, source_target_pairs={{0,2},{1,3},{2,0},{3,1},{4,6},{5,7},{6,4},{7,5},{8,10},{9,11},{10,... | collective-permute-start | bytes 638984 | tf_op jit(solution)/shard_map/ppermute | solution.py:611
  69.3 1.7 %collective-permute-start.21 = (bf16[2,4,208,128]{3,2,1,0:T(8,128)(2,1)S(1)}, bf16[2,4,208,128]{3,2,1,0:T(8,128)(2,1)S(1)}, u32[]{:S(2)}, u32[]{:S(2)}) collective-permute-start(bf16[2,4,208,128]{3,2,1,0:T(8,128)(2,1)S(1)} %near_join_0_0.1.token.refs_0_), channel_id=1, source_target_pairs={{0,16},{16,0},{1,17},{17,1},{2,18},{18,2},{3,19},{19,3},{4,20},{20... | collective-permute-start | bytes 1277960 | tf_op jit(solution)/shard_map/ppermute | solution.py:611
  71.0 3.8 %inputs_2.1 = (f32[2048,512]{1,0:T(8,128)}, f32[80,2048]{1,0:T(8,128)}, f32[8,128]{1,0:T(8,128)S(1)}) custom-call(bf16[4,208,128]{2,1,0:T(8,128)(2,1)S(1)} %far_join_1.1.token, bf16[256,512]{1,0:T(8,128)(2,1)S(1)} %collective-permute-done.18.received, bf16[2048,512]{1,0:T(8,128)(2,1)S(1)} %get-tuple-element.86.gout, ...), custom_call_target="tpu_custom_call", output_to_operand_aliasing={{0}: (12, {}), {1}: (13, {})} | custom-call | flops 1 | bytes 1 | tf_op jit(solution)/shard_map/inputs_2/pallas_call | solution.py:536
  74.9 4.3 %collective-permute-done.24 = bf16[4,208,128]{2,1,0:T(8,128)(2,1)S(1)} collective-permute-done((bf16[4,208,128]{2,1,0:T(8,128)(2,1)S(1)}, bf16[4,208,128]{2,1,0:T(8,128)(2,1)S(1)}, u32[]{:S(2)}, u32[]{:S(2)}) %collective-permute-start.24) | collective-permute-done | bytes 213024 | tf_op jit(solution)/shard_map/ppermute | solution.py:611
  79.2 1.0 %collective-permute-done.23 = bf16[4,208,128]{2,1,0:T(8,128)(2,1)S(1)} collective-permute-done((bf16[4,208,128]{2,1,0:T(8,128)(2,1)S(1)}, bf16[4,208,128]{2,1,0:T(8,128)(2,1)S(1)}, u32[]{:S(2)}, u32[]{:S(2)}) %collective-permute-start.23) | collective-permute-done | bytes 213024 | tf_op jit(solution)/shard_map/ppermute | solution.py:611
  80.7 2.0 %unpack_0.1 = (f32[512,1024]{1,0:T(8,128)}, f32[512,1024]{1,0:T(8,128)}, f32[80,1024]{1,0:T(8,128)}, f32[1,1024]{1,0:T(1,128)}, f32[512,512]{1,0:T(8,128)}, /*in...) custom-call(bf16[2,4,208,128]{3,2,1,0:T(8,128)(2,1)S(1)} %collective-permute-done.20.token.refs_2_, ...), custom_call_target="tpu_custom_call" | custom-call | flops 1 | bytes 1 | tf_op jit(solution)/shard_map/unpack_0/pallas_call | solution.py:598
  82.7 2.0 %unpack_1.1 = (f32[512,1024]{1,0:T(8,128)}, f32[512,1024]{1,0:T(8,128)}, f32[80,1024]{1,0:T(8,128)}, f32[1,1024]{1,0:T(1,128)}, f32[512,512]{1,0:T(8,128)}, /*in...) custom-call(f32[8,128]{1,0:T(8,128)S(1)} %get-tuple-element.137.toke, ...), custom_call_target="tpu_custom_call", output_to_operand_aliasing={{0}: (5, {}), {1}: (6, {}), {2}: (7, {}), {3}: (8, {}), {4}... | custom-call | flops 1 | bytes 1 | tf_op jit(solution)/shard_map/unpack_1/pallas_call | solution.py:598
  (49 shorter events, 7.6 us)
Async XLA Ops:
  1.6 11.0 %collective-permute-start = (bf16[256,512]{1,0:T(8,128)(2,1)S(1)}, bf16[256,512]{1,0:T(8,128)(2,1)S(1)}, u32[]{:S(2)}, u32[]{:S(2)}) collective-permute-start(bf16[256,512]{1,0:T(8,128)(2,1)S(1)} %slice.3), channel_id=1, source_target_pairs={{0,1},{1,2},{2,3},{3,4},{4,5},{5,6},{6,7},{7,8},{8,9},{9,10},{10,1... | collective-permute-start | bytes 786440 | tf_op jit(solution)/shard_map/ppermute | solution.py:687
  15.5 4.6 %collective-permute-start.1 = (bf16[4,4,208,128]{3,2,1,0:T(8,128)(2,1)S(1)}, bf16[4,4,208,128]{3,2,1,0:T(8,128)(2,1)S(1)}, u32[]{:S(2)}, u32[]{:S(2)}) collective-permute-start(bf16[4,4,208,128]{3,2,1,0:T(8,128)(2,1)S(1)} %get-tuple-element.98.token), channel_id=1, source_target_pairs={{0,16},{16,0},{1,17},{17,1},{2,18},{18,2},{3,19},{19,3},{4,20},{20... | collective-permute-start | bytes 2555912 | tf_op jit(solution)/shard_map/ppermute | solution.py:611
  20.2 11.3 %collective-permute-start.2 = (bf16[4,208,128]{2,1,0:T(8,128)(2,1)S(1)}, bf16[4,208,128]{2,1,0:T(8,128)(2,1)S(1)}, u32[]{:S(2)}, u32[]{:S(2)}) collective-permute-start(bf16[4,208,128]{2,1,0:T(8,128)(2,1)S(1)} %bitcast.44), channel_id=1, source_target_pairs={{0,1},{1,0},{2,3},{3,2},{4,5},{5,4},{6,7},{7,6},{8,9},{9,8},{10,11... | collective-permute-start | bytes 638984 | tf_op jit(solution)/shard_map/ppermute | solution.py:611
  20.5 11.0 %collective-permute-start.3 = (bf16[4,208,128]{2,1,0:T(8,128)(2,1)S(1)}, bf16[4,208,128]{2,1,0:T(8,128)(2,1)S(1)}, u32[]{:S(2)}, u32[]{:S(2)}) collective-permute-start(bf16[4,208,128]{2,1,0:T(8,128)(2,1)S(1)} %bitcast.43), channel_id=1, source_target_pairs={{0,2},{1,3},{2,0},{3,1},{4,6},{5,7},{6,4},{7,5},{8,10},{9,11},{10,... | collective-permute-start | bytes 638984 | tf_op jit(solution)/shard_map/ppermute | solution.py:611
  21.8 10.9 %collective-permute-start.4 = (bf16[4,208,128]{2,1,0:T(8,128)(2,1)S(1)}, bf16[4,208,128]{2,1,0:T(8,128)(2,1)S(1)}, u32[]{:S(2)}, u32[]{:S(2)}) collective-permute-start(bf16[4,208,128]{2,1,0:T(8,128)(2,1)S(1)} %bitcast.41), channel_id=1, source_target_pairs={{0,3},{1,2},{2,1},{3,0},{4,7},{5,6},{6,5},{7,4},{8,11},{9,10},{10,... | collective-permute-start | bytes 638984 | tf_op jit(solution)/shard_map/ppermute | solution.py:611
  28.4 5.8 %collective-permute-start.5 = (bf16[4,4,208,128]{3,2,1,0:T(8,128)(2,1)S(1)}, bf16[4,4,208,128]{3,2,1,0:T(8,128)(2,1)S(1)}, u32[]{:S(2)}, u32[]{:S(2)}) collective-permute-start(bf16[4,4,208,128]{3,2,1,0:T(8,128)(2,1)S(1)} %theirs_1.1.token), channel_id=1, source_target_pairs={{0,16},{16,0},{1,17},{17,1},{2,18},{18,2},{3,19},{19,3},{4,20},{20... | collective-permute-start | bytes 2555912 | tf_op jit(solution)/shard_map/ppermute | solution.py:611
  32.8 4.3 %collective-permute-start.6 = (bf16[2,208,128]{2,1,0:T(8,128)(2,1)S(1)}, bf16[2,208,128]{2,1,0:T(8,128)(2,1)S(1)}, u32[]{:S(2)}, u32[]{:S(2)}) collective-permute-start(bf16[2,208,128]{2,1,0:T(8,128)(2,1)S(1)} %get-tuple-element.116), channel_id=1, source_target_pairs={{0,4},{4,0},{8,12},{12,8},{1,5},{5,1},{9,13},{13,9},{2,6},{6,2},{1... | collective-permute-start | bytes 319496 | tf_op jit(solution)/shard_map/ppermute | solution.py:611
  34.4 9.3 %collective-permute-start.8 = (bf16[4,208,128]{2,1,0:T(8,128)(2,1)S(1)}, bf16[4,208,128]{2,1,0:T(8,128)(2,1)S(1)}, u32[]{:S(2)}, u32[]{:S(2)}) collective-permute-start(bf16[4,208,128]{2,1,0:T(8,128)(2,1)S(1)} %bitcast.42), channel_id=1, source_target_pairs={{0,1},{1,0},{2,3},{3,2},{4,5},{5,4},{6,7},{7,6},{8,9},{9,8},{10,11... | collective-permute-start | bytes 638984 | tf_op jit(solution)/shard_map/ppermute | solution.py:611
  34.7 8.9 %collective-permute-start.9 = (bf16[4,208,128]{2,1,0:T(8,128)(2,1)S(1)}, bf16[4,208,128]{2,1,0:T(8,128)(2,1)S(1)}, u32[]{:S(2)}, u32[]{:S(2)}) collective-permute-start(bf16[4,208,128]{2,1,0:T(8,128)(2,1)S(1)} %bitcast.40), channel_id=1, source_target_pairs={{0,2},{1,3},{2,0},{3,1},{4,6},{5,7},{6,4},{7,5},{8,10},{9,11},{10,... | collective-permute-start | bytes 638984 | tf_op jit(solution)/shard_map/ppermute | solution.py:611
  35.9 8.6 %collective-permute-start.10 = (bf16[4,208,128]{2,1,0:T(8,128)(2,1)S(1)}, bf16[4,208,128]{2,1,0:T(8,128)(2,1)S(1)}, u32[]{:S(2)}, u32[]{:S(2)}) collective-permute-start(bf16[4,208,128]{2,1,0:T(8,128)(2,1)S(1)} %bitcast.38), channel_id=1, source_target_pairs={{0,3},{1,2},{2,1},{3,0},{4,7},{5,6},{6,5},{7,4},{8,11},{9,10},{10,... | collective-permute-start | bytes 638984 | tf_op jit(solution)/shard_map/ppermute | solution.py:611
  37.1 5.7 %collective-permute-start.7 = (bf16[2,208,128]{2,1,0:T(8,128)(2,1)S(1)}, bf16[2,208,128]{2,1,0:T(8,128)(2,1)S(1)}, u32[]{:S(2)}, u32[]{:S(2)}) collective-permute-start(bf16[2,208,128]{2,1,0:T(8,128)(2,1)S(1)} %far_sum_0.1.token.mine), channel_id=1, source_target_pairs={{0,8},{4,12},{8,0},{12,4},{1,9},{5,13},{9,1},{13,5},{2,10},{6,14},... | collective-permute-start | bytes 319496 | tf_op jit(solution)/shard_map/ppermute | solution.py:611
  42.9 3.7 %collective-permute-start.11 = (bf16[2,208,128]{2,1,0:T(8,128)(2,1)S(1)}, bf16[2,208,128]{2,1,0:T(8,128)(2,1)S(1)}, u32[]{:S(2)}, u32[]{:S(2)}) collective-permute-start(bf16[2,208,128]{2,1,0:T(8,128)(2,1)S(1)} %far_end_0.1.token.refs_0_), channel_id=1, source_target_pairs={{0,4},{4,0},{8,12},{12,8},{1,5},{5,1},{9,13},{13,9},{2,6},{6,2},{1... | collective-permute-start | bytes 319496 | tf_op jit(solution)/shard_map/ppermute | solution.py:611
  44.5 4.8 %collective-permute-start.12 = (bf16[2,208,128]{2,1,0:T(8,128)(2,1)S(1)}, bf16[2,208,128]{2,1,0:T(8,128)(2,1)S(1)}, u32[]{:S(2)}, u32[]{:S(2)}) collective-permute-start(bf16[2,208,128]{2,1,0:T(8,128)(2,1)S(1)} %get-tuple-element.123), channel_id=1, source_target_pairs={{0,4},{4,0},{8,12},{12,8},{1,5},{5,1},{9,13},{13,9},{2,6},{6,2},{1... | collective-permute-start | bytes 319496 | tf_op jit(solution)/shard_map/ppermute | solution.py:611
  46.6 12.4 %collective-permute-start.14 = (bf16[4,208,128]{2,1,0:T(8,128)(2,1)S(1)}, bf16[4,208,128]{2,1,0:T(8,128)(2,1)S(1)}, u32[]{:S(2)}, u32[]{:S(2)}) collective-permute-start(bf16[4,208,128]{2,1,0:T(8,128)(2,1)S(1)} %far_join_0.1.token), channel_id=1, source_target_pairs={{0,3},{1,2},{2,1},{3,0},{4,7},{5,6},{6,5},{7,4},{8,11},{9,10},{10,... | collective-permute-start | bytes 638984 | tf_op jit(solution)/shard_map/ppermute | solution.py:611
  47.8 11.2 %collective-permute-start.16 = (bf16[4,208,128]{2,1,0:T(8,128)(2,1)S(1)}, bf16[4,208,128]{2,1,0:T(8,128)(2,1)S(1)}, u32[]{:S(2)}, u32[]{:S(2)}) collective-permute-start(bf16[4,208,128]{2,1,0:T(8,128)(2,1)S(1)} %far_join_0.1.token), channel_id=1, source_target_pairs={{0,2},{1,3},{2,0},{3,1},{4,6},{5,7},{6,4},{7,5},{8,10},{9,11},{10,... | collective-permute-start | bytes 638984 | tf_op jit(solution)/shard_map/ppermute | solution.py:611
  48.9 10.2 %collective-permute-start.15 = (bf16[4,208,128]{2,1,0:T(8,128)(2,1)S(1)}, bf16[4,208,128]{2,1,0:T(8,128)(2,1)S(1)}, u32[]{:S(2)}, u32[]{:S(2)}) collective-permute-start(bf16[4,208,128]{2,1,0:T(8,128)(2,1)S(1)} %far_join_0.1.token), channel_id=1, source_target_pairs={{0,1},{1,0},{2,3},{3,2},{4,5},{5,4},{6,7},{7,6},{8,9},{9,8},{10,11... | collective-permute-start | bytes 638984 | tf_op jit(solution)/shard_map/ppermute | solution.py:611
  49.3 6.0 %collective-permute-start.13 = (bf16[2,208,128]{2,1,0:T(8,128)(2,1)S(1)}, bf16[2,208,128]{2,1,0:T(8,128)(2,1)S(1)}, u32[]{:S(2)}, u32[]{:S(2)}) collective-permute-start(bf16[2,208,128]{2,1,0:T(8,128)(2,1)S(1)} %far_sum_1.1.token.mine), channel_id=1, source_target_pairs={{0,8},{4,12},{8,0},{12,4},{1,9},{5,13},{9,1},{13,5},{2,10},{6,14},... | collective-permute-start | bytes 319496 | tf_op jit(solution)/shard_map/ppermute | solution.py:611
  55.3 4.4 %collective-permute-start.17 = (bf16[2,208,128]{2,1,0:T(8,128)(2,1)S(1)}, bf16[2,208,128]{2,1,0:T(8,128)(2,1)S(1)}, u32[]{:S(2)}, u32[]{:S(2)}) collective-permute-start(bf16[2,208,128]{2,1,0:T(8,128)(2,1)S(1)} %far_end_1.1.token.refs_0_), channel_id=1, source_target_pairs={{0,4},{4,0},{8,12},{12,8},{1,5},{5,1},{9,13},{13,9},{2,6},{6,2},{1... | collective-permute-start | bytes 319496 | tf_op jit(solution)/shard_map/ppermute | solution.py:611
  56.1 13.2 %collective-permute-start.18 = (bf16[256,512]{1,0:T(8,128)(2,1)S(1)}, bf16[256,512]{1,0:T(8,128)(2,1)S(1)}, u32[]{:S(2)}, u32[]{:S(2)}) collective-permute-start(bf16[256,512]{1,0:T(8,128)(2,1)S(1)} %early.1.token), channel_id=1, source_target_pairs={{1,0},{2,1},{3,2},{4,3},{5,4},{6,5},{7,6},{8,7},{9,8},{10,9},{11,1... | collective-permute-start | bytes 786440 | tf_op jit(solution)/shard_map/ppermute | solution.py:687
  59.7 15.1 %collective-permute-start.19 = (bf16[4,208,128]{2,1,0:T(8,128)(2,1)S(1)}, bf16[4,208,128]{2,1,0:T(8,128)(2,1)S(1)}, u32[]{:S(2)}, u32[]{:S(2)}) collective-permute-start(bf16[4,208,128]{2,1,0:T(8,128)(2,1)S(1)} %far_join_1.1.token), channel_id=1, source_target_pairs={{0,3},{1,2},{2,1},{3,0},{4,7},{5,6},{6,5},{7,4},{8,11},{9,10},{10,... | collective-permute-start | bytes 638984 | tf_op jit(solution)/shard_map/ppermute | solution.py:611
  61.0 18.2 %collective-permute-start.24 = (bf16[4,208,128]{2,1,0:T(8,128)(2,1)S(1)}, bf16[4,208,128]{2,1,0:T(8,128)(2,1)S(1)}, u32[]{:S(2)}, u32[]{:S(2)}) collective-permute-start(bf16[4,208,128]{2,1,0:T(8,128)(2,1)S(1)} %far_join_1.1.token), channel_id=1, source_target_pairs={{0,2},{1,3},{2,0},{3,1},{4,6},{5,7},{6,4},{7,5},{8,10},{9,11},{10,... | collective-permute-start | bytes 638984 | tf_op jit(solution)/shard_map/ppermute | solution.py:611
  69.1 11.1 %collective-permute-start.23 = (bf16[4,208,128]{2,1,0:T(8,128)(2,1)S(1)}, bf16[4,208,128]{2,1,0:T(8,128)(2,1)S(1)}, u32[]{:S(2)}, u32[]{:S(2)}) collective-permute-start(bf16[4,208,128]{2,1,0:T(8,128)(2,1)S(1)} %far_join_1.1.token), channel_id=1, source_target_pairs={{0,1},{1,0},{2,3},{3,2},{4,5},{5,4},{6,7},{7,6},{8,9},{9,8},{10,11... | collective-permute-start | bytes 638984 | tf_op jit(solution)/shard_map/ppermute | solution.py:611
  69.1 11.6 %collective-permute-start.22 = (bf16[2,4,208,128]{3,2,1,0:T(8,128)(2,1)S(1)}, bf16[2,4,208,128]{3,2,1,0:T(8,128)(2,1)S(1)}, u32[]{:S(2)}, u32[]{:S(2)}) collective-permute-start(bf16[2,4,208,128]{3,2,1,0:T(8,128)(2,1)S(1)} %near_join_0_1.1.token.refs_1_), channel_id=1, source_target_pairs={{0,16},{16,0},{1,17},{17,1},{2,18},{18,2},{3,19},{19,3},{4,20},{20... | collective-permute-start | bytes 1277960 | tf_op jit(solution)/shard_map/ppermute | solution.py:611
  69.3 11.4 %collective-permute-start.21 = (bf16[2,4,208,128]{3,2,1,0:T(8,128)(2,1)S(1)}, bf16[2,4,208,128]{3,2,1,0:T(8,128)(2,1)S(1)}, u32[]{:S(2)}, u32[]{:S(2)}) collective-permute-start(bf16[2,4,208,128]{3,2,1,0:T(8,128)(2,1)S(1)} %near_join_0_0.1.token.refs_0_), channel_id=1, source_target_pairs={{0,16},{16,0},{1,17},{17,1},{2,18},{18,2},{3,19},{19,3},{4,20},{20... | collective-permute-start | bytes 1277960 | tf_op jit(solution)/shard_map/ppermute | solution.py:611
  74.8 5.9 %collective-permute-start.20 = (bf16[2,4,208,128]{3,2,1,0:T(8,128)(2,1)S(1)}, bf16[2,4,208,128]{3,2,1,0:T(8,128)(2,1)S(1)}, u32[]{:S(2)}, u32[]{:S(2)}) collective-permute-start(bf16[2,4,208,128]{3,2,1,0:T(8,128)(2,1)S(1)} %near_join_1_0.1.token.refs_0_), channel_id=1, source_target_pairs={{0,16},{16,0},{1,17},{17,1},{2,18},{18,2},{3,19},{19,3},{4,20},{20... | collective-permute-start | bytes 1277960 | tf_op jit(solution)/shard_map/ppermute | solution.py:611
  80.2 2.5 %collective-permute-start.25 = (bf16[2,4,208,128]{3,2,1,0:T(8,128)(2,1)S(1)}, bf16[2,4,208,128]{3,2,1,0:T(8,128)(2,1)S(1)}, u32[]{:S(2)}, u32[]{:S(2)}) collective-permute-start(bf16[2,4,208,128]{3,2,1,0:T(8,128)(2,1)S(1)} %near_join_1_1.1.refs_1_), channel_id=1, source_target_pairs={{0,16},{16,0},{1,17},{17,1},{2,18},{18,2},{3,19},{19,3},{4,20},{20... | collective-permute-start | bytes 1277960 | tf_op jit(solution)/shard_map/ppermute | solution.py:611

commit v2 on v1

--- a/solution.py
+++ b/solution.py
@@ -19,7 +19,7 @@
 BF16 = jnp.bfloat16
 MEGA = 1 << 20
 COSTS = {
-    "load": 8, "head": 2, "near_sum_0": 7, "mine_1": 2,
+    "load": 8, "head": 2, "near_sum_0": 7, "mine_1": 2, "near_part_0": 1,
     "far_sum_0": 8, "near_sum_1": 4, "near_join_0_1": 2, "near_join_1_1": 4, "far_join_0": 4,
 }
 FLOPS = 10**9
@@ -165,10 +165,6 @@
 
 def tiles_of(start, stop):
     return [slice(a, a + DILATION_STEP) for a in range(start, stop, DILATION_STEP)]
-
-
-def split_rows(rows):
-    return 3 * DILATION_STEP
 
 
 def load_body(
@@ -316,45 +312,28 @@
     )(token, pos, dpre_0, dpre_1, w_in_0, w_in_1)
 
 
-def most_body(token, valid, past, sig, x_turned, gout, gskip, w_in, w_cond, b_conv, w_res, w_skip, *outs):
+def forward_body(token, halo, pos, valid, past, sig, x_turned, gout, gskip, w_in, w_cond, b_conv, w_res, w_skip, *outs):
+    weights = (w_in, w_cond, b_conv, w_res, w_skip)
+    head_rows(1, halo, pos, valid, sig, x_turned, gout, gskip, weights, outs[:3])
     forward_tiles(
-        1, tiles_of(DILATION_STEP, split_rows(sig.shape[0])), None, None, valid, past, sig, x_turned, gout, gskip,
-        (w_in, w_cond, b_conv, w_res, w_skip), outs, DILATION_STEP,
+        1, tiles_of(DILATION_STEP, sig.shape[0]), None, None, valid, past, sig, x_turned, gout, gskip, weights, outs[3:],
+        DILATION_STEP,
     )
 
 
-def forward_most(token, *args):
+def forward_1(token, *args):
     part = args[-1].shape[0]
-    return call(
-        most_body,
+    parts = call(
+        forward_body,
         "forward_1",
         [ANYWHERE] + [VMEM] * len(args),
-        [VMEM] * 3,
-        rest_shapes(split_rows(args[2].shape[0]) - DILATION_STEP, part),
-    )(token, *args)
-
-
-def ends_body(token, halo, pos, valid, past, sig, x_turned, gout, gskip, w_in, w_cond, b_conv, w_res, w_skip, *outs):
-    weights = (w_in, w_cond, b_conv, w_res, w_skip)
-    rows = sig.shape[0]
-    head_rows(1, halo, pos, valid, sig, x_turned, gout, gskip, weights, outs[:3])
-    forward_tiles(
-        1, tiles_of(split_rows(rows), rows), None, None, valid, past, sig, x_turned, gout, gskip, weights, outs[3:],
-        split_rows(rows),
-    )
-
-
-def forward_ends(token, *args):
-    part = args[-1].shape[0]
-    rows = args[4].shape[0]
-    parts = call(
-        ends_body,
-        "ends_1",
-        [ANYWHERE] + [VMEM] * len(args),
         [VMEM] * 6,
-        rest_shapes(DILATION_STEP, part) + rest_shapes(rows - split_rows(rows), part),
+        rest_shapes(DILATION_STEP, part) + rest_shapes(args[4].shape[0] - DILATION_STEP, part),
     )(token, *args)
     return parts[:3], parts[3:]
+
+
+GROUPS = (((3, 1), (2, 0)), ((1, 2, 3, 0),))
 
 
 def own_place():
@@ -371,7 +350,9 @@
 
 def gradients_body(far, block, half, own, count, extra, token, valid, x_turned, gout, gskip, past_head, *refs):
     kepts, dpres, refs = refs[:count], refs[count : 2 * count], refs[2 * count :]
-    sources, (out, *targets) = refs[:extra], refs[extra : len(refs) - 1 - bool(extra)]
+    groups = GROUPS[half]
+    sources, outs = refs[:extra], refs[extra : len(refs) - 1 - bool(extra)]
+    outs, targets = outs[: len(groups)], outs[len(groups) :]
     acc = refs[-1 - bool(extra)]
     copies = []
     if extra:
@@ -422,10 +403,11 @@
                     acc[high - low + 2 * part : high - low + 2 * part + ONES, :] = made[part:]
             at += ONES
             acc[at:, :] = jnp.zeros((size - at, acc.shape[1]), F32)
-        for r in range(far):
-            for c in range(NEAR):
-                value = acc[r * block : (r + 1) * block, c * LANES : (c + 1) * LANES]
-                out[c ^ xy, turned(r ^ z, far)] = value.astype(out.dtype)
+        for group, out in zip(groups, outs):
+            for i, p in enumerate(group):
+                here = pl.ds(pl.multiple_of((xy ^ p) * LANES, LANES), LANES)
+                for r in range(far):
+                    out[i, turned(r ^ z, far)] = acc[r * block : (r + 1) * block, here].astype(out.dtype)
 
     for k in range(2):
         pl.when(which == k)(functools.partial(region, k))
@@ -434,11 +416,10 @@
 
 
 def gradients(half, own, token, far, block, valid, x_turned, gout, gskip, past_head, pieces, loads=()):
-    packed = (NEAR, far, block, LANES)
     wide = pieces[0][2].shape[1]
     count = len(pieces)
     sources = [in_hbm(x) for x in loads]
-    outs = [jax.ShapeDtypeStruct(packed, F32 if own else BF16)]
+    outs = [jax.ShapeDtypeStruct((len(group), far, block, LANES), F32 if own else BF16) for group in GROUPS[half]]
     scratch = [pltpu.VMEM((far * block, wide), F32)]
     if loads:
         outs += half_weights(loads[0], *loads[2:4]) + [jax.ShapeDtypeStruct(x.shape, x.dtype) for x in loads[4:]]
@@ -721,10 +702,16 @@
     b_conv, b_res, b_skip = (b.reshape(1, -1) for b in (b_conv, b_res, b_skip))
 
     def core_sum(half, token, theirs, mine):
-        kept, *sent = added(
-            f"core_sum_{half}", token, mine, [swapped(theirs, "core", 1)], [(1, F32)] + [(1, BF16)] * (NEAR - 1)
-        )
-        return kept[0], exchanged([x[0] for x in sent])
+        got = {}
+        for k, group in enumerate(GROUPS[half]):
+            blocks = added(
+                f"core_sum_{half}_{k}", token, mine[k], [swapped(theirs[k], "core", 1)],
+                [(1, BF16 if p else F32) for p in group],
+            )
+            token = blocks[0]
+            for p, part in zip(group, blocks):
+                got[p] = swapped(part[0], "near", p) if p else part[0]
+        return got[0], [got[p] for p in range(1, NEAR)]
 
     def near_sum(half, token, kept, got):
         kept, sent = added(f"near_sum_{half}", token, kept, got, [(far // 2, F32), (far // 2, BF16)])
@@ -767,17 +754,17 @@
     past_head, head_0 = head(halo, pos, val, *common, w_in_0, w_cond, b_conv, *outer_0)
     made_0 = (head_0, rest_0)
     fixed = (far, block, val, x_turned, grad_out, grad_skip, past_head)
-    theirs_0, w_in_1, *outer_1, b_res, b_skip = gradients(0, False, past_head, *fixed, made_0, loads)
+    *theirs_0, w_in_1, w_res_1, w_skip_1, b_res, b_skip = gradients(0, False, past_head, *fixed, made_0, loads)
+    outer_1 = (w_res_1, w_skip_1)
     weights_1 = (w_in_1, w_cond, b_conv, *outer_1)
-    (mine_0,) = gradients(0, True, theirs_0, *fixed, made_0)
-    most_1 = forward_most(mine_0, val, past, *common, *weights_1)
-    kept_0, got_0 = core_sum(0, most_1[0], theirs_0, mine_0)
-    head_1, last_1 = forward_ends(kept_0, halo, pos, val, past, *common, *weights_1)
-    made_1 = (head_1, most_1, last_1)
+    mine_0 = gradients(0, True, theirs_0[0], *fixed, made_0)
+    kept_0, got_0 = core_sum(0, mine_0[0], theirs_0, mine_0)
+    made_1 = forward_1(kept_0, halo, pos, val, past, *common, *weights_1)
     dpre_0, dpre_1 = ([p[2] for p in made] for made in (made_0, made_1))
-    (theirs_1,) = gradients(1, False, kept_0, *fixed, made_1)
-    (mine_1,) = gradients(1, True, theirs_1, *fixed, made_1)
-    kept_0, got_0 = near_sum(0, mine_1, kept_0, got_0)
+    theirs_1 = gradients(1, False, kept_0, *fixed, made_1)
+    mine_1 = gradients(1, True, theirs_1[0], *fixed, made_1)
+    (part,) = added("near_part_0", mine_1[0], got_0[2], [got_0[0]], [(far, F32)])
+    kept_0, got_0 = near_sum(0, part, kept_0, [part, got_0[1]])
     kept_1, got_1 = core_sum(1, kept_0, theirs_1, mine_1)
     ends_0, got_0 = far_sum(0, kept_1, kept_0, got_0)
     *grads, mark = input_gradients((0, 1), ends_0, [])
@@ -789,7 +776,7 @@
         ends_1, val, signal, [p[0] for p in made_0], [p[0] for p in made_1], outer_0, outer_1, b_res, b_skip
     )
     ends_1, got_1 = far_end(1, mark, ends_1, got_1)
-    early = early_rows(ends_1, pos, head_0[2], head_1[2], w_in_0, w_in_1)
+    early = early_rows(ends_1, pos, dpre_0[0], dpre_1[0], w_in_0, w_in_1)
     received = passed_along(early, -1)
     first = near_join(0, 0, early, ends_0, got_0)
     second = near_join(0, 1, first[0], ends_0, got_0)

time: 85.2 us -> 86.2 us (1.012)
  starting transfers between devices: 34.6 us -> 40.4 us
  waiting for transfers between devices: 9.8 us -> 4.58 us
    ppermute x24 -> x25, starting transfers between devices: 28.6 us -> 34.7 us  [swapped(): lax.ppermute(x, axis, [(i, i ^ k) for i in range(lax.axis_size(axis))])]
    ppermute x24 -> x25, waiting for transfers between devices: 9.8 us -> 4.58 us  [swapped(): lax.ppermute(x, axis, [(i, i ^ k) for i in range(lax.axis_size(axis))])]
    pallas_call x2 -> x1, Pallas kernels: 4.82 us -> 4.56 us  [forward_1(): call(forward_body, 'forward_1', [ANYWHERE] + [VMEM] * len(args), [VMEM] *...]
  transfers between devices with their start and end apart: 26 -> 27, of which waited for: 7 -> 6; matrix products, arithmetic and copies ran while one was open for 0% -> 0% of each run, Pallas kernels for 39% -> 39%
where the time goes in v2:
time: 86.2 us; the launch traced here: 86 us
  starting transfers between devices  40.4 us (47%)
  Pallas kernels  39 us (45%)
  waiting for transfers between devices  4.58 us (5%)
  between operations  1.04 us (1%)
  local copies, waits for them, and re-layouts  0.97 us (1%)
    ppermute x25, starting transfers between devices, swapped(): lax.ppermute(x, axis, [(i, i ^ k) for i in range(lax.axis_size(axis))])  34.7 us
    pallas_call x4, Pallas kernels, gradients(): call(functools.partial(gradients_body, far, block, half, own, count, len(...  9.17 us
    pallas_call x1, Pallas kernels, load(): call(load_body, 'load', [ANYWHERE] * len(sources), [VMEM] * len(shapes),...  7.83 us
    pallas_call x2, Pallas kernels, inputs(): call(functools.partial(inputs_body, steps, counts), f'inputs_{steps[0]}',...  7.71 us
    ppermute x2, starting transfers between devices, passed_along(): return lax.ppermute(x, AXES, pairs)  5.76 us
    ppermute x25, waiting for transfers between devices, swapped(): lax.ppermute(x, axis, [(i, i ^ k) for i in range(lax.axis_size(axis))])  4.58 us
    pallas_call x1, Pallas kernels, forward_1(): call(forward_body, 'forward_1', [ANYWHERE] + [VMEM] * len(args), [VMEM] *...  4.56 us
    pallas_call x2, Pallas kernels, unpack(): call(functools.partial(unpack_body, far, block), f'unpack_{half}', [ANYWH...  4 us
  transfers between devices with their start and end apart: 27, of which 6 were waited for; matrix products, arithmetic and copies ran while one was open for 0% of the time, Pallas kernels for 39%

profile of v2, /device:TPU:3, one launch (start us, length us, event | category | flops | bytes accessed | tf_op | source)
XLA Modules:
  0.0 86.0 jit_solution(6165946954661563401)
XLA Ops:
  0.6 1.0 %slice.3 = bf16[256,512]{1,0:T(8,128)(2,1)S(1)} slice(bf16[2048,512]{1,0:T(8,128)(2,1)} %sig.1), slice={[1792:2048], [0:512]} | slice | bytes 524288 | tf_op jit(solution)/shard_map/slice | solution.py:747
  1.6 3.1 %collective-permute-start = (bf16[256,512]{1,0:T(8,128)(2,1)S(1)}, bf16[256,512]{1,0:T(8,128)(2,1)S(1)}, u32[]{:S(2)}, u32[]{:S(2)}) collective-permute-start(bf16[256,512]{1,0:T(8,128)(2,1)S(1)} %slice.3), channel_id=1, source_target_pairs={{0,1},{1,2},{2,3},{3,4},{4,5},{5,6},{6,7},{7,8},{8,9},{9,10},{10,1... | collective-permute-start | bytes 786440 | tf_op jit(solution)/shard_map/ppermute | solution.py:668
  4.7 7.8 %load.1 = (s32[16,128]{1,0:T(8,128)S(1)}, s32[16,128]{1,0:T(8,128)S(1)}, f32[1,1024]{1,0:T(1,128)S(1)}, bf16[80,1024]{1,0:T(8,128)(2,1)S(1)}, bf16[1024,512]{1,0...) custom-call(s32[16,128]{1,0:T(8,128)} %bitcast.50, ...), custom_call_target="tpu_custom_call" | custom-call | flops 8000000000 | bytes 1 | tf_op jit(solution)/shard_map/load/pallas_call | solution.py:253
  13.4 2.3 %theirs_0.1 = (bf16[2,4,208,128]{3,2,1,0:T(8,128)(2,1)S(1)}, bf16[2,4,208,128]{3,2,1,0:T(8,128)(2,1)S(1)}, bf16[1024,512]{1,0:T(8,128)(2,1)S(1)}, bf16[256,512]{...) custom-call(bf16[512,256]{1,0:T(8,128)(2,1)S(1)} %get-tuple-element.93.token.past_he, ...), custom_call_target="tpu_custom_call" | custom-call | flops 1 | bytes 1 | tf_op jit(solution)/shard_map/theirs_0/pallas_call | solution.py:427
  15.7 1.0 %collective-permute-start.1 = (bf16[2,4,208,128]{3,2,1,0:T(8,128)(2,1)S(1)}, bf16[2,4,208,128]{3,2,1,0:T(8,128)(2,1)S(1)}, u32[]{:S(2)}, u32[]{:S(2)}) collective-permute-start(bf16[2,4,208,128]{3,2,1,0:T(8,128)(2,1)S(1)} %get-tuple-element.98.token), channel_id=1, source_target_pairs={{0,16},{16,0},{1,17},{17,1},{2,18},{18,2},{3,19},{19,3},{4,20},{20... | collective-permute-start | bytes 1277960 | tf_op jit(solution)/shard_map/ppermute | solution.py:592
  16.8 2.3 %mine_0.1 = (f32[2,4,208,128]{3,2,1,0:T(8,128)S(1)}, f32[2,4,208,128]{3,2,1,0:T(8,128)S(1)}) custom-call(bf16[2,4,208,128]{3,2,1,0:T(8,128)(2,1)S(1)} %get-tuple-element.98.token, s32[16,128]{1,0:T(8,128)S(1)} %get-tuple-element.83.valid, bf16[1120,2048]{1,0:T(8,128)(2,1)S(1)} %get-tuple-element.85.x_turned, bf16[2048,512]{1,0:T(8,128)(2,1)S(1)} %get-tuple-element.86.gout, ...), custom_call_target="tpu_custom_call" | custom-call | flops 1 | bytes 1 | tf_op jit(solution)/shard_map/mine_0/pallas_call | solution.py:427
  19.2 1.3 %collective-permute-start.3 = (bf16[4,208,128]{2,1,0:T(8,128)(2,1)S(1)}, bf16[4,208,128]{2,1,0:T(8,128)(2,1)S(1)}, u32[]{:S(2)}, u32[]{:S(2)}) collective-permute-start(bf16[4,208,128]{2,1,0:T(8,128)(2,1)S(1)} %bitcast.32), channel_id=1, source_target_pairs={{0,3},{1,2},{2,1},{3,0},{4,7},{5,6},{6,5},{7,4},{8,11},{9,10},{10,... | collective-permute-start | bytes 638984 | tf_op jit(solution)/shard_map/ppermute | solution.py:592
  20.5 1.2 %collective-permute-start.4 = (bf16[4,208,128]{2,1,0:T(8,128)(2,1)S(1)}, bf16[4,208,128]{2,1,0:T(8,128)(2,1)S(1)}, u32[]{:S(2)}, u32[]{:S(2)}) collective-permute-start(bf16[4,208,128]{2,1,0:T(8,128)(2,1)S(1)} %bitcast.38), channel_id=1, source_target_pairs={{0,1},{1,0},{2,3},{3,2},{4,5},{5,4},{6,7},{7,6},{8,9},{9,8},{10,11... | collective-permute-start | bytes 638984 | tf_op jit(solution)/shard_map/ppermute | solution.py:592
  22.1 4.6 %forward_1.1 = (bf16[256,256]{1,0:T(8,128)(2,1)S(1)}, bf16[256,256]{1,0:T(8,128)(2,1)S(1)}, bf16[256,512]{1,0:T(8,128)(2,1)S(1)}, bf16[1792,256]{1,0:T(8,128)(2,...) custom-call(f32[4,208,128]{2,1,0:T(8,128)S(1)} %bitcast.27, ...), custom_call_target="tpu_custom_call" | custom-call | flops 1 | bytes 1 | tf_op jit(solution)/shard_map/forward_1/pallas_call | solution.py:326
  26.7 2.2 %theirs_1.1.token = bf16[4,4,208,128]{3,2,1,0:T(8,128)(2,1)S(1)} custom-call(f32[4,208,128]{2,1,0:T(8,128)S(1)} %bitcast.28, s32[16,128]{1,0:T(8,128)S(1)} %get-tuple-element.83.valid, bf16[1120,2048]{1,0:T(8,128)(2,1)S(1)} %get-tuple-element.85.x_turned, bf16[2048,512]{1,0:T(8,128)(2,1)S(1)} %get-tuple-element.86.gout, ...), custom_call_target="tpu_custom_call" | custom-call | flops 1 | bytes 1 | tf_op jit(solution)/shard_map/theirs_1/pallas_call | solution.py:427
  28.9 1.3 %collective-permute-start.6 = (bf16[4,4,208,128]{3,2,1,0:T(8,128)(2,1)S(1)}, bf16[4,4,208,128]{3,2,1,0:T(8,128)(2,1)S(1)}, u32[]{:S(2)}, u32[]{:S(2)}) collective-permute-start(bf16[4,4,208,128]{3,2,1,0:T(8,128)(2,1)S(1)} %theirs_1.1.token), channel_id=1, source_target_pairs={{0,16},{16,0},{1,17},{17,1},{2,18},{18,2},{3,19},{19,3},{4,20},{20... | collective-permute-start | bytes 2555912 | tf_op jit(solution)/shard_map/ppermute | solution.py:592
  30.2 2.4 %mine_1.1.token.refs_0_ = f32[4,4,208,128]{3,2,1,0:T(8,128)S(1)} custom-call(bf16[4,4,208,128]{3,2,1,0:T(8,128)(2,1)S(1)} %theirs_1.1.token, s32[16,128]{1,0:T(8,128)S(1)} %get-tuple-element.83.valid, bf16[1120,2048]{1,0:T(8,128)(2,1)S(1)} %get-tuple-element.85.x_turned, bf16[2048,512]{1,0:T(8,128)(2,1)S(1)} %get-tuple-element.86.gout, ...), custom_call_target="tpu_custom_call" | custom-call | flops 2000000000 | bytes 1 | tf_op jit(solution)/shard_map/mine_1/pallas_call | solution.py:427
  32.8 1.4 %collective-permute-start.7 = (bf16[2,208,128]{2,1,0:T(8,128)(2,1)S(1)}, bf16[2,208,128]{2,1,0:T(8,128)(2,1)S(1)}, u32[]{:S(2)}, u32[]{:S(2)}) collective-permute-start(bf16[2,208,128]{2,1,0:T(8,128)(2,1)S(1)} %get-tuple-element.116), channel_id=1, source_target_pairs={{0,4},{4,0},{8,12},{12,8},{1,5},{5,1},{9,13},{13,9},{2,6},{6,2},{1... | collective-permute-start | bytes 319496 | tf_op jit(solution)/shard_map/ppermute | solution.py:592
  35.8 1.1 %collective-permute-start.11 = (bf16[4,208,128]{2,1,0:T(8,128)(2,1)S(1)}, bf16[4,208,128]{2,1,0:T(8,128)(2,1)S(1)}, u32[]{:S(2)}, u32[]{:S(2)}) collective-permute-start(bf16[4,208,128]{2,1,0:T(8,128)(2,1)S(1)} %bitcast.39), channel_id=1, source_target_pairs={{0,3},{1,2},{2,1},{3,0},{4,7},{5,6},{6,5},{7,4},{8,11},{9,10},{10,... | collective-permute-start | bytes 638984 | tf_op jit(solution)/shard_map/ppermute | solution.py:592
  37.4 2.4 %collective-permute-start.8 = (bf16[2,208,128]{2,1,0:T(8,128)(2,1)S(1)}, bf16[2,208,128]{2,1,0:T(8,128)(2,1)S(1)}, u32[]{:S(2)}, u32[]{:S(2)}) collective-permute-start(bf16[2,208,128]{2,1,0:T(8,128)(2,1)S(1)} %far_sum_0.1.token.mine), channel_id=1, source_target_pairs={{0,8},{4,12},{8,0},{12,4},{1,9},{5,13},{9,1},{13,5},{2,10},{6,14},... | collective-permute-start | bytes 319496 | tf_op jit(solution)/shard_map/ppermute | solution.py:592
  39.8 3.9 %inputs_0.1 = (f32[2048,512]{1,0:T(8,128)}, f32[80,2048]{1,0:T(8,128)}, f32[8,128]{1,0:T(8,128)S(1)}) custom-call(bf16[2,208,128]{2,1,0:T(8,128)(2,1)S(1)} %far_sum_0.1.token.mine, bf16[256,256]{1,0:T(8,128)(2,1)S(1)} %get-tuple-element.117.received.refs_0_, bf16[2048,512]{1,0:T(8,128)(2,1)S(1)} %get-tuple-element.86.gout, ...), custom_call_target="tpu_custom_call" | custom-call | flops 1 | bytes 1 | tf_op jit(solution)/shard_map/inputs_0/pallas_call | solution.py:517
  43.8 2.3 %collective-permute-start.12 = (bf16[2,208,128]{2,1,0:T(8,128)(2,1)S(1)}, bf16[2,208,128]{2,1,0:T(8,128)(2,1)S(1)}, u32[]{:S(2)}, u32[]{:S(2)}) collective-permute-start(bf16[2,208,128]{2,1,0:T(8,128)(2,1)S(1)} %far_end_0.1.token.refs_0_), channel_id=1, source_target_pairs={{0,4},{4,0},{8,12},{12,8},{1,5},{5,1},{9,13},{13,9},{2,6},{6,2},{1... | collective-permute-start | bytes 319496 | tf_op jit(solution)/shard_map/ppermute | solution.py:592
  46.7 1.4 %collective-permute-done.12.refs_1_ = bf16[2,208,128]{2,1,0:T(8,128)(2,1)S(1)} collective-permute-done((bf16[2,208,128]{2,1,0:T(8,128)(2,1)S(1)}, bf16[2,208,128]{2,1,0:T(8,128)(2,1)S(1)}, u32[]{:S(2)}, u32[]{:S(2)}) %collective-permute-start.12) | collective-permute-done | bytes 106528 | tf_op jit(solution)/shard_map/ppermute | solution.py:592
  48.2 1.3 %collective-permute-start.15 = (bf16[4,208,128]{2,1,0:T(8,128)(2,1)S(1)}, bf16[4,208,128]{2,1,0:T(8,128)(2,1)S(1)}, u32[]{:S(2)}, u32[]{:S(2)}) collective-permute-start(bf16[4,208,128]{2,1,0:T(8,128)(2,1)S(1)} %far_join_0.1.token), channel_id=1, source_target_pairs={{0,3},{1,2},{2,1},{3,0},{4,7},{5,6},{6,5},{7,4},{8,11},{9,10},{10,... | collective-permute-start | bytes 638984 | tf_op jit(solution)/shard_map/ppermute | solution.py:592
  49.4 0.8 collective-permute-start.17
  51.5 3.3 %collective-permute-start.14 = (bf16[2,208,128]{2,1,0:T(8,128)(2,1)S(1)}, bf16[2,208,128]{2,1,0:T(8,128)(2,1)S(1)}, u32[]{:S(2)}, u32[]{:S(2)}) collective-permute-start(bf16[2,208,128]{2,1,0:T(8,128)(2,1)S(1)} %far_sum_1.1.token.mine), channel_id=1, source_target_pairs={{0,8},{4,12},{8,0},{12,4},{1,9},{5,13},{9,1},{13,5},{2,10},{6,14},... | collective-permute-start | bytes 319496 | tf_op jit(solution)/shard_map/ppermute | solution.py:592
  54.8 3.6 %outputs.1 = (bf16[2048,512]{1,0:T(8,128)(2,1)}, bf16[2048,512]{1,0:T(8,128)(2,1)}, f32[8,128]{1,0:T(8,128)S(1)}) custom-call(bf16[2,208,128]{2,1,0:T(8,128)(2,1)S(1)} %far_sum_1.1.token.mine, s32[16,128]{1,0:T(8,128)S(1)} %get-tuple-element.83.valid, bf16[2048,512]{1,0:T(8,128)(2,1)S(1)} %get-tuple-element.84.sig, ...), custom_call_target="tpu_custom_call" | custom-call | flops 1 | bytes 1 | tf_op jit(solution)/shard_map/outputs/pallas_call | solution.py:460
  58.5 1.2 %collective-permute-start.18 = (bf16[2,208,128]{2,1,0:T(8,128)(2,1)S(1)}, bf16[2,208,128]{2,1,0:T(8,128)(2,1)S(1)}, u32[]{:S(2)}, u32[]{:S(2)}) collective-permute-start(bf16[2,208,128]{2,1,0:T(8,128)(2,1)S(1)} %far_end_1.1.token.refs_0_), channel_id=1, source_target_pairs={{0,4},{4,0},{8,12},{12,8},{1,5},{5,1},{9,13},{13,9},{2,6},{6,2},{1... | collective-permute-start | bytes 319496 | tf_op jit(solution)/shard_map/ppermute | solution.py:592
  60.2 2.6 %collective-permute-start.19 = (bf16[256,512]{1,0:T(8,128)(2,1)S(1)}, bf16[256,512]{1,0:T(8,128)(2,1)S(1)}, u32[]{:S(2)}, u32[]{:S(2)}) collective-permute-start(bf16[256,512]{1,0:T(8,128)(2,1)S(1)} %early.1.token), channel_id=1, source_target_pairs={{1,0},{2,1},{3,2},{4,3},{5,4},{6,5},{7,6},{8,7},{9,8},{10,9},{11,1... | collective-permute-start | bytes 786440 | tf_op jit(solution)/shard_map/ppermute | solution.py:668
  63.0 1.7 %collective-permute-start.20 = (bf16[4,208,128]{2,1,0:T(8,128)(2,1)S(1)}, bf16[4,208,128]{2,1,0:T(8,128)(2,1)S(1)}, u32[]{:S(2)}, u32[]{:S(2)}) collective-permute-start(bf16[4,208,128]{2,1,0:T(8,128)(2,1)S(1)} %far_join_1.1.token), channel_id=1, source_target_pairs={{0,3},{1,2},{2,1},{3,0},{4,7},{5,6},{6,5},{7,4},{8,11},{9,10},{10,... | collective-permute-start | bytes 638984 | tf_op jit(solution)/shard_map/ppermute | solution.py:592
  64.7 4.8 %collective-permute-start.25 = (bf16[4,208,128]{2,1,0:T(8,128)(2,1)S(1)}, bf16[4,208,128]{2,1,0:T(8,128)(2,1)S(1)}, u32[]{:S(2)}, u32[]{:S(2)}) collective-permute-start(bf16[4,208,128]{2,1,0:T(8,128)(2,1)S(1)} %far_join_1.1.token), channel_id=1, source_target_pairs={{0,2},{1,3},{2,0},{3,1},{4,6},{5,7},{6,4},{7,5},{8,10},{9,11},{10,... | collective-permute-start | bytes 638984 | tf_op jit(solution)/shard_map/ppermute | solution.py:592
  69.5 1.4 %collective-permute-start.23 = (bf16[2,4,208,128]{3,2,1,0:T(8,128)(2,1)S(1)}, bf16[2,4,208,128]{3,2,1,0:T(8,128)(2,1)S(1)}, u32[]{:S(2)}, u32[]{:S(2)}) collective-permute-start(bf16[2,4,208,128]{3,2,1,0:T(8,128)(2,1)S(1)} %near_join_0_1.1.token.refs_1_), channel_id=1, source_target_pairs={{0,16},{16,0},{1,17},{17,1},{2,18},{18,2},{3,19},{19,3},{4,20},{20... | collective-permute-start | bytes 1277960 | tf_op jit(solution)/shard_map/ppermute | solution.py:592
  70.9 4.8 %collective-permute-start.22 = (bf16[2,4,208,128]{3,2,1,0:T(8,128)(2,1)S(1)}, bf16[2,4,208,128]{3,2,1,0:T(8,128)(2,1)S(1)}, u32[]{:S(2)}, u32[]{:S(2)}) collective-permute-start(bf16[2,4,208,128]{3,2,1,0:T(8,128)(2,1)S(1)} %near_join_0_0.1.token.refs_0_), channel_id=1, source_target_pairs={{0,16},{16,0},{1,17},{17,1},{2,18},{18,2},{3,19},{19,3},{4,20},{20... | collective-permute-start | bytes 1277960 | tf_op jit(solution)/shard_map/ppermute | solution.py:592
  75.6 3.8 %inputs_2.1 = (f32[2048,512]{1,0:T(8,128)}, f32[80,2048]{1,0:T(8,128)}, f32[8,128]{1,0:T(8,128)S(1)}) custom-call(bf16[4,208,128]{2,1,0:T(8,128)(2,1)S(1)} %far_join_1.1.token, bf16[256,512]{1,0:T(8,128)(2,1)S(1)} %collective-permute-done.19.received, bf16[2048,512]{1,0:T(8,128)(2,1)S(1)} %get-tuple-element.86.gout, ...), custom_call_target="tpu_custom_call", output_to_operand_aliasing={{0}: (11, {}), {1}: (12, {})} | custom-call | flops 1 | bytes 1 | tf_op jit(solution)/shard_map/inputs_2/pallas_call | solution.py:517
  80.3 1.0 %collective-permute-done.24 = bf16[4,208,128]{2,1,0:T(8,128)(2,1)S(1)} collective-permute-done((bf16[4,208,128]{2,1,0:T(8,128)(2,1)S(1)}, bf16[4,208,128]{2,1,0:T(8,128)(2,1)S(1)}, u32[]{:S(2)}, u32[]{:S(2)}) %collective-permute-start.24) | collective-permute-done | bytes 213024 | tf_op jit(solution)/shard_map/ppermute | solution.py:592
  81.9 2.0 %unpack_0.1 = (f32[512,1024]{1,0:T(8,128)}, f32[512,1024]{1,0:T(8,128)}, f32[80,1024]{1,0:T(8,128)}, f32[1,1024]{1,0:T(1,128)}, f32[512,512]{1,0:T(8,128)}, /*in...) custom-call(bf16[2,4,208,128]{3,2,1,0:T(8,128)(2,1)S(1)} %collective-permute-done.21.token.refs_2_, ...), custom_call_target="tpu_custom_call" | custom-call | flops 1 | bytes 1 | tf_op jit(solution)/shard_map/unpack_0/pallas_call | solution.py:579
  83.9 2.0 %unpack_1.1 = (f32[512,1024]{1,0:T(8,128)}, f32[512,1024]{1,0:T(8,128)}, f32[80,1024]{1,0:T(8,128)}, f32[1,1024]{1,0:T(1,128)}, f32[512,512]{1,0:T(8,128)}, /*in...) custom-call(f32[8,128]{1,0:T(8,128)S(1)} %get-tuple-element.137.toke, ...), custom_call_target="tpu_custom_call", output_to_operand_aliasing={{0}: (5, {}), {1}: (6, {}), {2}: (7, {}), {3}: (8, {}), {4}... | custom-call | flops 1 | bytes 1 | tf_op jit(solution)/shard_map/unpack_1/pallas_call | solution.py:579
  (52 shorter events, 7.7 us)
Async XLA Ops:
  1.6 11.0 %collective-permute-start = (bf16[256,512]{1,0:T(8,128)(2,1)S(1)}, bf16[256,512]{1,0:T(8,128)(2,1)S(1)}, u32[]{:S(2)}, u32[]{:S(2)}) collective-permute-start(bf16[256,512]{1,0:T(8,128)(2,1)S(1)} %slice.3), channel_id=1, source_target_pairs={{0,1},{1,2},{2,3},{3,4},{4,5},{5,6},{6,7},{7,8},{8,9},{9,10},{10,1... | collective-permute-start | bytes 786440 | tf_op jit(solution)/shard_map/ppermute | solution.py:668
  15.7 3.5 %collective-permute-start.1 = (bf16[2,4,208,128]{3,2,1,0:T(8,128)(2,1)S(1)}, bf16[2,4,208,128]{3,2,1,0:T(8,128)(2,1)S(1)}, u32[]{:S(2)}, u32[]{:S(2)}) collective-permute-start(bf16[2,4,208,128]{3,2,1,0:T(8,128)(2,1)S(1)} %get-tuple-element.98.token), channel_id=1, source_target_pairs={{0,16},{16,0},{1,17},{17,1},{2,18},{18,2},{3,19},{19,3},{4,20},{20... | collective-permute-start | bytes 1277960 | tf_op jit(solution)/shard_map/ppermute | solution.py:592
  16.7 5.0 %collective-permute-start.2 = (bf16[2,4,208,128]{3,2,1,0:T(8,128)(2,1)S(1)}, bf16[2,4,208,128]{3,2,1,0:T(8,128)(2,1)S(1)}, u32[]{:S(2)}, u32[]{:S(2)}) collective-permute-start(bf16[2,4,208,128]{3,2,1,0:T(8,128)(2,1)S(1)} %get-tuple-element.102), channel_id=1, source_target_pairs={{0,16},{16,0},{1,17},{17,1},{2,18},{18,2},{3,19},{19,3},{4,20},{20... | collective-permute-start | bytes 1277960 | tf_op jit(solution)/shard_map/ppermute | solution.py:592
  19.2 13.4 %collective-permute-start.3 = (bf16[4,208,128]{2,1,0:T(8,128)(2,1)S(1)}, bf16[4,208,128]{2,1,0:T(8,128)(2,1)S(1)}, u32[]{:S(2)}, u32[]{:S(2)}) collective-permute-start(bf16[4,208,128]{2,1,0:T(8,128)(2,1)S(1)} %bitcast.32), channel_id=1, source_target_pairs={{0,3},{1,2},{2,1},{3,0},{4,7},{5,6},{6,5},{7,4},{8,11},{9,10},{10,... | collective-permute-start | bytes 638984 | tf_op jit(solution)/shard_map/ppermute | solution.py:592
  20.5 12.1 %collective-permute-start.4 = (bf16[4,208,128]{2,1,0:T(8,128)(2,1)S(1)}, bf16[4,208,128]{2,1,0:T(8,128)(2,1)S(1)}, u32[]{:S(2)}, u32[]{:S(2)}) collective-permute-start(bf16[4,208,128]{2,1,0:T(8,128)(2,1)S(1)} %bitcast.38), channel_id=1, source_target_pairs={{0,1},{1,0},{2,3},{3,2},{4,5},{5,4},{6,7},{7,6},{8,9},{9,8},{10,11... | collective-permute-start | bytes 638984 | tf_op jit(solution)/shard_map/ppermute | solution.py:592
  21.8 10.8 %collective-permute-start.5 = (bf16[4,208,128]{2,1,0:T(8,128)(2,1)S(1)}, bf16[4,208,128]{2,1,0:T(8,128)(2,1)S(1)}, u32[]{:S(2)}, u32[]{:S(2)}) collective-permute-start(bf16[4,208,128]{2,1,0:T(8,128)(2,1)S(1)} %bitcast.44), channel_id=1, source_target_pairs={{0,2},{1,3},{2,0},{3,1},{4,6},{5,7},{6,4},{7,5},{8,10},{9,11},{10,... | collective-permute-start | bytes 638984 | tf_op jit(solution)/shard_map/ppermute | solution.py:592
  28.9 5.3 %collective-permute-start.6 = (bf16[4,4,208,128]{3,2,1,0:T(8,128)(2,1)S(1)}, bf16[4,4,208,128]{3,2,1,0:T(8,128)(2,1)S(1)}, u32[]{:S(2)}, u32[]{:S(2)}) collective-permute-start(bf16[4,4,208,128]{3,2,1,0:T(8,128)(2,1)S(1)} %theirs_1.1.token), channel_id=1, source_target_pairs={{0,16},{16,0},{1,17},{17,1},{2,18},{18,2},{3,19},{19,3},{4,20},{20... | collective-permute-start | bytes 2555912 | tf_op jit(solution)/shard_map/ppermute | solution.py:592
  32.8 4.6 %collective-permute-start.7 = (bf16[2,208,128]{2,1,0:T(8,128)(2,1)S(1)}, bf16[2,208,128]{2,1,0:T(8,128)(2,1)S(1)}, u32[]{:S(2)}, u32[]{:S(2)}) collective-permute-start(bf16[2,208,128]{2,1,0:T(8,128)(2,1)S(1)} %get-tuple-element.116), channel_id=1, source_target_pairs={{0,4},{4,0},{8,12},{12,8},{1,5},{5,1},{9,13},{13,9},{2,6},{6,2},{1... | collective-permute-start | bytes 319496 | tf_op jit(solution)/shard_map/ppermute | solution.py:592
  34.3 11.8 %collective-permute-start.9 = (bf16[4,208,128]{2,1,0:T(8,128)(2,1)S(1)}, bf16[4,208,128]{2,1,0:T(8,128)(2,1)S(1)}, u32[]{:S(2)}, u32[]{:S(2)}) collective-permute-start(bf16[4,208,128]{2,1,0:T(8,128)(2,1)S(1)} %bitcast.43), channel_id=1, source_target_pairs={{0,1},{1,0},{2,3},{3,2},{4,5},{5,4},{6,7},{7,6},{8,9},{9,8},{10,11... | collective-permute-start | bytes 638984 | tf_op jit(solution)/shard_map/ppermute | solution.py:592
  35.1 11.0 %collective-permute-start.10 = (bf16[4,208,128]{2,1,0:T(8,128)(2,1)S(1)}, bf16[4,208,128]{2,1,0:T(8,128)(2,1)S(1)}, u32[]{:S(2)}, u32[]{:S(2)}) collective-permute-start(bf16[4,208,128]{2,1,0:T(8,128)(2,1)S(1)} %bitcast.41), channel_id=1, source_target_pairs={{0,2},{1,3},{2,0},{3,1},{4,6},{5,7},{6,4},{7,5},{8,10},{9,11},{10,... | collective-permute-start | bytes 638984 | tf_op jit(solution)/shard_map/ppermute | solution.py:592
  35.8 10.6 %collective-permute-start.11 = (bf16[4,208,128]{2,1,0:T(8,128)(2,1)S(1)}, bf16[4,208,128]{2,1,0:T(8,128)(2,1)S(1)}, u32[]{:S(2)}, u32[]{:S(2)}) collective-permute-start(bf16[4,208,128]{2,1,0:T(8,128)(2,1)S(1)} %bitcast.39), channel_id=1, source_target_pairs={{0,3},{1,2},{2,1},{3,0},{4,7},{5,6},{6,5},{7,4},{8,11},{9,10},{10,... | collective-permute-start | bytes 638984 | tf_op jit(solution)/shard_map/ppermute | solution.py:592
  37.4 6.3 %collective-permute-start.8 = (bf16[2,208,128]{2,1,0:T(8,128)(2,1)S(1)}, bf16[2,208,128]{2,1,0:T(8,128)(2,1)S(1)}, u32[]{:S(2)}, u32[]{:S(2)}) collective-permute-start(bf16[2,208,128]{2,1,0:T(8,128)(2,1)S(1)} %far_sum_0.1.token.mine), channel_id=1, source_target_pairs={{0,8},{4,12},{8,0},{12,4},{1,9},{5,13},{9,1},{13,5},{2,10},{6,14},... | collective-permute-start | bytes 319496 | tf_op jit(solution)/shard_map/ppermute | solution.py:592
  43.8 4.3 %collective-permute-start.12 = (bf16[2,208,128]{2,1,0:T(8,128)(2,1)S(1)}, bf16[2,208,128]{2,1,0:T(8,128)(2,1)S(1)}, u32[]{:S(2)}, u32[]{:S(2)}) collective-permute-start(bf16[2,208,128]{2,1,0:T(8,128)(2,1)S(1)} %far_end_0.1.token.refs_0_), channel_id=1, source_target_pairs={{0,4},{4,0},{8,12},{12,8},{1,5},{5,1},{9,13},{13,9},{2,6},{6,2},{1... | collective-permute-start | bytes 319496 | tf_op jit(solution)/shard_map/ppermute | solution.py:592
  46.5 5.0 %collective-permute-start.13 = (bf16[2,208,128]{2,1,0:T(8,128)(2,1)S(1)}, bf16[2,208,128]{2,1,0:T(8,128)(2,1)S(1)}, u32[]{:S(2)}, u32[]{:S(2)}) collective-permute-start(bf16[2,208,128]{2,1,0:T(8,128)(2,1)S(1)} %get-tuple-element.123), channel_id=1, source_target_pairs={{0,4},{4,0},{8,12},{12,8},{1,5},{5,1},{9,13},{13,9},{2,6},{6,2},{1... | collective-permute-start | bytes 319496 | tf_op jit(solution)/shard_map/ppermute | solution.py:592
  48.2 14.7 %collective-permute-start.15 = (bf16[4,208,128]{2,1,0:T(8,128)(2,1)S(1)}, bf16[4,208,128]{2,1,0:T(8,128)(2,1)S(1)}, u32[]{:S(2)}, u32[]{:S(2)}) collective-permute-start(bf16[4,208,128]{2,1,0:T(8,128)(2,1)S(1)} %far_join_0.1.token), channel_id=1, source_target_pairs={{0,3},{1,2},{2,1},{3,0},{4,7},{5,6},{6,5},{7,4},{8,11},{9,10},{10,... | collective-permute-start | bytes 638984 | tf_op jit(solution)/shard_map/ppermute | solution.py:592
  49.4 13.5 %collective-permute-start.17 = (bf16[4,208,128]{2,1,0:T(8,128)(2,1)S(1)}, bf16[4,208,128]{2,1,0:T(8,128)(2,1)S(1)}, u32[]{:S(2)}, u32[]{:S(2)}) collective-permute-start(bf16[4,208,128]{2,1,0:T(8,128)(2,1)S(1)} %far_join_0.1.token), channel_id=1, source_target_pairs={{0,2},{1,3},{2,0},{3,1},{4,6},{5,7},{6,4},{7,5},{8,10},{9,11},{10,... | collective-permute-start | bytes 638984 | tf_op jit(solution)/shard_map/ppermute | solution.py:592
  50.3 12.6 %collective-permute-start.16 = (bf16[4,208,128]{2,1,0:T(8,128)(2,1)S(1)}, bf16[4,208,128]{2,1,0:T(8,128)(2,1)S(1)}, u32[]{:S(2)}, u32[]{:S(2)}) collective-permute-start(bf16[4,208,128]{2,1,0:T(8,128)(2,1)S(1)} %far_join_0.1.token), channel_id=1, source_target_pairs={{0,1},{1,0},{2,3},{3,2},{4,5},{5,4},{6,7},{7,6},{8,9},{9,8},{10,11... | collective-permute-start | bytes 638984 | tf_op jit(solution)/shard_map/ppermute | solution.py:592
  51.5 6.9 %collective-permute-start.14 = (bf16[2,208,128]{2,1,0:T(8,128)(2,1)S(1)}, bf16[2,208,128]{2,1,0:T(8,128)(2,1)S(1)}, u32[]{:S(2)}, u32[]{:S(2)}) collective-permute-start(bf16[2,208,128]{2,1,0:T(8,128)(2,1)S(1)} %far_sum_1.1.token.mine), channel_id=1, source_target_pairs={{0,8},{4,12},{8,0},{12,4},{1,9},{5,13},{9,1},{13,5},{2,10},{6,14},... | collective-permute-start | bytes 319496 | tf_op jit(solution)/shard_map/ppermute | solution.py:592
  58.5 4.4 %collective-permute-start.18 = (bf16[2,208,128]{2,1,0:T(8,128)(2,1)S(1)}, bf16[2,208,128]{2,1,0:T(8,128)(2,1)S(1)}, u32[]{:S(2)}, u32[]{:S(2)}) collective-permute-start(bf16[2,208,128]{2,1,0:T(8,128)(2,1)S(1)} %far_end_1.1.token.refs_0_), channel_id=1, source_target_pairs={{0,4},{4,0},{8,12},{12,8},{1,5},{5,1},{9,13},{13,9},{2,6},{6,2},{1... | collective-permute-start | bytes 319496 | tf_op jit(solution)/shard_map/ppermute | solution.py:592
  60.2 10.7 %collective-permute-start.19 = (bf16[256,512]{1,0:T(8,128)(2,1)S(1)}, bf16[256,512]{1,0:T(8,128)(2,1)S(1)}, u32[]{:S(2)}, u32[]{:S(2)}) collective-permute-start(bf16[256,512]{1,0:T(8,128)(2,1)S(1)} %early.1.token), channel_id=1, source_target_pairs={{1,0},{2,1},{3,2},{4,3},{5,4},{6,5},{7,6},{8,7},{9,8},{10,9},{11,1... | collective-permute-start | bytes 786440 | tf_op jit(solution)/shard_map/ppermute | solution.py:668
  63.0 16.5 %collective-permute-start.20 = (bf16[4,208,128]{2,1,0:T(8,128)(2,1)S(1)}, bf16[4,208,128]{2,1,0:T(8,128)(2,1)S(1)}, u32[]{:S(2)}, u32[]{:S(2)}) collective-permute-start(bf16[4,208,128]{2,1,0:T(8,128)(2,1)S(1)} %far_join_1.1.token), channel_id=1, source_target_pairs={{0,3},{1,2},{2,1},{3,0},{4,7},{5,6},{6,5},{7,4},{8,11},{9,10},{10,... | collective-permute-start | bytes 638984 | tf_op jit(solution)/shard_map/ppermute | solution.py:592
  64.7 15.6 %collective-permute-start.25 = (bf16[4,208,128]{2,1,0:T(8,128)(2,1)S(1)}, bf16[4,208,128]{2,1,0:T(8,128)(2,1)S(1)}, u32[]{:S(2)}, u32[]{:S(2)}) collective-permute-start(bf16[4,208,128]{2,1,0:T(8,128)(2,1)S(1)} %far_join_1.1.token), channel_id=1, source_target_pairs={{0,2},{1,3},{2,0},{3,1},{4,6},{5,7},{6,4},{7,5},{8,10},{9,11},{10,... | collective-permute-start | bytes 638984 | tf_op jit(solution)/shard_map/ppermute | solution.py:592
  69.5 11.8 %collective-permute-start.24 = (bf16[4,208,128]{2,1,0:T(8,128)(2,1)S(1)}, bf16[4,208,128]{2,1,0:T(8,128)(2,1)S(1)}, u32[]{:S(2)}, u32[]{:S(2)}) collective-permute-start(bf16[4,208,128]{2,1,0:T(8,128)(2,1)S(1)} %far_join_1.1.token), channel_id=1, source_target_pairs={{0,1},{1,0},{2,3},{3,2},{4,5},{5,4},{6,7},{7,6},{8,9},{9,8},{10,11... | collective-permute-start | bytes 638984 | tf_op jit(solution)/shard_map/ppermute | solution.py:592
  69.5 12.4 %collective-permute-start.23 = (bf16[2,4,208,128]{3,2,1,0:T(8,128)(2,1)S(1)}, bf16[2,4,208,128]{3,2,1,0:T(8,128)(2,1)S(1)}, u32[]{:S(2)}, u32[]{:S(2)}) collective-permute-start(bf16[2,4,208,128]{3,2,1,0:T(8,128)(2,1)S(1)} %near_join_0_1.1.token.refs_1_), channel_id=1, source_target_pairs={{0,16},{16,0},{1,17},{17,1},{2,18},{18,2},{3,19},{19,3},{4,20},{20... | collective-permute-start | bytes 1277960 | tf_op jit(solution)/shard_map/ppermute | solution.py:592
  70.9 11.0 %collective-permute-start.22 = (bf16[2,4,208,128]{3,2,1,0:T(8,128)(2,1)S(1)}, bf16[2,4,208,128]{3,2,1,0:T(8,128)(2,1)S(1)}, u32[]{:S(2)}, u32[]{:S(2)}) collective-permute-start(bf16[2,4,208,128]{3,2,1,0:T(8,128)(2,1)S(1)} %near_join_0_0.1.token.refs_0_), channel_id=1, source_target_pairs={{0,16},{16,0},{1,17},{17,1},{2,18},{18,2},{3,19},{19,3},{4,20},{20... | collective-permute-start | bytes 1277960 | tf_op jit(solution)/shard_map/ppermute | solution.py:592
  79.5 2.4 %collective-permute-start.21 = (bf16[2,4,208,128]{3,2,1,0:T(8,128)(2,1)S(1)}, bf16[2,4,208,128]{3,2,1,0:T(8,128)(2,1)S(1)}, u32[]{:S(2)}, u32[]{:S(2)}) collective-permute-start(bf16[2,4,208,128]{3,2,1,0:T(8,128)(2,1)S(1)} %near_join_1_0.1.token.refs_0_), channel_id=1, source_target_pairs={{0,16},{16,0},{1,17},{17,1},{2,18},{18,2},{3,19},{19,3},{4,20},{20... | collective-permute-start | bytes 1277960 | tf_op jit(solution)/shard_map/ppermute | solution.py:592
  81.3 2.6 %collective-permute-start.26 = (bf16[2,4,208,128]{3,2,1,0:T(8,128)(2,1)S(1)}, bf16[2,4,208,128]{3,2,1,0:T(8,128)(2,1)S(1)}, u32[]{:S(2)}, u32[]{:S(2)}) collective-permute-start(bf16[2,4,208,128]{3,2,1,0:T(8,128)(2,1)S(1)} %near_join_1_1.1.refs_1_), channel_id=1, source_target_pairs={{0,16},{16,0},{1,17},{17,1},{2,18},{18,2},{3,19},{19,3},{4,20},{20... | collective-permute-start | bytes 1277960 | tf_op jit(solution)/shard_map/ppermute | solution.py:592

commit v3 on v2

--- a/solution.py
+++ b/solution.py
@@ -20,7 +20,7 @@
 MEGA = 1 << 20
 COSTS = {
     "load": 8, "head": 2, "near_sum_0": 7, "mine_1": 2, "near_part_0": 1,
-    "far_sum_0": 8, "near_sum_1": 4, "near_join_0_1": 2, "near_join_1_1": 4, "far_join_0": 4,
+    "near_part_1": 2, "near_sum_1": 4, "near_join_0_1": 2, "near_join_1_1": 4, "far_join_0": 4,
 }
 FLOPS = 10**9
 
@@ -384,7 +384,11 @@
                 return below(past_head[low : min(high, width), :], x_turned[width : max(high, width), here])
             return x_turned[low:high, here]
 
-        acc[: high - low, :] = product(turned_rows, dpres)
+        def keep(first, value):
+            for c in range(NEAR):
+                acc[c, first : first + value.shape[0], :] = value[:, c * LANES : (c + 1) * LANES]
+
+        keep(0, product(turned_rows, dpres))
         at = high - low
         if high == ends:
             mask = jnp.broadcast_to(row(lines_of(valid, slice(0, rows)).astype(F32)).astype(BF16), (ONES, rows))
@@ -397,17 +401,16 @@
                 for kept in kepts:
                     cuts.append(cuts[-1] + kept.shape[1])
                 made = product(kept_rows, [ref.at[pl.ds(a, b - a)] for a, b in zip(cuts, cuts[1:])])
-                acc[at : at + part, :] = made[:part]
+                keep(at, made[:part])
                 at += part
                 if i == half:
-                    acc[high - low + 2 * part : high - low + 2 * part + ONES, :] = made[part:]
+                    keep(high - low + 2 * part, made[part:])
             at += ONES
-            acc[at:, :] = jnp.zeros((size - at, acc.shape[1]), F32)
+            acc[:, at:, :] = jnp.zeros((NEAR, size - at, LANES), F32)
         for group, out in zip(groups, outs):
             for i, p in enumerate(group):
-                here = pl.ds(pl.multiple_of((xy ^ p) * LANES, LANES), LANES)
                 for r in range(far):
-                    out[i, turned(r ^ z, far)] = acc[r * block : (r + 1) * block, here].astype(out.dtype)
+                    out[i, turned(r ^ z, far)] = acc[xy ^ p, r * block : (r + 1) * block, :].astype(out.dtype)
 
     for k in range(2):
         pl.when(which == k)(functools.partial(region, k))
@@ -416,11 +419,10 @@
 
 
 def gradients(half, own, token, far, block, valid, x_turned, gout, gskip, past_head, pieces, loads=()):
-    wide = pieces[0][2].shape[1]
     count = len(pieces)
     sources = [in_hbm(x) for x in loads]
     outs = [jax.ShapeDtypeStruct((len(group), far, block, LANES), F32 if own else BF16) for group in GROUPS[half]]
-    scratch = [pltpu.VMEM((far * block, wide), F32)]
+    scratch = [pltpu.VMEM((NEAR, far * block, LANES), F32)]
     if loads:
         outs += half_weights(loads[0], *loads[2:4]) + [jax.ShapeDtypeStruct(x.shape, x.dtype) for x in loads[4:]]
         scratch.append(pltpu.SemaphoreType.DMA((6 + len(loads[4:]),)))
@@ -769,7 +771,8 @@
     ends_0, got_0 = far_sum(0, kept_1, kept_0, got_0)
     *grads, mark = input_gradients((0, 1), ends_0, [])
     ends_0, got_0 = far_end(0, mark, ends_0, got_0)
-    kept_1, got_1 = near_sum(1, ends_0, kept_1, got_1)
+    (part,) = added("near_part_1", ends_0, got_1[2], [got_1[1]], [(far, F32)])
+    kept_1, got_1 = near_sum(1, part, kept_1, [part, got_1[0]])
     ends_0, got_0 = far_join(0, kept_1, ends_0, got_0)
     ends_1, got_1 = far_sum(1, ends_0, kept_1, got_1)
     output, skip_out, mark = outputs(

time: 86.2 us -> 85.6 us (level)
  starting transfers between devices: 40.4 us -> 38.5 us
  waiting for transfers between devices: 4.58 us -> 6.39 us
    ppermute x25, starting transfers between devices: 34.7 us -> 32 us  [swapped(): lax.ppermute(x, axis, [(i, i ^ k) for i in range(lax.axis_size(axis))])]
    ppermute x25, waiting for transfers between devices: 4.58 us -> 6.39 us  [swapped(): lax.ppermute(x, axis, [(i, i ^ k) for i in range(lax.axis_size(axis))])]
where the time goes in v3:
time: 85.6 us; the launch traced here: 85.4 us
  starting transfers between devices  38.5 us (45%)
  Pallas kernels  38.5 us (45%)
  waiting for transfers between devices  6.39 us (7%)
  between operations  1.04 us (1%)
  local copies, waits for them, and re-layouts  0.97 us (1%)
    ppermute x25, starting transfers between devices, swapped(): lax.ppermute(x, axis, [(i, i ^ k) for i in range(lax.axis_size(axis))])  32 us
    pallas_call x4, Pallas kernels, gradients(): call(functools.partial(gradients_body, far, block, half, own, count, len(...  8.67 us
    pallas_call x1, Pallas kernels, load(): call(load_body, 'load', [ANYWHERE] * len(sources), [VMEM] * len(shapes),...  7.83 us
    pallas_call x2, Pallas kernels, inputs(): call(functools.partial(inputs_body, steps, counts), f'inputs_{steps[0]}',...  7.72 us
    ppermute x2, starting transfers between devices, passed_along(): return lax.ppermute(x, AXES, pairs)  6.5 us
    ppermute x25, waiting for transfers between devices, swapped(): lax.ppermute(x, axis, [(i, i ^ k) for i in range(lax.axis_size(axis))])  6.39 us
    pallas_call x1, Pallas kernels, forward_1(): call(forward_body, 'forward_1', [ANYWHERE] + [VMEM] * len(args), [VMEM] *...  4.56 us
    pallas_call x2, Pallas kernels, unpack(): call(functools.partial(unpack_body, far, block), f'unpack_{half}', [ANYWH...  4 us
  transfers between devices with their start and end apart: 27, of which 6 were waited for; matrix products, arithmetic and copies ran while one was open for 0% of the time, Pallas kernels for 39%

profile of v3, /device:TPU:3, one launch (start us, length us, event | category | flops | bytes accessed | tf_op | source)
XLA Modules:
  0.0 85.4 jit_solution(5278972520408013767)
XLA Ops:
  1.6 3.1 %collective-permute-start = (bf16[256,512]{1,0:T(8,128)(2,1)S(1)}, bf16[256,512]{1,0:T(8,128)(2,1)S(1)}, u32[]{:S(2)}, u32[]{:S(2)}) collective-permute-start(bf16[256,512]{1,0:T(8,128)(2,1)S(1)} %slice.3), channel_id=1, source_target_pairs={{0,1},{1,2},{2,3},{3,4},{4,5},{5,6},{6,7},{7,8},{8,9},{9,10},{10,1... | collective-permute-start | bytes 786440 | tf_op jit(solution)/shard_map/ppermute | solution.py:670
  4.7 7.8 %load.1 = (s32[16,128]{1,0:T(8,128)S(1)}, s32[16,128]{1,0:T(8,128)S(1)}, f32[1,1024]{1,0:T(1,128)S(1)}, bf16[80,1024]{1,0:T(8,128)(2,1)S(1)}, bf16[1024,512]{1,0...) custom-call(s32[16,128]{1,0:T(8,128)} %bitcast.50, ...), custom_call_target="tpu_custom_call" | custom-call | flops 8000000000 | bytes 1 | tf_op jit(solution)/shard_map/load/pallas_call | solution.py:253
  13.4 2.1 %theirs_0.1 = (bf16[2,4,208,128]{3,2,1,0:T(8,128)(2,1)S(1)}, bf16[2,4,208,128]{3,2,1,0:T(8,128)(2,1)S(1)}, bf16[1024,512]{1,0:T(8,128)(2,1)S(1)}, bf16[256,512]{...) custom-call(bf16[512,256]{1,0:T(8,128)(2,1)S(1)} %get-tuple-element.93.token.past_he, ...), custom_call_target="tpu_custom_call" | custom-call | flops 1 | bytes 1 | tf_op jit(solution)/shard_map/theirs_0/pallas_call | solution.py:429
  15.5 1.0 %collective-permute-start.1 = (bf16[2,4,208,128]{3,2,1,0:T(8,128)(2,1)S(1)}, bf16[2,4,208,128]{3,2,1,0:T(8,128)(2,1)S(1)}, u32[]{:S(2)}, u32[]{:S(2)}) collective-permute-start(bf16[2,4,208,128]{3,2,1,0:T(8,128)(2,1)S(1)} %get-tuple-element.98.token), channel_id=1, source_target_pairs={{0,16},{16,0},{1,17},{17,1},{2,18},{18,2},{3,19},{19,3},{4,20},{20... | collective-permute-start | bytes 1277960 | tf_op jit(solution)/shard_map/ppermute | solution.py:594
  16.7 2.2 %mine_0.1 = (f32[2,4,208,128]{3,2,1,0:T(8,128)S(1)}, f32[2,4,208,128]{3,2,1,0:T(8,128)S(1)}) custom-call(bf16[2,4,208,128]{3,2,1,0:T(8,128)(2,1)S(1)} %get-tuple-element.98.token, s32[16,128]{1,0:T(8,128)S(1)} %get-tuple-element.83.valid, bf16[1120,2048]{1,0:T(8,128)(2,1)S(1)} %get-tuple-element.85.x_turned, bf16[2048,512]{1,0:T(8,128)(2,1)S(1)} %get-tuple-element.86.gout, ...), custom_call_target="tpu_custom_call" | custom-call | flops 1 | bytes 1 | tf_op jit(solution)/shard_map/mine_0/pallas_call | solution.py:429
  19.0 1.3 %collective-permute-start.3 = (bf16[4,208,128]{2,1,0:T(8,128)(2,1)S(1)}, bf16[4,208,128]{2,1,0:T(8,128)(2,1)S(1)}, u32[]{:S(2)}, u32[]{:S(2)}) collective-permute-start(bf16[4,208,128]{2,1,0:T(8,128)(2,1)S(1)} %bitcast.34), channel_id=1, source_target_pairs={{0,3},{1,2},{2,1},{3,0},{4,7},{5,6},{6,5},{7,4},{8,11},{9,10},{10,... | collective-permute-start | bytes 638984 | tf_op jit(solution)/shard_map/ppermute | solution.py:594
  20.3 1.2 %collective-permute-start.4 = (bf16[4,208,128]{2,1,0:T(8,128)(2,1)S(1)}, bf16[4,208,128]{2,1,0:T(8,128)(2,1)S(1)}, u32[]{:S(2)}, u32[]{:S(2)}) collective-permute-start(bf16[4,208,128]{2,1,0:T(8,128)(2,1)S(1)} %bitcast.39), channel_id=1, source_target_pairs={{0,1},{1,0},{2,3},{3,2},{4,5},{5,4},{6,7},{7,6},{8,9},{9,8},{10,11... | collective-permute-start | bytes 638984 | tf_op jit(solution)/shard_map/ppermute | solution.py:594
  21.9 4.6 %forward_1.1 = (bf16[256,256]{1,0:T(8,128)(2,1)S(1)}, bf16[256,256]{1,0:T(8,128)(2,1)S(1)}, bf16[256,512]{1,0:T(8,128)(2,1)S(1)}, bf16[1792,256]{1,0:T(8,128)(2,...) custom-call(f32[4,208,128]{2,1,0:T(8,128)S(1)} %bitcast.27, ...), custom_call_target="tpu_custom_call" | custom-call | flops 1 | bytes 1 | tf_op jit(solution)/shard_map/forward_1/pallas_call | solution.py:326
  26.4 2.0 %theirs_1.1.token = bf16[4,4,208,128]{3,2,1,0:T(8,128)(2,1)S(1)} custom-call(f32[4,208,128]{2,1,0:T(8,128)S(1)} %bitcast.28, s32[16,128]{1,0:T(8,128)S(1)} %get-tuple-element.83.valid, bf16[1120,2048]{1,0:T(8,128)(2,1)S(1)} %get-tuple-element.85.x_turned, bf16[2048,512]{1,0:T(8,128)(2,1)S(1)} %get-tuple-element.86.gout, ...), custom_call_target="tpu_custom_call" | custom-call | flops 1 | bytes 1 | tf_op jit(solution)/shard_map/theirs_1/pallas_call | solution.py:429
  28.5 1.3 %collective-permute-start.6 = (bf16[4,4,208,128]{3,2,1,0:T(8,128)(2,1)S(1)}, bf16[4,4,208,128]{3,2,1,0:T(8,128)(2,1)S(1)}, u32[]{:S(2)}, u32[]{:S(2)}) collective-permute-start(bf16[4,4,208,128]{3,2,1,0:T(8,128)(2,1)S(1)} %theirs_1.1.token), channel_id=1, source_target_pairs={{0,16},{16,0},{1,17},{17,1},{2,18},{18,2},{3,19},{19,3},{4,20},{20... | collective-permute-start | bytes 2555912 | tf_op jit(solution)/shard_map/ppermute | solution.py:594
  29.8 2.3 %mine_1.1.token.refs_0_ = f32[4,4,208,128]{3,2,1,0:T(8,128)S(1)} custom-call(bf16[4,4,208,128]{3,2,1,0:T(8,128)(2,1)S(1)} %theirs_1.1.token, s32[16,128]{1,0:T(8,128)S(1)} %get-tuple-element.83.valid, bf16[1120,2048]{1,0:T(8,128)(2,1)S(1)} %get-tuple-element.85.x_turned, bf16[2048,512]{1,0:T(8,128)(2,1)S(1)} %get-tuple-element.86.gout, ...), custom_call_target="tpu_custom_call" | custom-call | flops 2000000000 | bytes 1 | tf_op jit(solution)/shard_map/mine_1/pallas_call | solution.py:429
  32.3 1.4 %collective-permute-start.7 = (bf16[2,208,128]{2,1,0:T(8,128)(2,1)S(1)}, bf16[2,208,128]{2,1,0:T(8,128)(2,1)S(1)}, u32[]{:S(2)}, u32[]{:S(2)}) collective-permute-start(bf16[2,208,128]{2,1,0:T(8,128)(2,1)S(1)} %get-tuple-element.116), channel_id=1, source_target_pairs={{0,4},{4,0},{8,12},{12,8},{1,5},{5,1},{9,13},{13,9},{2,6},{6,2},{1... | collective-permute-start | bytes 319496 | tf_op jit(solution)/shard_map/ppermute | solution.py:594
  33.8 1.3 %collective-permute-start.9 = (bf16[4,208,128]{2,1,0:T(8,128)(2,1)S(1)}, bf16[4,208,128]{2,1,0:T(8,128)(2,1)S(1)}, u32[]{:S(2)}, u32[]{:S(2)}) collective-permute-start(bf16[4,208,128]{2,1,0:T(8,128)(2,1)S(1)} %bitcast.43), channel_id=1, source_target_pairs={{0,3},{1,2},{2,1},{3,0},{4,7},{5,6},{6,5},{7,4},{8,11},{9,10},{10,... | collective-permute-start | bytes 638984 | tf_op jit(solution)/shard_map/ppermute | solution.py:594
  35.8 1.0 %collective-permute-done.7.refs_1_ = bf16[2,208,128]{2,1,0:T(8,128)(2,1)S(1)} collective-permute-done((bf16[2,208,128]{2,1,0:T(8,128)(2,1)S(1)}, bf16[2,208,128]{2,1,0:T(8,128)(2,1)S(1)}, u32[]{:S(2)}, u32[]{:S(2)}) %collective-permute-start.7) | collective-permute-done | bytes 106528 | tf_op jit(solution)/shard_map/ppermute | solution.py:594
  36.8 2.4 %collective-permute-start.8 = (bf16[2,208,128]{2,1,0:T(8,128)(2,1)S(1)}, bf16[2,208,128]{2,1,0:T(8,128)(2,1)S(1)}, u32[]{:S(2)}, u32[]{:S(2)}) collective-permute-start(bf16[2,208,128]{2,1,0:T(8,128)(2,1)S(1)} %far_sum_0.1.token.mine), channel_id=1, source_target_pairs={{0,8},{4,12},{8,0},{12,4},{1,9},{5,13},{9,1},{13,5},{2,10},{6,14},... | collective-permute-start | bytes 319496 | tf_op jit(solution)/shard_map/ppermute | solution.py:594
  40.1 3.9 %inputs_0.1 = (f32[2048,512]{1,0:T(8,128)}, f32[80,2048]{1,0:T(8,128)}, f32[8,128]{1,0:T(8,128)S(1)}) custom-call(bf16[2,208,128]{2,1,0:T(8,128)(2,1)S(1)} %far_sum_0.1.token.mine, bf16[256,256]{1,0:T(8,128)(2,1)S(1)} %get-tuple-element.117.received.refs_0_, bf16[2048,512]{1,0:T(8,128)(2,1)S(1)} %get-tuple-element.86.gout, ...), custom_call_target="tpu_custom_call" | custom-call | flops 1 | bytes 1 | tf_op jit(solution)/shard_map/inputs_0/pallas_call | solution.py:519
  44.0 1.4 %collective-permute-start.12 = (bf16[2,208,128]{2,1,0:T(8,128)(2,1)S(1)}, bf16[2,208,128]{2,1,0:T(8,128)(2,1)S(1)}, u32[]{:S(2)}, u32[]{:S(2)}) collective-permute-start(bf16[2,208,128]{2,1,0:T(8,128)(2,1)S(1)} %far_end_0.1.token.refs_0_), channel_id=1, source_target_pairs={{0,4},{4,0},{8,12},{12,8},{1,5},{5,1},{9,13},{13,9},{2,6},{6,2},{1... | collective-permute-start | bytes 319496 | tf_op jit(solution)/shard_map/ppermute | solution.py:594
  45.4 1.1 %collective-permute-done.10.refs_1_ = bf16[4,208,128]{2,1,0:T(8,128)(2,1)S(1)} collective-permute-done((bf16[4,208,128]{2,1,0:T(8,128)(2,1)S(1)}, bf16[4,208,128]{2,1,0:T(8,128)(2,1)S(1)}, u32[]{:S(2)}, u32[]{:S(2)}) %collective-permute-start.10) | collective-permute-done | bytes 213024 | tf_op jit(solution)/shard_map/ppermute | solution.py:594
  47.7 1.8 %collective-permute-start.15 = (bf16[4,208,128]{2,1,0:T(8,128)(2,1)S(1)}, bf16[4,208,128]{2,1,0:T(8,128)(2,1)S(1)}, u32[]{:S(2)}, u32[]{:S(2)}) collective-permute-start(bf16[4,208,128]{2,1,0:T(8,128)(2,1)S(1)} %far_join_0.1.token), channel_id=1, source_target_pairs={{0,3},{1,2},{2,1},{3,0},{4,7},{5,6},{6,5},{7,4},{8,11},{9,10},{10,... | collective-permute-start | bytes 638984 | tf_op jit(solution)/shard_map/ppermute | solution.py:594
  50.4 1.1 %collective-permute-done.13.refs_1_ = bf16[2,208,128]{2,1,0:T(8,128)(2,1)S(1)} collective-permute-done((bf16[2,208,128]{2,1,0:T(8,128)(2,1)S(1)}, bf16[2,208,128]{2,1,0:T(8,128)(2,1)S(1)}, u32[]{:S(2)}, u32[]{:S(2)}) %collective-permute-start.13) | collective-permute-done | bytes 106528 | tf_op jit(solution)/shard_map/ppermute | solution.py:594
  51.5 2.3 %collective-permute-start.14 = (bf16[2,208,128]{2,1,0:T(8,128)(2,1)S(1)}, bf16[2,208,128]{2,1,0:T(8,128)(2,1)S(1)}, u32[]{:S(2)}, u32[]{:S(2)}) collective-permute-start(bf16[2,208,128]{2,1,0:T(8,128)(2,1)S(1)} %far_sum_1.1.token.mine), channel_id=1, source_target_pairs={{0,8},{4,12},{8,0},{12,4},{1,9},{5,13},{9,1},{13,5},{2,10},{6,14},... | collective-permute-start | bytes 319496 | tf_op jit(solution)/shard_map/ppermute | solution.py:594
  53.8 3.6 %outputs.1 = (bf16[2048,512]{1,0:T(8,128)(2,1)}, bf16[2048,512]{1,0:T(8,128)(2,1)}, f32[8,128]{1,0:T(8,128)S(1)}) custom-call(bf16[2,208,128]{2,1,0:T(8,128)(2,1)S(1)} %far_sum_1.1.token.mine, s32[16,128]{1,0:T(8,128)S(1)} %get-tuple-element.83.valid, bf16[2048,512]{1,0:T(8,128)(2,1)S(1)} %get-tuple-element.84.sig, ...), custom_call_target="tpu_custom_call" | custom-call | flops 1 | bytes 1 | tf_op jit(solution)/shard_map/outputs/pallas_call | solution.py:462
  57.5 1.0 %collective-permute-start.18 = (bf16[2,208,128]{2,1,0:T(8,128)(2,1)S(1)}, bf16[2,208,128]{2,1,0:T(8,128)(2,1)S(1)}, u32[]{:S(2)}, u32[]{:S(2)}) collective-permute-start(bf16[2,208,128]{2,1,0:T(8,128)(2,1)S(1)} %far_end_1.1.token.refs_0_), channel_id=1, source_target_pairs={{0,4},{4,0},{8,12},{12,8},{1,5},{5,1},{9,13},{13,9},{2,6},{6,2},{1... | collective-permute-start | bytes 319496 | tf_op jit(solution)/shard_map/ppermute | solution.py:594
  59.0 3.4 %collective-permute-start.19 = (bf16[256,512]{1,0:T(8,128)(2,1)S(1)}, bf16[256,512]{1,0:T(8,128)(2,1)S(1)}, u32[]{:S(2)}, u32[]{:S(2)}) collective-permute-start(bf16[256,512]{1,0:T(8,128)(2,1)S(1)} %early.1.token), channel_id=1, source_target_pairs={{1,0},{2,1},{3,2},{4,3},{5,4},{6,5},{7,6},{8,7},{9,8},{10,9},{11,1... | collective-permute-start | bytes 786440 | tf_op jit(solution)/shard_map/ppermute | solution.py:670
  63.5 5.3 %collective-permute-start.25 = (bf16[4,208,128]{2,1,0:T(8,128)(2,1)S(1)}, bf16[4,208,128]{2,1,0:T(8,128)(2,1)S(1)}, u32[]{:S(2)}, u32[]{:S(2)}) collective-permute-start(bf16[4,208,128]{2,1,0:T(8,128)(2,1)S(1)} %far_join_1.1.token), channel_id=1, source_target_pairs={{0,2},{1,3},{2,0},{3,1},{4,6},{5,7},{6,4},{7,5},{8,10},{9,11},{10,... | collective-permute-start | bytes 638984 | tf_op jit(solution)/shard_map/ppermute | solution.py:594
  68.8 1.3 %collective-permute-start.23 = (bf16[2,4,208,128]{3,2,1,0:T(8,128)(2,1)S(1)}, bf16[2,4,208,128]{3,2,1,0:T(8,128)(2,1)S(1)}, u32[]{:S(2)}, u32[]{:S(2)}) collective-permute-start(bf16[2,4,208,128]{3,2,1,0:T(8,128)(2,1)S(1)} %near_join_0_1.1.token.refs_1_), channel_id=1, source_target_pairs={{0,16},{16,0},{1,17},{17,1},{2,18},{18,2},{3,19},{19,3},{4,20},{20... | collective-permute-start | bytes 1277960 | tf_op jit(solution)/shard_map/ppermute | solution.py:594
  70.1 3.8 %collective-permute-start.22 = (bf16[2,4,208,128]{3,2,1,0:T(8,128)(2,1)S(1)}, bf16[2,4,208,128]{3,2,1,0:T(8,128)(2,1)S(1)}, u32[]{:S(2)}, u32[]{:S(2)}) collective-permute-start(bf16[2,4,208,128]{3,2,1,0:T(8,128)(2,1)S(1)} %near_join_0_0.1.token.refs_0_), channel_id=1, source_target_pairs={{0,16},{16,0},{1,17},{17,1},{2,18},{18,2},{3,19},{19,3},{4,20},{20... | collective-permute-start | bytes 1277960 | tf_op jit(solution)/shard_map/ppermute | solution.py:594
  73.9 3.8 %inputs_2.1 = (f32[2048,512]{1,0:T(8,128)}, f32[80,2048]{1,0:T(8,128)}, f32[8,128]{1,0:T(8,128)S(1)}) custom-call(bf16[4,208,128]{2,1,0:T(8,128)(2,1)S(1)} %far_join_1.1.token, bf16[256,512]{1,0:T(8,128)(2,1)S(1)} %collective-permute-done.19.received, bf16[2048,512]{1,0:T(8,128)(2,1)S(1)} %get-tuple-element.86.gout, ...), custom_call_target="tpu_custom_call", output_to_operand_aliasing={{0}: (11, {}), {1}: (12, {})} | custom-call | flops 1 | bytes 1 | tf_op jit(solution)/shard_map/inputs_2/pallas_call | solution.py:519
  77.8 1.9 %collective-permute-done.25 = bf16[4,208,128]{2,1,0:T(8,128)(2,1)S(1)} collective-permute-done((bf16[4,208,128]{2,1,0:T(8,128)(2,1)S(1)}, bf16[4,208,128]{2,1,0:T(8,128)(2,1)S(1)}, u32[]{:S(2)}, u32[]{:S(2)}) %collective-permute-start.25) | collective-permute-done | bytes 213024 | tf_op jit(solution)/shard_map/ppermute | solution.py:594
  80.2 1.2 %collective-permute-start.26 = (bf16[2,4,208,128]{3,2,1,0:T(8,128)(2,1)S(1)}, bf16[2,4,208,128]{3,2,1,0:T(8,128)(2,1)S(1)}, u32[]{:S(2)}, u32[]{:S(2)}) collective-permute-start(bf16[2,4,208,128]{3,2,1,0:T(8,128)(2,1)S(1)} %near_join_1_1.1.refs_1_), channel_id=1, source_target_pairs={{0,16},{16,0},{1,17},{17,1},{2,18},{18,2},{3,19},{19,3},{4,20},{20... | collective-permute-start | bytes 1277960 | tf_op jit(solution)/shard_map/ppermute | solution.py:594
  81.3 2.0 %unpack_0.1 = (f32[512,1024]{1,0:T(8,128)}, f32[512,1024]{1,0:T(8,128)}, f32[80,1024]{1,0:T(8,128)}, f32[1,1024]{1,0:T(1,128)}, f32[512,512]{1,0:T(8,128)}, /*in...) custom-call(bf16[2,4,208,128]{3,2,1,0:T(8,128)(2,1)S(1)} %collective-permute-done.21.token.refs_2_, ...), custom_call_target="tpu_custom_call" | custom-call | flops 1 | bytes 1 | tf_op jit(solution)/shard_map/unpack_0/pallas_call | solution.py:581
  83.3 2.0 %unpack_1.1 = (f32[512,1024]{1,0:T(8,128)}, f32[512,1024]{1,0:T(8,128)}, f32[80,1024]{1,0:T(8,128)}, f32[1,1024]{1,0:T(1,128)}, f32[512,512]{1,0:T(8,128)}, /*in...) custom-call(f32[8,128]{1,0:T(8,128)S(1)} %get-tuple-element.137.toke, ...), custom_call_target="tpu_custom_call", output_to_operand_aliasing={{0}: (5, {}), {1}: (6, {}), {2}: (7, {}), {3}: (8, {}), {4}... | custom-call | flops 1 | bytes 1 | tf_op jit(solution)/shard_map/unpack_1/pallas_call | solution.py:581
  (53 shorter events, 8.5 us)
Async XLA Ops:
  1.6 11.0 %collective-permute-start = (bf16[256,512]{1,0:T(8,128)(2,1)S(1)}, bf16[256,512]{1,0:T(8,128)(2,1)S(1)}, u32[]{:S(2)}, u32[]{:S(2)}) collective-permute-start(bf16[256,512]{1,0:T(8,128)(2,1)S(1)} %slice.3), channel_id=1, source_target_pairs={{0,1},{1,2},{2,3},{3,4},{4,5},{5,6},{6,7},{7,8},{8,9},{9,10},{10,1... | collective-permute-start | bytes 786440 | tf_op jit(solution)/shard_map/ppermute | solution.py:670
  15.5 3.4 %collective-permute-start.1 = (bf16[2,4,208,128]{3,2,1,0:T(8,128)(2,1)S(1)}, bf16[2,4,208,128]{3,2,1,0:T(8,128)(2,1)S(1)}, u32[]{:S(2)}, u32[]{:S(2)}) collective-permute-start(bf16[2,4,208,128]{3,2,1,0:T(8,128)(2,1)S(1)} %get-tuple-element.98.token), channel_id=1, source_target_pairs={{0,16},{16,0},{1,17},{17,1},{2,18},{18,2},{3,19},{19,3},{4,20},{20... | collective-permute-start | bytes 1277960 | tf_op jit(solution)/shard_map/ppermute | solution.py:594
  16.6 4.9 %collective-permute-start.2 = (bf16[2,4,208,128]{3,2,1,0:T(8,128)(2,1)S(1)}, bf16[2,4,208,128]{3,2,1,0:T(8,128)(2,1)S(1)}, u32[]{:S(2)}, u32[]{:S(2)}) collective-permute-start(bf16[2,4,208,128]{3,2,1,0:T(8,128)(2,1)S(1)} %get-tuple-element.102), channel_id=1, source_target_pairs={{0,16},{16,0},{1,17},{17,1},{2,18},{18,2},{3,19},{19,3},{4,20},{20... | collective-permute-start | bytes 1277960 | tf_op jit(solution)/shard_map/ppermute | solution.py:594
  19.0 13.1 %collective-permute-start.3 = (bf16[4,208,128]{2,1,0:T(8,128)(2,1)S(1)}, bf16[4,208,128]{2,1,0:T(8,128)(2,1)S(1)}, u32[]{:S(2)}, u32[]{:S(2)}) collective-permute-start(bf16[4,208,128]{2,1,0:T(8,128)(2,1)S(1)} %bitcast.34), channel_id=1, source_target_pairs={{0,3},{1,2},{2,1},{3,0},{4,7},{5,6},{6,5},{7,4},{8,11},{9,10},{10,... | collective-permute-start | bytes 638984 | tf_op jit(solution)/shard_map/ppermute | solution.py:594
  20.3 11.8 %collective-permute-start.4 = (bf16[4,208,128]{2,1,0:T(8,128)(2,1)S(1)}, bf16[4,208,128]{2,1,0:T(8,128)(2,1)S(1)}, u32[]{:S(2)}, u32[]{:S(2)}) collective-permute-start(bf16[4,208,128]{2,1,0:T(8,128)(2,1)S(1)} %bitcast.39), channel_id=1, source_target_pairs={{0,1},{1,0},{2,3},{3,2},{4,5},{5,4},{6,7},{7,6},{8,9},{9,8},{10,11... | collective-permute-start | bytes 638984 | tf_op jit(solution)/shard_map/ppermute | solution.py:594
  21.6 10.6 %collective-permute-start.5 = (bf16[4,208,128]{2,1,0:T(8,128)(2,1)S(1)}, bf16[4,208,128]{2,1,0:T(8,128)(2,1)S(1)}, u32[]{:S(2)}, u32[]{:S(2)}) collective-permute-start(bf16[4,208,128]{2,1,0:T(8,128)(2,1)S(1)} %bitcast.44), channel_id=1, source_target_pairs={{0,2},{1,3},{2,0},{3,1},{4,6},{5,7},{6,4},{7,5},{8,10},{9,11},{10,... | collective-permute-start | bytes 638984 | tf_op jit(solution)/shard_map/ppermute | solution.py:594
  28.5 5.2 %collective-permute-start.6 = (bf16[4,4,208,128]{3,2,1,0:T(8,128)(2,1)S(1)}, bf16[4,4,208,128]{3,2,1,0:T(8,128)(2,1)S(1)}, u32[]{:S(2)}, u32[]{:S(2)}) collective-permute-start(bf16[4,4,208,128]{3,2,1,0:T(8,128)(2,1)S(1)} %theirs_1.1.token), channel_id=1, source_target_pairs={{0,16},{16,0},{1,17},{17,1},{2,18},{18,2},{3,19},{19,3},{4,20},{20... | collective-permute-start | bytes 2555912 | tf_op jit(solution)/shard_map/ppermute | solution.py:594
  32.3 4.5 %collective-permute-start.7 = (bf16[2,208,128]{2,1,0:T(8,128)(2,1)S(1)}, bf16[2,208,128]{2,1,0:T(8,128)(2,1)S(1)}, u32[]{:S(2)}, u32[]{:S(2)}) collective-permute-start(bf16[2,208,128]{2,1,0:T(8,128)(2,1)S(1)} %get-tuple-element.116), channel_id=1, source_target_pairs={{0,4},{4,0},{8,12},{12,8},{1,5},{5,1},{9,13},{13,9},{2,6},{6,2},{1... | collective-permute-start | bytes 319496 | tf_op jit(solution)/shard_map/ppermute | solution.py:594
  33.8 11.6 %collective-permute-start.9 = (bf16[4,208,128]{2,1,0:T(8,128)(2,1)S(1)}, bf16[4,208,128]{2,1,0:T(8,128)(2,1)S(1)}, u32[]{:S(2)}, u32[]{:S(2)}) collective-permute-start(bf16[4,208,128]{2,1,0:T(8,128)(2,1)S(1)} %bitcast.43), channel_id=1, source_target_pairs={{0,3},{1,2},{2,1},{3,0},{4,7},{5,6},{6,5},{7,4},{8,11},{9,10},{10,... | collective-permute-start | bytes 638984 | tf_op jit(solution)/shard_map/ppermute | solution.py:594
  35.0 11.4 %collective-permute-start.10 = (bf16[4,208,128]{2,1,0:T(8,128)(2,1)S(1)}, bf16[4,208,128]{2,1,0:T(8,128)(2,1)S(1)}, u32[]{:S(2)}, u32[]{:S(2)}) collective-permute-start(bf16[4,208,128]{2,1,0:T(8,128)(2,1)S(1)} %bitcast.41), channel_id=1, source_target_pairs={{0,2},{1,3},{2,0},{3,1},{4,6},{5,7},{6,4},{7,5},{8,10},{9,11},{10,... | collective-permute-start | bytes 638984 | tf_op jit(solution)/shard_map/ppermute | solution.py:594
  36.8 7.2 %collective-permute-start.8 = (bf16[2,208,128]{2,1,0:T(8,128)(2,1)S(1)}, bf16[2,208,128]{2,1,0:T(8,128)(2,1)S(1)}, u32[]{:S(2)}, u32[]{:S(2)}) collective-permute-start(bf16[2,208,128]{2,1,0:T(8,128)(2,1)S(1)} %far_sum_0.1.token.mine), channel_id=1, source_target_pairs={{0,8},{4,12},{8,0},{12,4},{1,9},{5,13},{9,1},{13,5},{2,10},{6,14},... | collective-permute-start | bytes 319496 | tf_op jit(solution)/shard_map/ppermute | solution.py:594
  39.2 7.4 %collective-permute-start.11 = (bf16[4,208,128]{2,1,0:T(8,128)(2,1)S(1)}, bf16[4,208,128]{2,1,0:T(8,128)(2,1)S(1)}, u32[]{:S(2)}, u32[]{:S(2)}) collective-permute-start(bf16[4,208,128]{2,1,0:T(8,128)(2,1)S(1)} %bitcast.38), channel_id=1, source_target_pairs={{0,1},{1,0},{2,3},{3,2},{4,5},{5,4},{6,7},{7,6},{8,9},{9,8},{10,11... | collective-permute-start | bytes 638984 | tf_op jit(solution)/shard_map/ppermute | solution.py:594
  44.0 3.6 %collective-permute-start.12 = (bf16[2,208,128]{2,1,0:T(8,128)(2,1)S(1)}, bf16[2,208,128]{2,1,0:T(8,128)(2,1)S(1)}, u32[]{:S(2)}, u32[]{:S(2)}) collective-permute-start(bf16[2,208,128]{2,1,0:T(8,128)(2,1)S(1)} %far_end_0.1.token.refs_0_), channel_id=1, source_target_pairs={{0,4},{4,0},{8,12},{12,8},{1,5},{5,1},{9,13},{13,9},{2,6},{6,2},{1... | collective-permute-start | bytes 319496 | tf_op jit(solution)/shard_map/ppermute | solution.py:594
  46.6 4.9 %collective-permute-start.13 = (bf16[2,208,128]{2,1,0:T(8,128)(2,1)S(1)}, bf16[2,208,128]{2,1,0:T(8,128)(2,1)S(1)}, u32[]{:S(2)}, u32[]{:S(2)}) collective-permute-start(bf16[2,208,128]{2,1,0:T(8,128)(2,1)S(1)} %get-tuple-element.123), channel_id=1, source_target_pairs={{0,4},{4,0},{8,12},{12,8},{1,5},{5,1},{9,13},{13,9},{2,6},{6,2},{1... | collective-permute-start | bytes 319496 | tf_op jit(solution)/shard_map/ppermute | solution.py:594
  47.7 14.7 %collective-permute-start.15 = (bf16[4,208,128]{2,1,0:T(8,128)(2,1)S(1)}, bf16[4,208,128]{2,1,0:T(8,128)(2,1)S(1)}, u32[]{:S(2)}, u32[]{:S(2)}) collective-permute-start(bf16[4,208,128]{2,1,0:T(8,128)(2,1)S(1)} %far_join_0.1.token), channel_id=1, source_target_pairs={{0,3},{1,2},{2,1},{3,0},{4,7},{5,6},{6,5},{7,4},{8,11},{9,10},{10,... | collective-permute-start | bytes 638984 | tf_op jit(solution)/shard_map/ppermute | solution.py:594
  49.4 13.0 %collective-permute-start.17 = (bf16[4,208,128]{2,1,0:T(8,128)(2,1)S(1)}, bf16[4,208,128]{2,1,0:T(8,128)(2,1)S(1)}, u32[]{:S(2)}, u32[]{:S(2)}) collective-permute-start(bf16[4,208,128]{2,1,0:T(8,128)(2,1)S(1)} %far_join_0.1.token), channel_id=1, source_target_pairs={{0,2},{1,3},{2,0},{3,1},{4,6},{5,7},{6,4},{7,5},{8,10},{9,11},{10,... | collective-permute-start | bytes 638984 | tf_op jit(solution)/shard_map/ppermute | solution.py:594
  49.6 12.8 %collective-permute-start.16 = (bf16[4,208,128]{2,1,0:T(8,128)(2,1)S(1)}, bf16[4,208,128]{2,1,0:T(8,128)(2,1)S(1)}, u32[]{:S(2)}, u32[]{:S(2)}) collective-permute-start(bf16[4,208,128]{2,1,0:T(8,128)(2,1)S(1)} %far_join_0.1.token), channel_id=1, source_target_pairs={{0,1},{1,0},{2,3},{3,2},{4,5},{5,4},{6,7},{7,6},{8,9},{9,8},{10,11... | collective-permute-start | bytes 638984 | tf_op jit(solution)/shard_map/ppermute | solution.py:594
  51.5 6.0 %collective-permute-start.14 = (bf16[2,208,128]{2,1,0:T(8,128)(2,1)S(1)}, bf16[2,208,128]{2,1,0:T(8,128)(2,1)S(1)}, u32[]{:S(2)}, u32[]{:S(2)}) collective-permute-start(bf16[2,208,128]{2,1,0:T(8,128)(2,1)S(1)} %far_sum_1.1.token.mine), channel_id=1, source_target_pairs={{0,8},{4,12},{8,0},{12,4},{1,9},{5,13},{9,1},{13,5},{2,10},{6,14},... | collective-permute-start | bytes 319496 | tf_op jit(solution)/shard_map/ppermute | solution.py:594
  57.5 4.9 %collective-permute-start.18 = (bf16[2,208,128]{2,1,0:T(8,128)(2,1)S(1)}, bf16[2,208,128]{2,1,0:T(8,128)(2,1)S(1)}, u32[]{:S(2)}, u32[]{:S(2)}) collective-permute-start(bf16[2,208,128]{2,1,0:T(8,128)(2,1)S(1)} %far_end_1.1.token.refs_0_), channel_id=1, source_target_pairs={{0,4},{4,0},{8,12},{12,8},{1,5},{5,1},{9,13},{13,9},{2,6},{6,2},{1... | collective-permute-start | bytes 319496 | tf_op jit(solution)/shard_map/ppermute | solution.py:594
  59.0 11.1 %collective-permute-start.19 = (bf16[256,512]{1,0:T(8,128)(2,1)S(1)}, bf16[256,512]{1,0:T(8,128)(2,1)S(1)}, u32[]{:S(2)}, u32[]{:S(2)}) collective-permute-start(bf16[256,512]{1,0:T(8,128)(2,1)S(1)} %early.1.token), channel_id=1, source_target_pairs={{1,0},{2,1},{3,2},{4,3},{5,4},{6,5},{7,6},{8,7},{9,8},{10,9},{11,1... | collective-permute-start | bytes 786440 | tf_op jit(solution)/shard_map/ppermute | solution.py:670
  62.5 15.2 %collective-permute-start.20 = (bf16[4,208,128]{2,1,0:T(8,128)(2,1)S(1)}, bf16[4,208,128]{2,1,0:T(8,128)(2,1)S(1)}, u32[]{:S(2)}, u32[]{:S(2)}) collective-permute-start(bf16[4,208,128]{2,1,0:T(8,128)(2,1)S(1)} %far_join_1.1.token), channel_id=1, source_target_pairs={{0,3},{1,2},{2,1},{3,0},{4,7},{5,6},{6,5},{7,4},{8,11},{9,10},{10,... | collective-permute-start | bytes 638984 | tf_op jit(solution)/shard_map/ppermute | solution.py:594
  63.5 16.3 %collective-permute-start.25 = (bf16[4,208,128]{2,1,0:T(8,128)(2,1)S(1)}, bf16[4,208,128]{2,1,0:T(8,128)(2,1)S(1)}, u32[]{:S(2)}, u32[]{:S(2)}) collective-permute-start(bf16[4,208,128]{2,1,0:T(8,128)(2,1)S(1)} %far_join_1.1.token), channel_id=1, source_target_pairs={{0,2},{1,3},{2,0},{3,1},{4,6},{5,7},{6,4},{7,5},{8,10},{9,11},{10,... | collective-permute-start | bytes 638984 | tf_op jit(solution)/shard_map/ppermute | solution.py:594
  68.8 11.4 %collective-permute-start.24 = (bf16[4,208,128]{2,1,0:T(8,128)(2,1)S(1)}, bf16[4,208,128]{2,1,0:T(8,128)(2,1)S(1)}, u32[]{:S(2)}, u32[]{:S(2)}) collective-permute-start(bf16[4,208,128]{2,1,0:T(8,128)(2,1)S(1)} %far_join_1.1.token), channel_id=1, source_target_pairs={{0,1},{1,0},{2,3},{3,2},{4,5},{5,4},{6,7},{7,6},{8,9},{9,8},{10,11... | collective-permute-start | bytes 638984 | tf_op jit(solution)/shard_map/ppermute | solution.py:594
  68.8 12.5 %collective-permute-start.23 = (bf16[2,4,208,128]{3,2,1,0:T(8,128)(2,1)S(1)}, bf16[2,4,208,128]{3,2,1,0:T(8,128)(2,1)S(1)}, u32[]{:S(2)}, u32[]{:S(2)}) collective-permute-start(bf16[2,4,208,128]{3,2,1,0:T(8,128)(2,1)S(1)} %near_join_0_1.1.token.refs_1_), channel_id=1, source_target_pairs={{0,16},{16,0},{1,17},{17,1},{2,18},{18,2},{3,19},{19,3},{4,20},{20... | collective-permute-start | bytes 1277960 | tf_op jit(solution)/shard_map/ppermute | solution.py:594
  70.1 11.3 %collective-permute-start.22 = (bf16[2,4,208,128]{3,2,1,0:T(8,128)(2,1)S(1)}, bf16[2,4,208,128]{3,2,1,0:T(8,128)(2,1)S(1)}, u32[]{:S(2)}, u32[]{:S(2)}) collective-permute-start(bf16[2,4,208,128]{3,2,1,0:T(8,128)(2,1)S(1)} %near_join_0_0.1.token.refs_0_), channel_id=1, source_target_pairs={{0,16},{16,0},{1,17},{17,1},{2,18},{18,2},{3,19},{19,3},{4,20},{20... | collective-permute-start | bytes 1277960 | tf_op jit(solution)/shard_map/ppermute | solution.py:594
  77.7 3.6 %collective-permute-start.21 = (bf16[2,4,208,128]{3,2,1,0:T(8,128)(2,1)S(1)}, bf16[2,4,208,128]{3,2,1,0:T(8,128)(2,1)S(1)}, u32[]{:S(2)}, u32[]{:S(2)}) collective-permute-start(bf16[2,4,208,128]{3,2,1,0:T(8,128)(2,1)S(1)} %near_join_1_0.1.token.refs_0_), channel_id=1, source_target_pairs={{0,16},{16,0},{1,17},{17,1},{2,18},{18,2},{3,19},{19,3},{4,20},{20... | collective-permute-start | bytes 1277960 | tf_op jit(solution)/shard_map/ppermute | solution.py:594
  80.2 3.2 %collective-permute-start.26 = (bf16[2,4,208,128]{3,2,1,0:T(8,128)(2,1)S(1)}, bf16[2,4,208,128]{3,2,1,0:T(8,128)(2,1)S(1)}, u32[]{:S(2)}, u32[]{:S(2)}) collective-permute-start(bf16[2,4,208,128]{3,2,1,0:T(8,128)(2,1)S(1)} %near_join_1_1.1.refs_1_), channel_id=1, source_target_pairs={{0,16},{16,0},{1,17},{17,1},{2,18},{18,2},{3,19},{19,3},{4,20},{20... | collective-permute-start | bytes 1277960 | tf_op jit(solution)/shard_map/ppermute | solution.py:594

commit v4 on v1

--- a/solution.py
+++ b/solution.py
@@ -20,7 +20,7 @@
 MEGA = 1 << 20
 COSTS = {
     "load": 8, "head": 2, "near_sum_0": 7, "mine_1": 2,
-    "far_sum_0": 8, "near_sum_1": 4, "near_join_0_1": 2, "near_join_1_1": 4, "far_join_0": 4,
+    "far_sum_0": 8, "near_sum_1": 4, "near_join_0_0": 2, "near_join_0_1": 2, "near_join_1_1": 4, "far_join_0": 4,
 }
 FLOPS = 10**9
 
@@ -785,9 +785,7 @@
     kept_1, got_1 = near_sum(1, ends_0, kept_1, got_1)
     ends_0, got_0 = far_join(0, kept_1, ends_0, got_0)
     ends_1, got_1 = far_sum(1, ends_0, kept_1, got_1)
-    output, skip_out, mark = outputs(
-        ends_1, val, signal, [p[0] for p in made_0], [p[0] for p in made_1], outer_0, outer_1, b_res, b_skip
-    )
+    *grads, mark = input_gradients((2,), ends_1, grads)
     ends_1, got_1 = far_end(1, mark, ends_1, got_1)
     early = early_rows(ends_1, pos, head_0[2], head_1[2], w_in_0, w_in_1)
     received = passed_along(early, -1)
@@ -795,7 +793,10 @@
     second = near_join(0, 1, first[0], ends_0, got_0)
     pairs_0 = [first, second]
     ends_1, got_1 = far_join(1, second[0], ends_1, got_1)
-    *grads, mark = input_gradients((2, 3), ends_1, grads)
+    output, skip_out, mark = outputs(
+        ends_1, val, signal, [p[0] for p in made_0], [p[0] for p in made_1], outer_0, outer_1, b_res, b_skip
+    )
+    *grads, mark = input_gradients((3,), mark, grads)
     first = near_join(1, 0, mark, ends_1, got_1)
     second = near_join(1, 1, first[0], ends_1, got_1)
     pairs_1 = [first, second]

time: 85.2 us -> 83.9 us (0.985)
  starting transfers between devices: 34.6 us -> 33.3 us
  Pallas kernels: 38.4 us -> 39.3 us
    pallas_call x2 -> x3, Pallas kernels: 7.67 us -> 8.48 us  [inputs(): call(functools.partial(inputs_body, steps, counts), f'inputs_{steps[0]}',...]
  transfers between devices with their start and end apart: 26 -> 26, of which waited for: 7 -> 8; matrix products, arithmetic and copies ran while one was open for 0% -> 0% of each run, Pallas kernels for 39% -> 41%
where the time goes in v4:
time: 83.9 us; the launch traced here: 83.7 us
  Pallas kernels  39.3 us (47%)
  starting transfers between devices  33.3 us (40%)
  waiting for transfers between devices  9.06 us (11%)
  between operations  1.02 us (1%)
  local copies, waits for them, and re-layouts  0.97 us (1%)
    ppermute x24, starting transfers between devices, swapped(): lax.ppermute(x, axis, [(i, i ^ k) for i in range(lax.axis_size(axis))])  27.9 us
    ppermute x24, waiting for transfers between devices, swapped(): lax.ppermute(x, axis, [(i, i ^ k) for i in range(lax.axis_size(axis))])  9.05 us
    pallas_call x3, Pallas kernels, inputs(): call(functools.partial(inputs_body, steps, counts), f'inputs_{steps[0]}',...  8.48 us
    pallas_call x4, Pallas kernels, gradients(): call(functools.partial(gradients_body, far, block, half, own, count, len(...  8.43 us
    pallas_call x1, Pallas kernels, load(): call(load_body, 'load', [ANYWHERE] * len(sources), [VMEM] * len(shapes),...  7.87 us
    ppermute x2, starting transfers between devices, passed_along(): return lax.ppermute(x, AXES, pairs)  5.41 us
    pallas_call x2, Pallas kernels, unpack(): call(functools.partial(unpack_body, far, block), f'unpack_{half}', [ANYWH...  4 us
    pallas_call x1, Pallas kernels, outputs(): call(functools.partial(outputs_body, counts), 'outputs', [ANYWHERE] + [VM...  3.61 us
  transfers between devices with their start and end apart: 26, of which 8 were waited for; matrix products, arithmetic and copies ran while one was open for 0% of the time, Pallas kernels for 41%

profile of v4, /device:TPU:3, one launch (start us, length us, event | category | flops | bytes accessed | tf_op | source)
XLA Modules:
  0.0 83.7 jit_solution(9006001330988765309)
XLA Ops:
  0.6 1.0 %slice.3 = bf16[256,512]{1,0:T(8,128)(2,1)S(1)} slice(bf16[2048,512]{1,0:T(8,128)(2,1)} %sig.1), slice={[1792:2048], [0:512]} | slice | bytes 524288 | tf_op jit(solution)/shard_map/slice | solution.py:760
  1.6 3.1 %collective-permute-start = (bf16[256,512]{1,0:T(8,128)(2,1)S(1)}, bf16[256,512]{1,0:T(8,128)(2,1)S(1)}, u32[]{:S(2)}, u32[]{:S(2)}) collective-permute-start(bf16[256,512]{1,0:T(8,128)(2,1)S(1)} %slice.3), channel_id=1, source_target_pairs={{0,1},{1,2},{2,3},{3,4},{4,5},{5,6},{6,7},{7,8},{8,9},{9,10},{10,1... | collective-permute-start | bytes 786440 | tf_op jit(solution)/shard_map/ppermute | solution.py:687
  4.7 7.9 %load.1 = (s32[16,128]{1,0:T(8,128)S(1)}, s32[16,128]{1,0:T(8,128)S(1)}, f32[1,1024]{1,0:T(1,128)S(1)}, bf16[80,1024]{1,0:T(8,128)(2,1)S(1)}, bf16[1024,512]{1,0...) custom-call(s32[16,128]{1,0:T(8,128)} %bitcast.50, ...), custom_call_target="tpu_custom_call" | custom-call | flops 8000000000 | bytes 1 | tf_op jit(solution)/shard_map/load/pallas_call | solution.py:257
  13.5 2.1 %theirs_0.1 = (bf16[4,4,208,128]{3,2,1,0:T(8,128)(2,1)S(1)}, bf16[1024,512]{1,0:T(8,128)(2,1)S(1)}, bf16[256,512]{1,0:T(8,128)(2,1)S(1)}, bf16[256,512]{1,0:T(8,...) custom-call(bf16[512,256]{1,0:T(8,128)(2,1)S(1)} %get-tuple-element.96.token.past_head, ...), custom_call_target="tpu_custom_call" | custom-call | flops 1 | bytes 1 | tf_op jit(solution)/shard_map/theirs_0/pallas_call | solution.py:446
  15.5 1.0 %collective-permute-start.1 = (bf16[4,4,208,128]{3,2,1,0:T(8,128)(2,1)S(1)}, bf16[4,4,208,128]{3,2,1,0:T(8,128)(2,1)S(1)}, u32[]{:S(2)}, u32[]{:S(2)}) collective-permute-start(bf16[4,4,208,128]{3,2,1,0:T(8,128)(2,1)S(1)} %get-tuple-element.101.token), channel_id=1, source_target_pairs={{0,16},{16,0},{1,17},{17,1},{2,18},{18,2},{3,19},{19,3},{4,20},{20... | collective-permute-start | bytes 2555912 | tf_op jit(solution)/shard_map/ppermute | solution.py:611
  16.5 2.2 %mine_0.1.token.refs_0_ = f32[4,4,208,128]{3,2,1,0:T(8,128)S(1)} custom-call(bf16[4,4,208,128]{3,2,1,0:T(8,128)(2,1)S(1)} %get-tuple-element.101.token, s32[16,128]{1,0:T(8,128)S(1)} %get-tuple-element.86.valid, bf16[1120,2048]{1,0:T(8,128)(2,1)S(1)} %get-tuple-element.88.x_turned, bf16[2048,512]{1,0:T(8,128)(2,1)S(1)} %get-tuple-element.89.gout, ...), custom_call_target="tpu_custom_call" | custom-call | flops 1 | bytes 1 | tf_op jit(solution)/shard_map/mine_0/pallas_call | solution.py:446
  18.7 1.4 %forward_1.1 = (bf16[512,256]{1,0:T(8,128)(2,1)S(1)}, bf16[256,512]{1,0:T(8,128)(2,1)S(1)}, bf16[512,512]{1,0:T(8,128)(2,1)S(1)}) custom-call(f32[4,4,208,128]{3,2,1,0:T(8,128)S(1)} %mine_0.1.token.refs_0_, s32[16,128]{1,0:T(8,128)S(1)} %get-tuple-element.86.valid, bf16[2048,512]{1,0:T(8,128)(2,1)S(1)} %get-tuple-element.102.past, ...), custom_call_target="tpu_custom_call" | custom-call | flops 1 | bytes 1 | tf_op jit(solution)/shard_map/forward_1/pallas_call | solution.py:328
  20.6 1.2 %collective-permute-start.3 = (bf16[4,208,128]{2,1,0:T(8,128)(2,1)S(1)}, bf16[4,208,128]{2,1,0:T(8,128)(2,1)S(1)}, u32[]{:S(2)}, u32[]{:S(2)}) collective-permute-start(bf16[4,208,128]{2,1,0:T(8,128)(2,1)S(1)} %bitcast.41), channel_id=1, source_target_pairs={{0,2},{1,3},{2,0},{3,1},{4,6},{5,7},{6,4},{7,5},{8,10},{9,11},{10,... | collective-permute-start | bytes 638984 | tf_op jit(solution)/shard_map/ppermute | solution.py:611
  21.8 1.2 %collective-permute-start.4 = (bf16[4,208,128]{2,1,0:T(8,128)(2,1)S(1)}, bf16[4,208,128]{2,1,0:T(8,128)(2,1)S(1)}, u32[]{:S(2)}, u32[]{:S(2)}) collective-permute-start(bf16[4,208,128]{2,1,0:T(8,128)(2,1)S(1)} %bitcast.38), channel_id=1, source_target_pairs={{0,3},{1,2},{2,1},{3,0},{4,7},{5,6},{6,5},{7,4},{8,11},{9,10},{10,... | collective-permute-start | bytes 638984 | tf_op jit(solution)/shard_map/ppermute | solution.py:611
  23.0 3.5 %ends_1.1 = (bf16[256,256]{1,0:T(8,128)(2,1)S(1)}, bf16[256,256]{1,0:T(8,128)(2,1)S(1)}, bf16[256,512]{1,0:T(8,128)(2,1)S(1)}, bf16[1280,256]{1,0:T(8,128)(2,1)S...) custom-call(f32[4,208,128]{2,1,0:T(8,128)S(1)} %bitcast.27, ...), custom_call_target="tpu_custom_call" | custom-call | flops 1 | bytes 1 | tf_op jit(solution)/shard_map/ends_1/pallas_call | solution.py:350
  26.5 2.0 %theirs_1.1.token = bf16[4,4,208,128]{3,2,1,0:T(8,128)(2,1)S(1)} custom-call(f32[4,208,128]{2,1,0:T(8,128)S(1)} %bitcast.28, s32[16,128]{1,0:T(8,128)S(1)} %get-tuple-element.86.valid, bf16[1120,2048]{1,0:T(8,128)(2,1)S(1)} %get-tuple-element.88.x_turned, bf16[2048,512]{1,0:T(8,128)(2,1)S(1)} %get-tuple-element.89.gout, ...), custom_call_target="tpu_custom_call" | custom-call | flops 1 | bytes 1 | tf_op jit(solution)/shard_map/theirs_1/pallas_call | solution.py:446
  29.3 2.2 %mine_1.1.token.refs_0_ = f32[4,4,208,128]{3,2,1,0:T(8,128)S(1)} custom-call(bf16[4,4,208,128]{3,2,1,0:T(8,128)(2,1)S(1)} %theirs_1.1.token, s32[16,128]{1,0:T(8,128)S(1)} %get-tuple-element.86.valid, bf16[1120,2048]{1,0:T(8,128)(2,1)S(1)} %get-tuple-element.88.x_turned, bf16[2048,512]{1,0:T(8,128)(2,1)S(1)} %get-tuple-element.89.gout, ...), custom_call_target="tpu_custom_call" | custom-call | flops 2000000000 | bytes 1 | tf_op jit(solution)/shard_map/mine_1/pallas_call | solution.py:446
  31.6 1.2 %collective-permute-done.4.refs_3_ = bf16[4,208,128]{2,1,0:T(8,128)(2,1)S(1)} collective-permute-done((bf16[4,208,128]{2,1,0:T(8,128)(2,1)S(1)}, bf16[4,208,128]{2,1,0:T(8,128)(2,1)S(1)}, u32[]{:S(2)}, u32[]{:S(2)}) %collective-permute-start.4) | collective-permute-done | bytes 213024 | tf_op jit(solution)/shard_map/ppermute | solution.py:611
  32.9 1.4 %collective-permute-start.6 = (bf16[2,208,128]{2,1,0:T(8,128)(2,1)S(1)}, bf16[2,208,128]{2,1,0:T(8,128)(2,1)S(1)}, u32[]{:S(2)}, u32[]{:S(2)}) collective-permute-start(bf16[2,208,128]{2,1,0:T(8,128)(2,1)S(1)} %get-tuple-element.119), channel_id=1, source_target_pairs={{0,4},{4,0},{8,12},{12,8},{1,5},{5,1},{9,13},{13,9},{2,6},{6,2},{1... | collective-permute-start | bytes 319496 | tf_op jit(solution)/shard_map/ppermute | solution.py:611
  34.8 1.2 %collective-permute-start.9 = (bf16[4,208,128]{2,1,0:T(8,128)(2,1)S(1)}, bf16[4,208,128]{2,1,0:T(8,128)(2,1)S(1)}, u32[]{:S(2)}, u32[]{:S(2)}) collective-permute-start(bf16[4,208,128]{2,1,0:T(8,128)(2,1)S(1)} %bitcast.37), channel_id=1, source_target_pairs={{0,2},{1,3},{2,0},{3,1},{4,6},{5,7},{6,4},{7,5},{8,10},{9,11},{10,... | collective-permute-start | bytes 638984 | tf_op jit(solution)/shard_map/ppermute | solution.py:611
  35.9 1.2 %collective-permute-start.10 = (bf16[4,208,128]{2,1,0:T(8,128)(2,1)S(1)}, bf16[4,208,128]{2,1,0:T(8,128)(2,1)S(1)}, u32[]{:S(2)}, u32[]{:S(2)}) collective-permute-start(bf16[4,208,128]{2,1,0:T(8,128)(2,1)S(1)} %bitcast.36), channel_id=1, source_target_pairs={{0,3},{1,2},{2,1},{3,0},{4,7},{5,6},{6,5},{7,4},{8,11},{9,10},{10,... | collective-permute-start | bytes 638984 | tf_op jit(solution)/shard_map/ppermute | solution.py:611
  37.2 1.8 %collective-permute-start.7 = (bf16[2,208,128]{2,1,0:T(8,128)(2,1)S(1)}, bf16[2,208,128]{2,1,0:T(8,128)(2,1)S(1)}, u32[]{:S(2)}, u32[]{:S(2)}) collective-permute-start(bf16[2,208,128]{2,1,0:T(8,128)(2,1)S(1)} %far_sum_0.1.token.mine), channel_id=1, source_target_pairs={{0,8},{4,12},{8,0},{12,4},{1,9},{5,13},{9,1},{13,5},{2,10},{6,14},... | collective-permute-start | bytes 319496 | tf_op jit(solution)/shard_map/ppermute | solution.py:611
  38.9 3.9 %inputs_0.1 = (f32[2048,512]{1,0:T(8,128)}, f32[80,2048]{1,0:T(8,128)}, f32[8,128]{1,0:T(8,128)S(1)}) custom-call(bf16[2,208,128]{2,1,0:T(8,128)(2,1)S(1)} %far_sum_0.1.token.mine, bf16[256,256]{1,0:T(8,128)(2,1)S(1)} %get-tuple-element.120.received.refs_0_, bf16[2048,512]{1,0:T(8,128)(2,1)S(1)} %get-tuple-element.89.gout, ...), custom_call_target="tpu_custom_call" | custom-call | flops 1 | bytes 1 | tf_op jit(solution)/shard_map/inputs_0/pallas_call | solution.py:536
  44.8 1.8 %collective-permute-done.11.refs_1_ = bf16[2,208,128]{2,1,0:T(8,128)(2,1)S(1)} collective-permute-done((bf16[2,208,128]{2,1,0:T(8,128)(2,1)S(1)}, bf16[2,208,128]{2,1,0:T(8,128)(2,1)S(1)}, u32[]{:S(2)}, u32[]{:S(2)}) %collective-permute-start.11) | collective-permute-done | bytes 106528 | tf_op jit(solution)/shard_map/ppermute | solution.py:611
  46.6 1.2 %collective-permute-start.14 = (bf16[4,208,128]{2,1,0:T(8,128)(2,1)S(1)}, bf16[4,208,128]{2,1,0:T(8,128)(2,1)S(1)}, u32[]{:S(2)}, u32[]{:S(2)}) collective-permute-start(bf16[4,208,128]{2,1,0:T(8,128)(2,1)S(1)} %far_join_0.1.token), channel_id=1, source_target_pairs={{0,3},{1,2},{2,1},{3,0},{4,7},{5,6},{6,5},{7,4},{8,11},{9,10},{10,... | collective-permute-start | bytes 638984 | tf_op jit(solution)/shard_map/ppermute | solution.py:611
  48.2 3.5 %collective-permute-start.13 = (bf16[2,208,128]{2,1,0:T(8,128)(2,1)S(1)}, bf16[2,208,128]{2,1,0:T(8,128)(2,1)S(1)}, u32[]{:S(2)}, u32[]{:S(2)}) collective-permute-start(bf16[2,208,128]{2,1,0:T(8,128)(2,1)S(1)} %far_sum_1.1.token.mine), channel_id=1, source_target_pairs={{0,8},{4,12},{8,0},{12,4},{1,9},{5,13},{9,1},{13,5},{2,10},{6,14},... | collective-permute-start | bytes 319496 | tf_op jit(solution)/shard_map/ppermute | solution.py:611
  51.9 1.4 %collective-permute-start.15 = (bf16[4,208,128]{2,1,0:T(8,128)(2,1)S(1)}, bf16[4,208,128]{2,1,0:T(8,128)(2,1)S(1)}, u32[]{:S(2)}, u32[]{:S(2)}) collective-permute-start(bf16[4,208,128]{2,1,0:T(8,128)(2,1)S(1)} %far_join_0.1.token), channel_id=1, source_target_pairs={{0,1},{1,0},{2,3},{3,2},{4,5},{5,4},{6,7},{7,6},{8,9},{9,8},{10,11... | collective-permute-start | bytes 638984 | tf_op jit(solution)/shard_map/ppermute | solution.py:611
  53.3 2.4 %inputs_2.1 = (f32[2048,512]{1,0:T(8,128)}, f32[80,2048]{1,0:T(8,128)}, f32[8,128]{1,0:T(8,128)S(1)}) custom-call(bf16[2,208,128]{2,1,0:T(8,128)(2,1)S(1)} %far_sum_1.1.token.mine, bf16[256,256]{1,0:T(8,128)(2,1)S(1)} %get-tuple-element.120.received.refs_0_, ...), custom_call_target="tpu_custom_call", output_to_operand_aliasing={{0}: (12, {}), {1}: (13, {})} | custom-call | flops 1 | bytes 1 | tf_op jit(solution)/shard_map/inputs_2/pallas_call | solution.py:536
  56.3 2.3 %collective-permute-start.18 = (bf16[256,512]{1,0:T(8,128)(2,1)S(1)}, bf16[256,512]{1,0:T(8,128)(2,1)S(1)}, u32[]{:S(2)}, u32[]{:S(2)}) collective-permute-start(bf16[256,512]{1,0:T(8,128)(2,1)S(1)} %early.1.token), channel_id=1, source_target_pairs={{1,0},{2,1},{3,2},{4,3},{5,4},{6,5},{7,6},{8,7},{9,8},{10,9},{11,1... | collective-permute-start | bytes 786440 | tf_op jit(solution)/shard_map/ppermute | solution.py:687
  59.9 1.3 %collective-permute-start.19 = (bf16[4,208,128]{2,1,0:T(8,128)(2,1)S(1)}, bf16[4,208,128]{2,1,0:T(8,128)(2,1)S(1)}, u32[]{:S(2)}, u32[]{:S(2)}) collective-permute-start(bf16[4,208,128]{2,1,0:T(8,128)(2,1)S(1)} %far_join_1.1.token), channel_id=1, source_target_pairs={{0,3},{1,2},{2,1},{3,0},{4,7},{5,6},{6,5},{7,4},{8,11},{9,10},{10,... | collective-permute-start | bytes 638984 | tf_op jit(solution)/shard_map/ppermute | solution.py:611
  61.2 6.2 %collective-permute-start.24 = (bf16[4,208,128]{2,1,0:T(8,128)(2,1)S(1)}, bf16[4,208,128]{2,1,0:T(8,128)(2,1)S(1)}, u32[]{:S(2)}, u32[]{:S(2)}) collective-permute-start(bf16[4,208,128]{2,1,0:T(8,128)(2,1)S(1)} %far_join_1.1.token), channel_id=1, source_target_pairs={{0,2},{1,3},{2,0},{3,1},{4,6},{5,7},{6,4},{7,5},{8,10},{9,11},{10,... | collective-permute-start | bytes 638984 | tf_op jit(solution)/shard_map/ppermute | solution.py:611
  68.3 3.6 %outputs.1 = (bf16[2048,512]{1,0:T(8,128)(2,1)}, bf16[2048,512]{1,0:T(8,128)(2,1)}, f32[8,128]{1,0:T(8,128)S(1)}) custom-call(bf16[4,208,128]{2,1,0:T(8,128)(2,1)S(1)} %far_join_1.1.token, s32[16,128]{1,0:T(8,128)S(1)} %get-tuple-element.86.valid, bf16[2048,512]{1,0:T(8,128)(2,1)S(1)} %get-tuple-element.87.sig, ...), custom_call_target="tpu_custom_call" | custom-call | flops 1 | bytes 1 | tf_op jit(solution)/shard_map/outputs/pallas_call | solution.py:479
  72.0 2.2 %inputs_3.1 = (f32[2048,512]{1,0:T(8,128)}, f32[80,2048]{1,0:T(8,128)}, f32[8,128]{1,0:T(8,128)S(1)}) custom-call(f32[8,128]{1,0:T(8,128)S(1)} %get-tuple-element.137.token, bf16[256,512]{1,0:T(8,128)(2,1)S(1)} %collective-permute-done.18.received, bf16[2048,512]{1,0:T(8,128)(2,1)S(1)} %get-tuple-element.89.gout, ...), custom_call_target="tpu_custom_call", output_to_operand_aliasing={{0}: (12, {}), {1}: (13, {})} | custom-call | flops 1 | bytes 1 | tf_op jit(solution)/shard_map/inputs_3/pallas_call | solution.py:536
  75.1 2.8 %collective-permute-done.24 = bf16[4,208,128]{2,1,0:T(8,128)(2,1)S(1)} collective-permute-done((bf16[4,208,128]{2,1,0:T(8,128)(2,1)S(1)}, bf16[4,208,128]{2,1,0:T(8,128)(2,1)S(1)}, u32[]{:S(2)}, u32[]{:S(2)}) %collective-permute-start.24) | collective-permute-done | bytes 213024 | tf_op jit(solution)/shard_map/ppermute | solution.py:611
  78.0 1.0 %collective-permute-done.23 = bf16[4,208,128]{2,1,0:T(8,128)(2,1)S(1)} collective-permute-done((bf16[4,208,128]{2,1,0:T(8,128)(2,1)S(1)}, bf16[4,208,128]{2,1,0:T(8,128)(2,1)S(1)}, u32[]{:S(2)}, u32[]{:S(2)}) %collective-permute-start.23) | collective-permute-done | bytes 213024 | tf_op jit(solution)/shard_map/ppermute | solution.py:611
  79.6 2.0 %unpack_0.1 = (f32[512,1024]{1,0:T(8,128)}, f32[512,1024]{1,0:T(8,128)}, f32[80,1024]{1,0:T(8,128)}, f32[1,1024]{1,0:T(1,128)}, f32[512,512]{1,0:T(8,128)}, /*in...) custom-call(bf16[2,4,208,128]{3,2,1,0:T(8,128)(2,1)S(1)} %collective-permute-done.20.token.refs_2_, ...), custom_call_target="tpu_custom_call" | custom-call | flops 1 | bytes 1 | tf_op jit(solution)/shard_map/unpack_0/pallas_call | solution.py:598
  81.6 2.0 %unpack_1.1 = (f32[512,1024]{1,0:T(8,128)}, f32[512,1024]{1,0:T(8,128)}, f32[80,1024]{1,0:T(8,128)}, f32[1,1024]{1,0:T(1,128)}, f32[512,512]{1,0:T(8,128)}, /*in...) custom-call(f32[8,128]{1,0:T(8,128)S(1)} %get-tuple-element.143.toke, ...), custom_call_target="tpu_custom_call", output_to_operand_aliasing={{0}: (5, {}), {1}: (6, {}), {2}: (7, {}), {3}: (8, {}), {4}... | custom-call | flops 1 | bytes 1 | tf_op jit(solution)/shard_map/unpack_1/pallas_call | solution.py:598
  (50 shorter events, 9.7 us)
Async XLA Ops:
  1.6 11.0 %collective-permute-start = (bf16[256,512]{1,0:T(8,128)(2,1)S(1)}, bf16[256,512]{1,0:T(8,128)(2,1)S(1)}, u32[]{:S(2)}, u32[]{:S(2)}) collective-permute-start(bf16[256,512]{1,0:T(8,128)(2,1)S(1)} %slice.3), channel_id=1, source_target_pairs={{0,1},{1,2},{2,3},{3,4},{4,5},{5,6},{6,7},{7,8},{8,9},{9,10},{10,1... | collective-permute-start | bytes 786440 | tf_op jit(solution)/shard_map/ppermute | solution.py:687
  15.5 4.6 %collective-permute-start.1 = (bf16[4,4,208,128]{3,2,1,0:T(8,128)(2,1)S(1)}, bf16[4,4,208,128]{3,2,1,0:T(8,128)(2,1)S(1)}, u32[]{:S(2)}, u32[]{:S(2)}) collective-permute-start(bf16[4,4,208,128]{3,2,1,0:T(8,128)(2,1)S(1)} %get-tuple-element.101.token), channel_id=1, source_target_pairs={{0,16},{16,0},{1,17},{17,1},{2,18},{18,2},{3,19},{19,3},{4,20},{20... | collective-permute-start | bytes 2555912 | tf_op jit(solution)/shard_map/ppermute | solution.py:611
  20.3 11.3 %collective-permute-start.2 = (bf16[4,208,128]{2,1,0:T(8,128)(2,1)S(1)}, bf16[4,208,128]{2,1,0:T(8,128)(2,1)S(1)}, u32[]{:S(2)}, u32[]{:S(2)}) collective-permute-start(bf16[4,208,128]{2,1,0:T(8,128)(2,1)S(1)} %bitcast.42), channel_id=1, source_target_pairs={{0,1},{1,0},{2,3},{3,2},{4,5},{5,4},{6,7},{7,6},{8,9},{9,8},{10,11... | collective-permute-start | bytes 638984 | tf_op jit(solution)/shard_map/ppermute | solution.py:611
  20.6 11.0 %collective-permute-start.3 = (bf16[4,208,128]{2,1,0:T(8,128)(2,1)S(1)}, bf16[4,208,128]{2,1,0:T(8,128)(2,1)S(1)}, u32[]{:S(2)}, u32[]{:S(2)}) collective-permute-start(bf16[4,208,128]{2,1,0:T(8,128)(2,1)S(1)} %bitcast.41), channel_id=1, source_target_pairs={{0,2},{1,3},{2,0},{3,1},{4,6},{5,7},{6,4},{7,5},{8,10},{9,11},{10,... | collective-permute-start | bytes 638984 | tf_op jit(solution)/shard_map/ppermute | solution.py:611
  21.8 10.9 %collective-permute-start.4 = (bf16[4,208,128]{2,1,0:T(8,128)(2,1)S(1)}, bf16[4,208,128]{2,1,0:T(8,128)(2,1)S(1)}, u32[]{:S(2)}, u32[]{:S(2)}) collective-permute-start(bf16[4,208,128]{2,1,0:T(8,128)(2,1)S(1)} %bitcast.38), channel_id=1, source_target_pairs={{0,3},{1,2},{2,1},{3,0},{4,7},{5,6},{6,5},{7,4},{8,11},{9,10},{10,... | collective-permute-start | bytes 638984 | tf_op jit(solution)/shard_map/ppermute | solution.py:611
  28.4 5.8 %collective-permute-start.5 = (bf16[4,4,208,128]{3,2,1,0:T(8,128)(2,1)S(1)}, bf16[4,4,208,128]{3,2,1,0:T(8,128)(2,1)S(1)}, u32[]{:S(2)}, u32[]{:S(2)}) collective-permute-start(bf16[4,4,208,128]{3,2,1,0:T(8,128)(2,1)S(1)} %theirs_1.1.token), channel_id=1, source_target_pairs={{0,16},{16,0},{1,17},{17,1},{2,18},{18,2},{3,19},{19,3},{4,20},{20... | collective-permute-start | bytes 2555912 | tf_op jit(solution)/shard_map/ppermute | solution.py:611
  32.9 4.3 %collective-permute-start.6 = (bf16[2,208,128]{2,1,0:T(8,128)(2,1)S(1)}, bf16[2,208,128]{2,1,0:T(8,128)(2,1)S(1)}, u32[]{:S(2)}, u32[]{:S(2)}) collective-permute-start(bf16[2,208,128]{2,1,0:T(8,128)(2,1)S(1)} %get-tuple-element.119), channel_id=1, source_target_pairs={{0,4},{4,0},{8,12},{12,8},{1,5},{5,1},{9,13},{13,9},{2,6},{6,2},{1... | collective-permute-start | bytes 319496 | tf_op jit(solution)/shard_map/ppermute | solution.py:611
  34.4 9.3 %collective-permute-start.8 = (bf16[4,208,128]{2,1,0:T(8,128)(2,1)S(1)}, bf16[4,208,128]{2,1,0:T(8,128)(2,1)S(1)}, u32[]{:S(2)}, u32[]{:S(2)}) collective-permute-start(bf16[4,208,128]{2,1,0:T(8,128)(2,1)S(1)} %bitcast.40), channel_id=1, source_target_pairs={{0,1},{1,0},{2,3},{3,2},{4,5},{5,4},{6,7},{7,6},{8,9},{9,8},{10,11... | collective-permute-start | bytes 638984 | tf_op jit(solution)/shard_map/ppermute | solution.py:611
  34.8 9.0 %collective-permute-start.9 = (bf16[4,208,128]{2,1,0:T(8,128)(2,1)S(1)}, bf16[4,208,128]{2,1,0:T(8,128)(2,1)S(1)}, u32[]{:S(2)}, u32[]{:S(2)}) collective-permute-start(bf16[4,208,128]{2,1,0:T(8,128)(2,1)S(1)} %bitcast.37), channel_id=1, source_target_pairs={{0,2},{1,3},{2,0},{3,1},{4,6},{5,7},{6,4},{7,5},{8,10},{9,11},{10,... | collective-permute-start | bytes 638984 | tf_op jit(solution)/shard_map/ppermute | solution.py:611
  35.9 8.5 %collective-permute-start.10 = (bf16[4,208,128]{2,1,0:T(8,128)(2,1)S(1)}, bf16[4,208,128]{2,1,0:T(8,128)(2,1)S(1)}, u32[]{:S(2)}, u32[]{:S(2)}) collective-permute-start(bf16[4,208,128]{2,1,0:T(8,128)(2,1)S(1)} %bitcast.36), channel_id=1, source_target_pairs={{0,3},{1,2},{2,1},{3,0},{4,7},{5,6},{6,5},{7,4},{8,11},{9,10},{10,... | collective-permute-start | bytes 638984 | tf_op jit(solution)/shard_map/ppermute | solution.py:611
  37.2 5.7 %collective-permute-start.7 = (bf16[2,208,128]{2,1,0:T(8,128)(2,1)S(1)}, bf16[2,208,128]{2,1,0:T(8,128)(2,1)S(1)}, u32[]{:S(2)}, u32[]{:S(2)}) collective-permute-start(bf16[2,208,128]{2,1,0:T(8,128)(2,1)S(1)} %far_sum_0.1.token.mine), channel_id=1, source_target_pairs={{0,8},{4,12},{8,0},{12,4},{1,9},{5,13},{9,1},{13,5},{2,10},{6,14},... | collective-permute-start | bytes 319496 | tf_op jit(solution)/shard_map/ppermute | solution.py:611
  42.9 3.7 %collective-permute-start.11 = (bf16[2,208,128]{2,1,0:T(8,128)(2,1)S(1)}, bf16[2,208,128]{2,1,0:T(8,128)(2,1)S(1)}, u32[]{:S(2)}, u32[]{:S(2)}) collective-permute-start(bf16[2,208,128]{2,1,0:T(8,128)(2,1)S(1)} %far_end_0.1.token.refs_0_), channel_id=1, source_target_pairs={{0,4},{4,0},{8,12},{12,8},{1,5},{5,1},{9,13},{13,9},{2,6},{6,2},{1... | collective-permute-start | bytes 319496 | tf_op jit(solution)/shard_map/ppermute | solution.py:611
  44.6 3.6 %collective-permute-start.12 = (bf16[2,208,128]{2,1,0:T(8,128)(2,1)S(1)}, bf16[2,208,128]{2,1,0:T(8,128)(2,1)S(1)}, u32[]{:S(2)}, u32[]{:S(2)}) collective-permute-start(bf16[2,208,128]{2,1,0:T(8,128)(2,1)S(1)} %get-tuple-element.126), channel_id=1, source_target_pairs={{0,4},{4,0},{8,12},{12,8},{1,5},{5,1},{9,13},{13,9},{2,6},{6,2},{1... | collective-permute-start | bytes 319496 | tf_op jit(solution)/shard_map/ppermute | solution.py:611
  46.6 12.0 %collective-permute-start.14 = (bf16[4,208,128]{2,1,0:T(8,128)(2,1)S(1)}, bf16[4,208,128]{2,1,0:T(8,128)(2,1)S(1)}, u32[]{:S(2)}, u32[]{:S(2)}) collective-permute-start(bf16[4,208,128]{2,1,0:T(8,128)(2,1)S(1)} %far_join_0.1.token), channel_id=1, source_target_pairs={{0,3},{1,2},{2,1},{3,0},{4,7},{5,6},{6,5},{7,4},{8,11},{9,10},{10,... | collective-permute-start | bytes 638984 | tf_op jit(solution)/shard_map/ppermute | solution.py:611
  48.2 7.5 %collective-permute-start.13 = (bf16[2,208,128]{2,1,0:T(8,128)(2,1)S(1)}, bf16[2,208,128]{2,1,0:T(8,128)(2,1)S(1)}, u32[]{:S(2)}, u32[]{:S(2)}) collective-permute-start(bf16[2,208,128]{2,1,0:T(8,128)(2,1)S(1)} %far_sum_1.1.token.mine), channel_id=1, source_target_pairs={{0,8},{4,12},{8,0},{12,4},{1,9},{5,13},{9,1},{13,5},{2,10},{6,14},... | collective-permute-start | bytes 319496 | tf_op jit(solution)/shard_map/ppermute | solution.py:611
  51.7 7.6 %collective-permute-start.16 = (bf16[4,208,128]{2,1,0:T(8,128)(2,1)S(1)}, bf16[4,208,128]{2,1,0:T(8,128)(2,1)S(1)}, u32[]{:S(2)}, u32[]{:S(2)}) collective-permute-start(bf16[4,208,128]{2,1,0:T(8,128)(2,1)S(1)} %far_join_0.1.token), channel_id=1, source_target_pairs={{0,2},{1,3},{2,0},{3,1},{4,6},{5,7},{6,4},{7,5},{8,10},{9,11},{10,... | collective-permute-start | bytes 638984 | tf_op jit(solution)/shard_map/ppermute | solution.py:611
  51.9 7.5 %collective-permute-start.15 = (bf16[4,208,128]{2,1,0:T(8,128)(2,1)S(1)}, bf16[4,208,128]{2,1,0:T(8,128)(2,1)S(1)}, u32[]{:S(2)}, u32[]{:S(2)}) collective-permute-start(bf16[4,208,128]{2,1,0:T(8,128)(2,1)S(1)} %far_join_0.1.token), channel_id=1, source_target_pairs={{0,1},{1,0},{2,3},{3,2},{4,5},{5,4},{6,7},{7,6},{8,9},{9,8},{10,11... | collective-permute-start | bytes 638984 | tf_op jit(solution)/shard_map/ppermute | solution.py:611
  55.8 4.1 %collective-permute-start.17 = (bf16[2,208,128]{2,1,0:T(8,128)(2,1)S(1)}, bf16[2,208,128]{2,1,0:T(8,128)(2,1)S(1)}, u32[]{:S(2)}, u32[]{:S(2)}) collective-permute-start(bf16[2,208,128]{2,1,0:T(8,128)(2,1)S(1)} %far_end_1.1.token.refs_0_), channel_id=1, source_target_pairs={{0,4},{4,0},{8,12},{12,8},{1,5},{5,1},{9,13},{13,9},{2,6},{6,2},{1... | collective-permute-start | bytes 319496 | tf_op jit(solution)/shard_map/ppermute | solution.py:611
  56.3 15.5 %collective-permute-start.18 = (bf16[256,512]{1,0:T(8,128)(2,1)S(1)}, bf16[256,512]{1,0:T(8,128)(2,1)S(1)}, u32[]{:S(2)}, u32[]{:S(2)}) collective-permute-start(bf16[256,512]{1,0:T(8,128)(2,1)S(1)} %early.1.token), channel_id=1, source_target_pairs={{1,0},{2,1},{3,2},{4,3},{5,4},{6,5},{7,6},{8,7},{9,8},{10,9},{11,1... | collective-permute-start | bytes 786440 | tf_op jit(solution)/shard_map/ppermute | solution.py:687
  59.9 14.3 %collective-permute-start.19 = (bf16[4,208,128]{2,1,0:T(8,128)(2,1)S(1)}, bf16[4,208,128]{2,1,0:T(8,128)(2,1)S(1)}, u32[]{:S(2)}, u32[]{:S(2)}) collective-permute-start(bf16[4,208,128]{2,1,0:T(8,128)(2,1)S(1)} %far_join_1.1.token), channel_id=1, source_target_pairs={{0,3},{1,2},{2,1},{3,0},{4,7},{5,6},{6,5},{7,4},{8,11},{9,10},{10,... | collective-permute-start | bytes 638984 | tf_op jit(solution)/shard_map/ppermute | solution.py:611
  61.2 16.7 %collective-permute-start.24 = (bf16[4,208,128]{2,1,0:T(8,128)(2,1)S(1)}, bf16[4,208,128]{2,1,0:T(8,128)(2,1)S(1)}, u32[]{:S(2)}, u32[]{:S(2)}) collective-permute-start(bf16[4,208,128]{2,1,0:T(8,128)(2,1)S(1)} %far_join_1.1.token), channel_id=1, source_target_pairs={{0,2},{1,3},{2,0},{3,1},{4,6},{5,7},{6,4},{7,5},{8,10},{9,11},{10,... | collective-permute-start | bytes 638984 | tf_op jit(solution)/shard_map/ppermute | solution.py:611
  67.4 11.6 %collective-permute-start.23 = (bf16[4,208,128]{2,1,0:T(8,128)(2,1)S(1)}, bf16[4,208,128]{2,1,0:T(8,128)(2,1)S(1)}, u32[]{:S(2)}, u32[]{:S(2)}) collective-permute-start(bf16[4,208,128]{2,1,0:T(8,128)(2,1)S(1)} %far_join_1.1.token), channel_id=1, source_target_pairs={{0,1},{1,0},{2,3},{3,2},{4,5},{5,4},{6,7},{7,6},{8,9},{9,8},{10,11... | collective-permute-start | bytes 638984 | tf_op jit(solution)/shard_map/ppermute | solution.py:611
  67.4 12.2 %collective-permute-start.22 = (bf16[2,4,208,128]{3,2,1,0:T(8,128)(2,1)S(1)}, bf16[2,4,208,128]{3,2,1,0:T(8,128)(2,1)S(1)}, u32[]{:S(2)}, u32[]{:S(2)}) collective-permute-start(bf16[2,4,208,128]{3,2,1,0:T(8,128)(2,1)S(1)} %near_join_0_1.1.token.refs_1_), channel_id=1, source_target_pairs={{0,16},{16,0},{1,17},{17,1},{2,18},{18,2},{3,19},{19,3},{4,20},{20... | collective-permute-start | bytes 1277960 | tf_op jit(solution)/shard_map/ppermute | solution.py:611
  71.9 7.7 %collective-permute-start.21 = (bf16[2,4,208,128]{3,2,1,0:T(8,128)(2,1)S(1)}, bf16[2,4,208,128]{3,2,1,0:T(8,128)(2,1)S(1)}, u32[]{:S(2)}, u32[]{:S(2)}) collective-permute-start(bf16[2,4,208,128]{3,2,1,0:T(8,128)(2,1)S(1)} %near_join_0_0.1.token.refs_0_), channel_id=1, source_target_pairs={{0,16},{16,0},{1,17},{17,1},{2,18},{18,2},{3,19},{19,3},{4,20},{20... | collective-permute-start | bytes 1277960 | tf_op jit(solution)/shard_map/ppermute | solution.py:611
  74.2 5.4 %collective-permute-start.20 = (bf16[2,4,208,128]{3,2,1,0:T(8,128)(2,1)S(1)}, bf16[2,4,208,128]{3,2,1,0:T(8,128)(2,1)S(1)}, u32[]{:S(2)}, u32[]{:S(2)}) collective-permute-start(bf16[2,4,208,128]{3,2,1,0:T(8,128)(2,1)S(1)} %near_join_1_0.1.token.refs_0_), channel_id=1, source_target_pairs={{0,16},{16,0},{1,17},{17,1},{2,18},{18,2},{3,19},{19,3},{4,20},{20... | collective-permute-start | bytes 1277960 | tf_op jit(solution)/shard_map/ppermute | solution.py:611
  79.0 2.6 %collective-permute-start.25 = (bf16[2,4,208,128]{3,2,1,0:T(8,128)(2,1)S(1)}, bf16[2,4,208,128]{3,2,1,0:T(8,128)(2,1)S(1)}, u32[]{:S(2)}, u32[]{:S(2)}) collective-permute-start(bf16[2,4,208,128]{3,2,1,0:T(8,128)(2,1)S(1)} %near_join_1_1.1.refs_1_), channel_id=1, source_target_pairs={{0,16},{16,0},{1,17},{17,1},{2,18},{18,2},{3,19},{19,3},{4,20},{20... | collective-permute-start | bytes 1277960 | tf_op jit(solution)/shard_map/ppermute | solution.py:611

commit v5 on v4

--- a/solution.py
+++ b/solution.py
@@ -20,7 +20,7 @@
 MEGA = 1 << 20
 COSTS = {
     "load": 8, "head": 2, "near_sum_0": 7, "mine_1": 2,
-    "far_sum_0": 8, "near_sum_1": 4, "near_join_0_0": 2, "near_join_0_1": 2, "near_join_1_1": 4, "far_join_0": 4,
+    "near_part_1": 2, "near_sum_1": 4, "near_join_0_0": 2, "near_join_0_1": 2, "near_join_1_1": 4, "far_join_0": 4,
 }
 FLOPS = 10**9
 
@@ -782,7 +782,8 @@
     ends_0, got_0 = far_sum(0, kept_1, kept_0, got_0)
     *grads, mark = input_gradients((0, 1), ends_0, [])
     ends_0, got_0 = far_end(0, mark, ends_0, got_0)
-    kept_1, got_1 = near_sum(1, ends_0, kept_1, got_1)
+    (part,) = added("near_part_1", ends_0, got_1[2], [got_1[1]], [(far, F32)])
+    kept_1, got_1 = near_sum(1, part, kept_1, [part, got_1[0]])
     ends_0, got_0 = far_join(0, kept_1, ends_0, got_0)
     ends_1, got_1 = far_sum(1, ends_0, kept_1, got_1)
     *grads, mark = input_gradients((2,), ends_1, grads)

time: 83.9 us -> 85.7 us (1.021)
  waiting for transfers between devices: 9.06 us -> 10.7 us
    ppermute x24, waiting for transfers between devices: 9.05 us -> 10.7 us  [swapped(): lax.ppermute(x, axis, [(i, i ^ k) for i in range(lax.axis_size(axis))])]
  transfers between devices with their start and end apart: 26 -> 26, of which waited for: 8 -> 8; matrix products, arithmetic and copies ran while one was open for 0% -> 0% of each run, Pallas kernels for 41% -> 40%
where the time goes in v5:
time: 85.7 us; the launch traced here: 84.8 us
  Pallas kernels  39.3 us (46%)
  starting transfers between devices  32.7 us (38%)
  waiting for transfers between devices  10.7 us (12%)
  between operations  1.03 us (1%)
  local copies, waits for them, and re-layouts  0.97 us (1%)
    ppermute x24, starting transfers between devices, swapped(): lax.ppermute(x, axis, [(i, i ^ k) for i in range(lax.axis_size(axis))])  27.1 us
    ppermute x24, waiting for transfers between devices, swapped(): lax.ppermute(x, axis, [(i, i ^ k) for i in range(lax.axis_size(axis))])  10.7 us
    pallas_call x3, Pallas kernels, inputs(): call(functools.partial(inputs_body, steps, counts), f'inputs_{steps[0]}',...  8.47 us
    pallas_call x4, Pallas kernels, gradients(): call(functools.partial(gradients_body, far, block, half, own, count, len(...  8.43 us
    pallas_call x1, Pallas kernels, load(): call(load_body, 'load', [ANYWHERE] * len(sources), [VMEM] * len(shapes),...  7.87 us
    ppermute x2, starting transfers between devices, passed_along(): return lax.ppermute(x, AXES, pairs)  5.64 us
    pallas_call x2, Pallas kernels, unpack(): call(functools.partial(unpack_body, far, block), f'unpack_{half}', [ANYWH...  4 us
    pallas_call x1, Pallas kernels, outputs(): call(functools.partial(outputs_body, counts), 'outputs', [ANYWHERE] + [VM...  3.62 us
  transfers between devices with their start and end apart: 26, of which 8 were waited for; matrix products, arithmetic and copies ran while one was open for 0% of the time, Pallas kernels for 40%

profile of v5, /device:TPU:3, one launch (start us, length us, event | category | flops | bytes accessed | tf_op | source)
XLA Modules:
  0.0 84.8 jit_solution(17900449582443817416)
XLA Ops:
  1.6 3.1 %collective-permute-start = (bf16[256,512]{1,0:T(8,128)(2,1)S(1)}, bf16[256,512]{1,0:T(8,128)(2,1)S(1)}, u32[]{:S(2)}, u32[]{:S(2)}) collective-permute-start(bf16[256,512]{1,0:T(8,128)(2,1)S(1)} %slice.3), channel_id=1, source_target_pairs={{0,1},{1,2},{2,3},{3,4},{4,5},{5,6},{6,7},{7,8},{8,9},{9,10},{10,1... | collective-permute-start | bytes 786440 | tf_op jit(solution)/shard_map/ppermute | solution.py:687
  4.7 7.9 %load.1 = (s32[16,128]{1,0:T(8,128)S(1)}, s32[16,128]{1,0:T(8,128)S(1)}, f32[1,1024]{1,0:T(1,128)S(1)}, bf16[80,1024]{1,0:T(8,128)(2,1)S(1)}, bf16[1024,512]{1,0...) custom-call(s32[16,128]{1,0:T(8,128)} %bitcast.50, ...), custom_call_target="tpu_custom_call" | custom-call | flops 8000000000 | bytes 1 | tf_op jit(solution)/shard_map/load/pallas_call | solution.py:257
  13.4 2.1 %theirs_0.1 = (bf16[4,4,208,128]{3,2,1,0:T(8,128)(2,1)S(1)}, bf16[1024,512]{1,0:T(8,128)(2,1)S(1)}, bf16[256,512]{1,0:T(8,128)(2,1)S(1)}, bf16[256,512]{1,0:T(8,...) custom-call(bf16[512,256]{1,0:T(8,128)(2,1)S(1)} %get-tuple-element.96.token.past_head, ...), custom_call_target="tpu_custom_call" | custom-call | flops 1 | bytes 1 | tf_op jit(solution)/shard_map/theirs_0/pallas_call | solution.py:446
  15.5 1.0 %collective-permute-start.1 = (bf16[4,4,208,128]{3,2,1,0:T(8,128)(2,1)S(1)}, bf16[4,4,208,128]{3,2,1,0:T(8,128)(2,1)S(1)}, u32[]{:S(2)}, u32[]{:S(2)}) collective-permute-start(bf16[4,4,208,128]{3,2,1,0:T(8,128)(2,1)S(1)} %get-tuple-element.101.token), channel_id=1, source_target_pairs={{0,16},{16,0},{1,17},{17,1},{2,18},{18,2},{3,19},{19,3},{4,20},{20... | collective-permute-start | bytes 2555912 | tf_op jit(solution)/shard_map/ppermute | solution.py:611
  16.5 2.2 %mine_0.1.token.refs_0_ = f32[4,4,208,128]{3,2,1,0:T(8,128)S(1)} custom-call(bf16[4,4,208,128]{3,2,1,0:T(8,128)(2,1)S(1)} %get-tuple-element.101.token, s32[16,128]{1,0:T(8,128)S(1)} %get-tuple-element.86.valid, bf16[1120,2048]{1,0:T(8,128)(2,1)S(1)} %get-tuple-element.88.x_turned, bf16[2048,512]{1,0:T(8,128)(2,1)S(1)} %get-tuple-element.89.gout, ...), custom_call_target="tpu_custom_call" | custom-call | flops 1 | bytes 1 | tf_op jit(solution)/shard_map/mine_0/pallas_call | solution.py:446
  18.7 1.3 %forward_1.1 = (bf16[512,256]{1,0:T(8,128)(2,1)S(1)}, bf16[256,512]{1,0:T(8,128)(2,1)S(1)}, bf16[512,512]{1,0:T(8,128)(2,1)S(1)}) custom-call(f32[4,4,208,128]{3,2,1,0:T(8,128)S(1)} %mine_0.1.token.refs_0_, s32[16,128]{1,0:T(8,128)S(1)} %get-tuple-element.86.valid, bf16[2048,512]{1,0:T(8,128)(2,1)S(1)} %get-tuple-element.102.past, ...), custom_call_target="tpu_custom_call" | custom-call | flops 1 | bytes 1 | tf_op jit(solution)/shard_map/forward_1/pallas_call | solution.py:328
  20.6 1.2 %collective-permute-start.3 = (bf16[4,208,128]{2,1,0:T(8,128)(2,1)S(1)}, bf16[4,208,128]{2,1,0:T(8,128)(2,1)S(1)}, u32[]{:S(2)}, u32[]{:S(2)}) collective-permute-start(bf16[4,208,128]{2,1,0:T(8,128)(2,1)S(1)} %bitcast.41), channel_id=1, source_target_pairs={{0,2},{1,3},{2,0},{3,1},{4,6},{5,7},{6,4},{7,5},{8,10},{9,11},{10,... | collective-permute-start | bytes 638984 | tf_op jit(solution)/shard_map/ppermute | solution.py:611
  21.8 1.2 %collective-permute-start.4 = (bf16[4,208,128]{2,1,0:T(8,128)(2,1)S(1)}, bf16[4,208,128]{2,1,0:T(8,128)(2,1)S(1)}, u32[]{:S(2)}, u32[]{:S(2)}) collective-permute-start(bf16[4,208,128]{2,1,0:T(8,128)(2,1)S(1)} %bitcast.38), channel_id=1, source_target_pairs={{0,3},{1,2},{2,1},{3,0},{4,7},{5,6},{6,5},{7,4},{8,11},{9,10},{10,... | collective-permute-start | bytes 638984 | tf_op jit(solution)/shard_map/ppermute | solution.py:611
  23.0 3.5 %ends_1.1 = (bf16[256,256]{1,0:T(8,128)(2,1)S(1)}, bf16[256,256]{1,0:T(8,128)(2,1)S(1)}, bf16[256,512]{1,0:T(8,128)(2,1)S(1)}, bf16[1280,256]{1,0:T(8,128)(2,1)S...) custom-call(f32[4,208,128]{2,1,0:T(8,128)S(1)} %bitcast.27, ...), custom_call_target="tpu_custom_call" | custom-call | flops 1 | bytes 1 | tf_op jit(solution)/shard_map/ends_1/pallas_call | solution.py:350
  26.5 2.0 %theirs_1.1.token = bf16[4,4,208,128]{3,2,1,0:T(8,128)(2,1)S(1)} custom-call(f32[4,208,128]{2,1,0:T(8,128)S(1)} %bitcast.28, s32[16,128]{1,0:T(8,128)S(1)} %get-tuple-element.86.valid, bf16[1120,2048]{1,0:T(8,128)(2,1)S(1)} %get-tuple-element.88.x_turned, bf16[2048,512]{1,0:T(8,128)(2,1)S(1)} %get-tuple-element.89.gout, ...), custom_call_target="tpu_custom_call" | custom-call | flops 1 | bytes 1 | tf_op jit(solution)/shard_map/theirs_1/pallas_call | solution.py:446
  29.3 2.2 %mine_1.1.token.refs_0_ = f32[4,4,208,128]{3,2,1,0:T(8,128)S(1)} custom-call(bf16[4,4,208,128]{3,2,1,0:T(8,128)(2,1)S(1)} %theirs_1.1.token, s32[16,128]{1,0:T(8,128)S(1)} %get-tuple-element.86.valid, bf16[1120,2048]{1,0:T(8,128)(2,1)S(1)} %get-tuple-element.88.x_turned, bf16[2048,512]{1,0:T(8,128)(2,1)S(1)} %get-tuple-element.89.gout, ...), custom_call_target="tpu_custom_call" | custom-call | flops 2000000000 | bytes 1 | tf_op jit(solution)/shard_map/mine_1/pallas_call | solution.py:446
  31.6 1.2 %collective-permute-done.4.refs_3_ = bf16[4,208,128]{2,1,0:T(8,128)(2,1)S(1)} collective-permute-done((bf16[4,208,128]{2,1,0:T(8,128)(2,1)S(1)}, bf16[4,208,128]{2,1,0:T(8,128)(2,1)S(1)}, u32[]{:S(2)}, u32[]{:S(2)}) %collective-permute-start.4) | collective-permute-done | bytes 213024 | tf_op jit(solution)/shard_map/ppermute | solution.py:611
  32.8 1.4 %collective-permute-start.6 = (bf16[2,208,128]{2,1,0:T(8,128)(2,1)S(1)}, bf16[2,208,128]{2,1,0:T(8,128)(2,1)S(1)}, u32[]{:S(2)}, u32[]{:S(2)}) collective-permute-start(bf16[2,208,128]{2,1,0:T(8,128)(2,1)S(1)} %get-tuple-element.119), channel_id=1, source_target_pairs={{0,4},{4,0},{8,12},{12,8},{1,5},{5,1},{9,13},{13,9},{2,6},{6,2},{1... | collective-permute-start | bytes 319496 | tf_op jit(solution)/shard_map/ppermute | solution.py:611
  34.4 1.2 %collective-permute-start.8 = (bf16[4,208,128]{2,1,0:T(8,128)(2,1)S(1)}, bf16[4,208,128]{2,1,0:T(8,128)(2,1)S(1)}, u32[]{:S(2)}, u32[]{:S(2)}) collective-permute-start(bf16[4,208,128]{2,1,0:T(8,128)(2,1)S(1)} %bitcast.40), channel_id=1, source_target_pairs={{0,3},{1,2},{2,1},{3,0},{4,7},{5,6},{6,5},{7,4},{8,11},{9,10},{10,... | collective-permute-start | bytes 638984 | tf_op jit(solution)/shard_map/ppermute | solution.py:611
  36.5 2.4 %collective-permute-start.7 = (bf16[2,208,128]{2,1,0:T(8,128)(2,1)S(1)}, bf16[2,208,128]{2,1,0:T(8,128)(2,1)S(1)}, u32[]{:S(2)}, u32[]{:S(2)}) collective-permute-start(bf16[2,208,128]{2,1,0:T(8,128)(2,1)S(1)} %far_sum_0.1.token.mine), channel_id=1, source_target_pairs={{0,8},{4,12},{8,0},{12,4},{1,9},{5,13},{9,1},{13,5},{2,10},{6,14},... | collective-permute-start | bytes 319496 | tf_op jit(solution)/shard_map/ppermute | solution.py:611
  39.2 3.9 %inputs_0.1 = (f32[2048,512]{1,0:T(8,128)}, f32[80,2048]{1,0:T(8,128)}, f32[8,128]{1,0:T(8,128)S(1)}) custom-call(bf16[2,208,128]{2,1,0:T(8,128)(2,1)S(1)} %far_sum_0.1.token.mine, bf16[256,256]{1,0:T(8,128)(2,1)S(1)} %get-tuple-element.120.received.refs_0_, bf16[2048,512]{1,0:T(8,128)(2,1)S(1)} %get-tuple-element.89.gout, ...), custom_call_target="tpu_custom_call" | custom-call | flops 1 | bytes 1 | tf_op jit(solution)/shard_map/inputs_0/pallas_call | solution.py:536
  43.1 1.4 %collective-permute-start.11 = (bf16[2,208,128]{2,1,0:T(8,128)(2,1)S(1)}, bf16[2,208,128]{2,1,0:T(8,128)(2,1)S(1)}, u32[]{:S(2)}, u32[]{:S(2)}) collective-permute-start(bf16[2,208,128]{2,1,0:T(8,128)(2,1)S(1)} %far_end_0.1.token.refs_0_), channel_id=1, source_target_pairs={{0,4},{4,0},{8,12},{12,8},{1,5},{5,1},{9,13},{13,9},{2,6},{6,2},{1... | collective-permute-start | bytes 319496 | tf_op jit(solution)/shard_map/ppermute | solution.py:611
  44.5 2.6 %collective-permute-done.9.refs_1_ = bf16[4,208,128]{2,1,0:T(8,128)(2,1)S(1)} collective-permute-done((bf16[4,208,128]{2,1,0:T(8,128)(2,1)S(1)}, bf16[4,208,128]{2,1,0:T(8,128)(2,1)S(1)}, u32[]{:S(2)}, u32[]{:S(2)}) %collective-permute-start.9) | collective-permute-done | bytes 213024 | tf_op jit(solution)/shard_map/ppermute | solution.py:611
  47.5 1.2 %collective-permute-start.14 = (bf16[4,208,128]{2,1,0:T(8,128)(2,1)S(1)}, bf16[4,208,128]{2,1,0:T(8,128)(2,1)S(1)}, u32[]{:S(2)}, u32[]{:S(2)}) collective-permute-start(bf16[4,208,128]{2,1,0:T(8,128)(2,1)S(1)} %far_join_0.1.token), channel_id=1, source_target_pairs={{0,3},{1,2},{2,1},{3,0},{4,7},{5,6},{6,5},{7,4},{8,11},{9,10},{10,... | collective-permute-start | bytes 638984 | tf_op jit(solution)/shard_map/ppermute | solution.py:611
  48.7 2.9 %collective-permute-done.12.refs_1_ = bf16[2,208,128]{2,1,0:T(8,128)(2,1)S(1)} collective-permute-done((bf16[2,208,128]{2,1,0:T(8,128)(2,1)S(1)}, bf16[2,208,128]{2,1,0:T(8,128)(2,1)S(1)}, u32[]{:S(2)}, u32[]{:S(2)}) %collective-permute-start.12) | collective-permute-done | bytes 106528 | tf_op jit(solution)/shard_map/ppermute | solution.py:611
  51.7 1.5 %collective-permute-start.13 = (bf16[2,208,128]{2,1,0:T(8,128)(2,1)S(1)}, bf16[2,208,128]{2,1,0:T(8,128)(2,1)S(1)}, u32[]{:S(2)}, u32[]{:S(2)}) collective-permute-start(bf16[2,208,128]{2,1,0:T(8,128)(2,1)S(1)} %far_sum_1.1.token.mine), channel_id=1, source_target_pairs={{0,8},{4,12},{8,0},{12,4},{1,9},{5,13},{9,1},{13,5},{2,10},{6,14},... | collective-permute-start | bytes 319496 | tf_op jit(solution)/shard_map/ppermute | solution.py:611
  54.7 2.4 %inputs_2.1 = (f32[2048,512]{1,0:T(8,128)}, f32[80,2048]{1,0:T(8,128)}, f32[8,128]{1,0:T(8,128)S(1)}) custom-call(bf16[2,208,128]{2,1,0:T(8,128)(2,1)S(1)} %far_sum_1.1.token.mine, bf16[256,256]{1,0:T(8,128)(2,1)S(1)} %get-tuple-element.120.received.refs_0_, ...), custom_call_target="tpu_custom_call", output_to_operand_aliasing={{0}: (12, {}), {1}: (13, {})} | custom-call | flops 1 | bytes 1 | tf_op jit(solution)/shard_map/inputs_2/pallas_call | solution.py:536
  57.1 1.0 %collective-permute-done.13.got = bf16[2,208,128]{2,1,0:T(8,128)(2,1)S(1)} collective-permute-done((bf16[2,208,128]{2,1,0:T(8,128)(2,1)S(1)}, bf16[2,208,128]{2,1,0:T(8,128)(2,1)S(1)}, u32[]{:S(2)}, u32[]{:S(2)}) %collective-permute-start.13) | collective-permute-done | bytes 106528 | tf_op jit(solution)/shard_map/ppermute | solution.py:611
  59.3 2.5 %collective-permute-start.18 = (bf16[256,512]{1,0:T(8,128)(2,1)S(1)}, bf16[256,512]{1,0:T(8,128)(2,1)S(1)}, u32[]{:S(2)}, u32[]{:S(2)}) collective-permute-start(bf16[256,512]{1,0:T(8,128)(2,1)S(1)} %early.1.token), channel_id=1, source_target_pairs={{1,0},{2,1},{3,2},{4,3},{5,4},{6,5},{7,6},{8,7},{9,8},{10,9},{11,1... | collective-permute-start | bytes 786440 | tf_op jit(solution)/shard_map/ppermute | solution.py:687
  62.1 1.7 %collective-permute-start.19 = (bf16[4,208,128]{2,1,0:T(8,128)(2,1)S(1)}, bf16[4,208,128]{2,1,0:T(8,128)(2,1)S(1)}, u32[]{:S(2)}, u32[]{:S(2)}) collective-permute-start(bf16[4,208,128]{2,1,0:T(8,128)(2,1)S(1)} %far_join_1.1.token), channel_id=1, source_target_pairs={{0,3},{1,2},{2,1},{3,0},{4,7},{5,6},{6,5},{7,4},{8,11},{9,10},{10,... | collective-permute-start | bytes 638984 | tf_op jit(solution)/shard_map/ppermute | solution.py:611
  63.8 4.3 %collective-permute-start.24 = (bf16[4,208,128]{2,1,0:T(8,128)(2,1)S(1)}, bf16[4,208,128]{2,1,0:T(8,128)(2,1)S(1)}, u32[]{:S(2)}, u32[]{:S(2)}) collective-permute-start(bf16[4,208,128]{2,1,0:T(8,128)(2,1)S(1)} %far_join_1.1.token), channel_id=1, source_target_pairs={{0,2},{1,3},{2,0},{3,1},{4,6},{5,7},{6,4},{7,5},{8,10},{9,11},{10,... | collective-permute-start | bytes 638984 | tf_op jit(solution)/shard_map/ppermute | solution.py:611
  68.7 3.6 %outputs.1 = (bf16[2048,512]{1,0:T(8,128)(2,1)}, bf16[2048,512]{1,0:T(8,128)(2,1)}, f32[8,128]{1,0:T(8,128)S(1)}) custom-call(bf16[4,208,128]{2,1,0:T(8,128)(2,1)S(1)} %far_join_1.1.token, s32[16,128]{1,0:T(8,128)S(1)} %get-tuple-element.86.valid, bf16[2048,512]{1,0:T(8,128)(2,1)S(1)} %get-tuple-element.87.sig, ...), custom_call_target="tpu_custom_call" | custom-call | flops 1 | bytes 1 | tf_op jit(solution)/shard_map/outputs/pallas_call | solution.py:479
  73.2 2.2 %inputs_3.1 = (f32[2048,512]{1,0:T(8,128)}, f32[80,2048]{1,0:T(8,128)}, f32[8,128]{1,0:T(8,128)S(1)}) custom-call(f32[8,128]{1,0:T(8,128)S(1)} %get-tuple-element.137.token, bf16[256,512]{1,0:T(8,128)(2,1)S(1)} %collective-permute-done.18.received, bf16[2048,512]{1,0:T(8,128)(2,1)S(1)} %get-tuple-element.89.gout, ...), custom_call_target="tpu_custom_call", output_to_operand_aliasing={{0}: (12, {}), {1}: (13, {})} | custom-call | flops 1 | bytes 1 | tf_op jit(solution)/shard_map/inputs_3/pallas_call | solution.py:536
  75.4 2.4 %collective-permute-start.20 = (bf16[2,4,208,128]{3,2,1,0:T(8,128)(2,1)S(1)}, bf16[2,4,208,128]{3,2,1,0:T(8,128)(2,1)S(1)}, u32[]{:S(2)}, u32[]{:S(2)}) collective-permute-start(bf16[2,4,208,128]{3,2,1,0:T(8,128)(2,1)S(1)} %near_join_1_0.1.token.refs_0_), channel_id=1, source_target_pairs={{0,16},{16,0},{1,17},{17,1},{2,18},{18,2},{3,19},{19,3},{4,20},{20... | collective-permute-start | bytes 1277960 | tf_op jit(solution)/shard_map/ppermute | solution.py:611
  77.8 1.7 %collective-permute-done.24 = bf16[4,208,128]{2,1,0:T(8,128)(2,1)S(1)} collective-permute-done((bf16[4,208,128]{2,1,0:T(8,128)(2,1)S(1)}, bf16[4,208,128]{2,1,0:T(8,128)(2,1)S(1)}, u32[]{:S(2)}, u32[]{:S(2)}) %collective-permute-start.24) | collective-permute-done | bytes 213024 | tf_op jit(solution)/shard_map/ppermute | solution.py:611
  80.7 2.0 %unpack_0.1 = (f32[512,1024]{1,0:T(8,128)}, f32[512,1024]{1,0:T(8,128)}, f32[80,1024]{1,0:T(8,128)}, f32[1,1024]{1,0:T(1,128)}, f32[512,512]{1,0:T(8,128)}, /*in...) custom-call(bf16[2,4,208,128]{3,2,1,0:T(8,128)(2,1)S(1)} %collective-permute-done.20.token.refs_2_, ...), custom_call_target="tpu_custom_call" | custom-call | flops 1 | bytes 1 | tf_op jit(solution)/shard_map/unpack_0/pallas_call | solution.py:598
  82.7 2.0 %unpack_1.1 = (f32[512,1024]{1,0:T(8,128)}, f32[512,1024]{1,0:T(8,128)}, f32[80,1024]{1,0:T(8,128)}, f32[1,1024]{1,0:T(1,128)}, f32[512,512]{1,0:T(8,128)}, /*in...) custom-call(f32[8,128]{1,0:T(8,128)S(1)} %get-tuple-element.143.toke, ...), custom_call_target="tpu_custom_call", output_to_operand_aliasing={{0}: (5, {}), {1}: (6, {}), {2}: (7, {}), {3}: (8, {}), {4}... | custom-call | flops 1 | bytes 1 | tf_op jit(solution)/shard_map/unpack_1/pallas_call | solution.py:598
  (51 shorter events, 10.6 us)
Async XLA Ops:
  1.6 11.0 %collective-permute-start = (bf16[256,512]{1,0:T(8,128)(2,1)S(1)}, bf16[256,512]{1,0:T(8,128)(2,1)S(1)}, u32[]{:S(2)}, u32[]{:S(2)}) collective-permute-start(bf16[256,512]{1,0:T(8,128)(2,1)S(1)} %slice.3), channel_id=1, source_target_pairs={{0,1},{1,2},{2,3},{3,4},{4,5},{5,6},{6,7},{7,8},{8,9},{9,10},{10,1... | collective-permute-start | bytes 786440 | tf_op jit(solution)/shard_map/ppermute | solution.py:687
  15.5 4.6 %collective-permute-start.1 = (bf16[4,4,208,128]{3,2,1,0:T(8,128)(2,1)S(1)}, bf16[4,4,208,128]{3,2,1,0:T(8,128)(2,1)S(1)}, u32[]{:S(2)}, u32[]{:S(2)}) collective-permute-start(bf16[4,4,208,128]{3,2,1,0:T(8,128)(2,1)S(1)} %get-tuple-element.101.token), channel_id=1, source_target_pairs={{0,16},{16,0},{1,17},{17,1},{2,18},{18,2},{3,19},{19,3},{4,20},{20... | collective-permute-start | bytes 2555912 | tf_op jit(solution)/shard_map/ppermute | solution.py:611
  20.2 11.3 %collective-permute-start.2 = (bf16[4,208,128]{2,1,0:T(8,128)(2,1)S(1)}, bf16[4,208,128]{2,1,0:T(8,128)(2,1)S(1)}, u32[]{:S(2)}, u32[]{:S(2)}) collective-permute-start(bf16[4,208,128]{2,1,0:T(8,128)(2,1)S(1)} %bitcast.42), channel_id=1, source_target_pairs={{0,1},{1,0},{2,3},{3,2},{4,5},{5,4},{6,7},{7,6},{8,9},{9,8},{10,11... | collective-permute-start | bytes 638984 | tf_op jit(solution)/shard_map/ppermute | solution.py:611
  20.6 11.0 %collective-permute-start.3 = (bf16[4,208,128]{2,1,0:T(8,128)(2,1)S(1)}, bf16[4,208,128]{2,1,0:T(8,128)(2,1)S(1)}, u32[]{:S(2)}, u32[]{:S(2)}) collective-permute-start(bf16[4,208,128]{2,1,0:T(8,128)(2,1)S(1)} %bitcast.41), channel_id=1, source_target_pairs={{0,2},{1,3},{2,0},{3,1},{4,6},{5,7},{6,4},{7,5},{8,10},{9,11},{10,... | collective-permute-start | bytes 638984 | tf_op jit(solution)/shard_map/ppermute | solution.py:611
  21.8 10.9 %collective-permute-start.4 = (bf16[4,208,128]{2,1,0:T(8,128)(2,1)S(1)}, bf16[4,208,128]{2,1,0:T(8,128)(2,1)S(1)}, u32[]{:S(2)}, u32[]{:S(2)}) collective-permute-start(bf16[4,208,128]{2,1,0:T(8,128)(2,1)S(1)} %bitcast.38), channel_id=1, source_target_pairs={{0,3},{1,2},{2,1},{3,0},{4,7},{5,6},{6,5},{7,4},{8,11},{9,10},{10,... | collective-permute-start | bytes 638984 | tf_op jit(solution)/shard_map/ppermute | solution.py:611
  28.4 5.8 %collective-permute-start.5 = (bf16[4,4,208,128]{3,2,1,0:T(8,128)(2,1)S(1)}, bf16[4,4,208,128]{3,2,1,0:T(8,128)(2,1)S(1)}, u32[]{:S(2)}, u32[]{:S(2)}) collective-permute-start(bf16[4,4,208,128]{3,2,1,0:T(8,128)(2,1)S(1)} %theirs_1.1.token), channel_id=1, source_target_pairs={{0,16},{16,0},{1,17},{17,1},{2,18},{18,2},{3,19},{19,3},{4,20},{20... | collective-permute-start | bytes 2555912 | tf_op jit(solution)/shard_map/ppermute | solution.py:611
  32.8 3.6 %collective-permute-start.6 = (bf16[2,208,128]{2,1,0:T(8,128)(2,1)S(1)}, bf16[2,208,128]{2,1,0:T(8,128)(2,1)S(1)}, u32[]{:S(2)}, u32[]{:S(2)}) collective-permute-start(bf16[2,208,128]{2,1,0:T(8,128)(2,1)S(1)} %get-tuple-element.119), channel_id=1, source_target_pairs={{0,4},{4,0},{8,12},{12,8},{1,5},{5,1},{9,13},{13,9},{2,6},{6,2},{1... | collective-permute-start | bytes 319496 | tf_op jit(solution)/shard_map/ppermute | solution.py:611
  34.4 10.1 %collective-permute-start.8 = (bf16[4,208,128]{2,1,0:T(8,128)(2,1)S(1)}, bf16[4,208,128]{2,1,0:T(8,128)(2,1)S(1)}, u32[]{:S(2)}, u32[]{:S(2)}) collective-permute-start(bf16[4,208,128]{2,1,0:T(8,128)(2,1)S(1)} %bitcast.40), channel_id=1, source_target_pairs={{0,3},{1,2},{2,1},{3,0},{4,7},{5,6},{6,5},{7,4},{8,11},{9,10},{10,... | collective-permute-start | bytes 638984 | tf_op jit(solution)/shard_map/ppermute | solution.py:611
  35.6 11.5 %collective-permute-start.9 = (bf16[4,208,128]{2,1,0:T(8,128)(2,1)S(1)}, bf16[4,208,128]{2,1,0:T(8,128)(2,1)S(1)}, u32[]{:S(2)}, u32[]{:S(2)}) collective-permute-start(bf16[4,208,128]{2,1,0:T(8,128)(2,1)S(1)} %bitcast.37), channel_id=1, source_target_pairs={{0,2},{1,3},{2,0},{3,1},{4,6},{5,7},{6,4},{7,5},{8,10},{9,11},{10,... | collective-permute-start | bytes 638984 | tf_op jit(solution)/shard_map/ppermute | solution.py:611
  36.5 6.6 %collective-permute-start.7 = (bf16[2,208,128]{2,1,0:T(8,128)(2,1)S(1)}, bf16[2,208,128]{2,1,0:T(8,128)(2,1)S(1)}, u32[]{:S(2)}, u32[]{:S(2)}) collective-permute-start(bf16[2,208,128]{2,1,0:T(8,128)(2,1)S(1)} %far_sum_0.1.token.mine), channel_id=1, source_target_pairs={{0,8},{4,12},{8,0},{12,4},{1,9},{5,13},{9,1},{13,5},{2,10},{6,14},... | collective-permute-start | bytes 319496 | tf_op jit(solution)/shard_map/ppermute | solution.py:611
  38.8 8.3 %collective-permute-start.10 = (bf16[4,208,128]{2,1,0:T(8,128)(2,1)S(1)}, bf16[4,208,128]{2,1,0:T(8,128)(2,1)S(1)}, u32[]{:S(2)}, u32[]{:S(2)}) collective-permute-start(bf16[4,208,128]{2,1,0:T(8,128)(2,1)S(1)} %bitcast.36), channel_id=1, source_target_pairs={{0,1},{1,0},{2,3},{3,2},{4,5},{5,4},{6,7},{7,6},{8,9},{9,8},{10,11... | collective-permute-start | bytes 638984 | tf_op jit(solution)/shard_map/ppermute | solution.py:611
  43.1 4.4 %collective-permute-start.11 = (bf16[2,208,128]{2,1,0:T(8,128)(2,1)S(1)}, bf16[2,208,128]{2,1,0:T(8,128)(2,1)S(1)}, u32[]{:S(2)}, u32[]{:S(2)}) collective-permute-start(bf16[2,208,128]{2,1,0:T(8,128)(2,1)S(1)} %far_end_0.1.token.refs_0_), channel_id=1, source_target_pairs={{0,4},{4,0},{8,12},{12,8},{1,5},{5,1},{9,13},{13,9},{2,6},{6,2},{1... | collective-permute-start | bytes 319496 | tf_op jit(solution)/shard_map/ppermute | solution.py:611
  47.2 4.4 %collective-permute-start.12 = (bf16[2,208,128]{2,1,0:T(8,128)(2,1)S(1)}, bf16[2,208,128]{2,1,0:T(8,128)(2,1)S(1)}, u32[]{:S(2)}, u32[]{:S(2)}) collective-permute-start(bf16[2,208,128]{2,1,0:T(8,128)(2,1)S(1)} %get-tuple-element.126), channel_id=1, source_target_pairs={{0,4},{4,0},{8,12},{12,8},{1,5},{5,1},{9,13},{13,9},{2,6},{6,2},{1... | collective-permute-start | bytes 319496 | tf_op jit(solution)/shard_map/ppermute | solution.py:611
  47.5 14.3 %collective-permute-start.14 = (bf16[4,208,128]{2,1,0:T(8,128)(2,1)S(1)}, bf16[4,208,128]{2,1,0:T(8,128)(2,1)S(1)}, u32[]{:S(2)}, u32[]{:S(2)}) collective-permute-start(bf16[4,208,128]{2,1,0:T(8,128)(2,1)S(1)} %far_join_0.1.token), channel_id=1, source_target_pairs={{0,3},{1,2},{2,1},{3,0},{4,7},{5,6},{6,5},{7,4},{8,11},{9,10},{10,... | collective-permute-start | bytes 638984 | tf_op jit(solution)/shard_map/ppermute | solution.py:611
  51.7 6.5 %collective-permute-start.13 = (bf16[2,208,128]{2,1,0:T(8,128)(2,1)S(1)}, bf16[2,208,128]{2,1,0:T(8,128)(2,1)S(1)}, u32[]{:S(2)}, u32[]{:S(2)}) collective-permute-start(bf16[2,208,128]{2,1,0:T(8,128)(2,1)S(1)} %far_sum_1.1.token.mine), channel_id=1, source_target_pairs={{0,8},{4,12},{8,0},{12,4},{1,9},{5,13},{9,1},{13,5},{2,10},{6,14},... | collective-permute-start | bytes 319496 | tf_op jit(solution)/shard_map/ppermute | solution.py:611
  53.2 8.7 %collective-permute-start.16 = (bf16[4,208,128]{2,1,0:T(8,128)(2,1)S(1)}, bf16[4,208,128]{2,1,0:T(8,128)(2,1)S(1)}, u32[]{:S(2)}, u32[]{:S(2)}) collective-permute-start(bf16[4,208,128]{2,1,0:T(8,128)(2,1)S(1)} %far_join_0.1.token), channel_id=1, source_target_pairs={{0,2},{1,3},{2,0},{3,1},{4,6},{5,7},{6,4},{7,5},{8,10},{9,11},{10,... | collective-permute-start | bytes 638984 | tf_op jit(solution)/shard_map/ppermute | solution.py:611
  54.0 7.9 %collective-permute-start.15 = (bf16[4,208,128]{2,1,0:T(8,128)(2,1)S(1)}, bf16[4,208,128]{2,1,0:T(8,128)(2,1)S(1)}, u32[]{:S(2)}, u32[]{:S(2)}) collective-permute-start(bf16[4,208,128]{2,1,0:T(8,128)(2,1)S(1)} %far_join_0.1.token), channel_id=1, source_target_pairs={{0,1},{1,0},{2,3},{3,2},{4,5},{5,4},{6,7},{7,6},{8,9},{9,8},{10,11... | collective-permute-start | bytes 638984 | tf_op jit(solution)/shard_map/ppermute | solution.py:611
  58.2 3.9 %collective-permute-start.17 = (bf16[2,208,128]{2,1,0:T(8,128)(2,1)S(1)}, bf16[2,208,128]{2,1,0:T(8,128)(2,1)S(1)}, u32[]{:S(2)}, u32[]{:S(2)}) collective-permute-start(bf16[2,208,128]{2,1,0:T(8,128)(2,1)S(1)} %far_end_1.1.token.refs_0_), channel_id=1, source_target_pairs={{0,4},{4,0},{8,12},{12,8},{1,5},{5,1},{9,13},{13,9},{2,6},{6,2},{1... | collective-permute-start | bytes 319496 | tf_op jit(solution)/shard_map/ppermute | solution.py:611
  59.3 13.0 %collective-permute-start.18 = (bf16[256,512]{1,0:T(8,128)(2,1)S(1)}, bf16[256,512]{1,0:T(8,128)(2,1)S(1)}, u32[]{:S(2)}, u32[]{:S(2)}) collective-permute-start(bf16[256,512]{1,0:T(8,128)(2,1)S(1)} %early.1.token), channel_id=1, source_target_pairs={{1,0},{2,1},{3,2},{4,3},{5,4},{6,5},{7,6},{8,7},{9,8},{10,9},{11,1... | collective-permute-start | bytes 786440 | tf_op jit(solution)/shard_map/ppermute | solution.py:687
  62.1 13.3 %collective-permute-start.19 = (bf16[4,208,128]{2,1,0:T(8,128)(2,1)S(1)}, bf16[4,208,128]{2,1,0:T(8,128)(2,1)S(1)}, u32[]{:S(2)}, u32[]{:S(2)}) collective-permute-start(bf16[4,208,128]{2,1,0:T(8,128)(2,1)S(1)} %far_join_1.1.token), channel_id=1, source_target_pairs={{0,3},{1,2},{2,1},{3,0},{4,7},{5,6},{6,5},{7,4},{8,11},{9,10},{10,... | collective-permute-start | bytes 638984 | tf_op jit(solution)/shard_map/ppermute | solution.py:611
  63.8 15.7 %collective-permute-start.24 = (bf16[4,208,128]{2,1,0:T(8,128)(2,1)S(1)}, bf16[4,208,128]{2,1,0:T(8,128)(2,1)S(1)}, u32[]{:S(2)}, u32[]{:S(2)}) collective-permute-start(bf16[4,208,128]{2,1,0:T(8,128)(2,1)S(1)} %far_join_1.1.token), channel_id=1, source_target_pairs={{0,2},{1,3},{2,0},{3,1},{4,6},{5,7},{6,4},{7,5},{8,10},{9,11},{10,... | collective-permute-start | bytes 638984 | tf_op jit(solution)/shard_map/ppermute | solution.py:611
  68.1 12.0 %collective-permute-start.23 = (bf16[4,208,128]{2,1,0:T(8,128)(2,1)S(1)}, bf16[4,208,128]{2,1,0:T(8,128)(2,1)S(1)}, u32[]{:S(2)}, u32[]{:S(2)}) collective-permute-start(bf16[4,208,128]{2,1,0:T(8,128)(2,1)S(1)} %far_join_1.1.token), channel_id=1, source_target_pairs={{0,1},{1,0},{2,3},{3,2},{4,5},{5,4},{6,7},{7,6},{8,9},{9,8},{10,11... | collective-permute-start | bytes 638984 | tf_op jit(solution)/shard_map/ppermute | solution.py:611
  68.1 12.5 %collective-permute-start.22 = (bf16[2,4,208,128]{3,2,1,0:T(8,128)(2,1)S(1)}, bf16[2,4,208,128]{3,2,1,0:T(8,128)(2,1)S(1)}, u32[]{:S(2)}, u32[]{:S(2)}) collective-permute-start(bf16[2,4,208,128]{3,2,1,0:T(8,128)(2,1)S(1)} %near_join_0_1.1.token.refs_1_), channel_id=1, source_target_pairs={{0,16},{16,0},{1,17},{17,1},{2,18},{18,2},{3,19},{19,3},{4,20},{20... | collective-permute-start | bytes 1277960 | tf_op jit(solution)/shard_map/ppermute | solution.py:611
  72.3 8.3 %collective-permute-start.21 = (bf16[2,4,208,128]{3,2,1,0:T(8,128)(2,1)S(1)}, bf16[2,4,208,128]{3,2,1,0:T(8,128)(2,1)S(1)}, u32[]{:S(2)}, u32[]{:S(2)}) collective-permute-start(bf16[2,4,208,128]{3,2,1,0:T(8,128)(2,1)S(1)} %near_join_0_0.1.token.refs_0_), channel_id=1, source_target_pairs={{0,16},{16,0},{1,17},{17,1},{2,18},{18,2},{3,19},{19,3},{4,20},{20... | collective-permute-start | bytes 1277960 | tf_op jit(solution)/shard_map/ppermute | solution.py:611
  75.4 5.2 %collective-permute-start.20 = (bf16[2,4,208,128]{3,2,1,0:T(8,128)(2,1)S(1)}, bf16[2,4,208,128]{3,2,1,0:T(8,128)(2,1)S(1)}, u32[]{:S(2)}, u32[]{:S(2)}) collective-permute-start(bf16[2,4,208,128]{3,2,1,0:T(8,128)(2,1)S(1)} %near_join_1_0.1.token.refs_0_), channel_id=1, source_target_pairs={{0,16},{16,0},{1,17},{17,1},{2,18},{18,2},{3,19},{19,3},{4,20},{20... | collective-permute-start | bytes 1277960 | tf_op jit(solution)/shard_map/ppermute | solution.py:611
  80.1 2.5 %collective-permute-start.25 = (bf16[2,4,208,128]{3,2,1,0:T(8,128)(2,1)S(1)}, bf16[2,4,208,128]{3,2,1,0:T(8,128)(2,1)S(1)}, u32[]{:S(2)}, u32[]{:S(2)}) collective-permute-start(bf16[2,4,208,128]{3,2,1,0:T(8,128)(2,1)S(1)} %near_join_1_1.1.refs_1_), channel_id=1, source_target_pairs={{0,16},{16,0},{1,17},{17,1},{2,18},{18,2},{3,19},{19,3},{4,20},{20... | collective-permute-start | bytes 1277960 | tf_op jit(solution)/shard_map/ppermute | solution.py:611
